TPU v7x, 1024 devices: a whole 4x4x32 slice. The times are simulated.
1024 devices in a mesh: dp: 64 (over y_lo, z), mp: 16 (over y_hi, x, core).
Axes of the slice: x: 4, y: 4 (y_hi: 2, y_lo: 2; y = y_hi * 2 + y_lo), z: 32, core: 2. Of those that a mesh axis runs over, the one named last changes fastest.
Arguments:
- bag_ids: int32 [4096, 64, 16], P('dp'), may hold values from 0 to 1023
- tables: bfloat16 [64, 1024, 256], P(None, 'mp'), may hold values from -1.5 to 1.5
- down_proj: bfloat16 [16384, 256], P('mp'), may hold values from -0.046875 to 0.046875
- up_proj: bfloat16 [256, 16384], P(None, 'mp'), may hold values from -0.375 to 0.375
- cotangent: bfloat16 [4096, 16384], P('dp', 'mp'), may hold values from -6 to 6
Outputs:
- cross_out: bfloat16 [4096, 16384], P('dp', 'mp')
- table_grads: bfloat16 [64, 64, 1024, 256], P('dp', None, 'mp')
- down_grad: float32 [16384, 256], P('mp')
- up_grad: float32 [256, 16384], P(None, 'mp')
All inputs are finite; a program needn't handle non-finite values.
Results may differ from a plain program's by a relative error of at most 0.028.
Values may be sent and summed in bfloat16 or wider, within the bound.
No kernel may reach another device: no remote copies, remote signals or barrier semaphores. Data moves between devices by JAX's collectives and lax.ppermute only.
A program may use at most 64 MiB of HBM per device.

v0:
```python
import jax
import jax.numpy as jnp
from jax import lax
from jax.sharding import PartitionSpec as P


def count_rows(bag_ids, row_count):
    sample_count, feature_count, bag_size = bag_ids.shape
    row_slots = jnp.arange(row_count, dtype=jnp.int32)
    flipped = jnp.transpose(bag_ids, (1, 0, 2))

    def add_slot(position, running):
        column = lax.dynamic_index_in_dim(flipped, position, 2, keepdims=False)
        return running + (column[:, :, None] == row_slots).astype(jnp.float32)

    empty = jnp.zeros((feature_count, sample_count, row_count), jnp.float32)
    return lax.fori_loop(0, bag_size, add_slot, empty).astype(jnp.bfloat16)


def shards(bag_ids, tables, down_proj, up_proj, cotangent):
    ways = lax.axis_size("mp")
    shard_index = lax.axis_index("mp")
    sample_count, feature_count, bag_size = bag_ids.shape
    row_count = tables.shape[1]
    embed_dim = tables.shape[2]
    local_features = feature_count // ways
    counts = count_rows(bag_ids - shard_index * row_count, row_count)
    partial_value = jnp.einsum(
        "fbr,fre->bfe", counts, tables, preferred_element_type=jnp.float32
    ).astype(jnp.bfloat16)
    merged = jnp.sum(
        lax.all_to_all(partial_value[None], "mp", split_axis=2, concat_axis=0, tiled=True),
        axis=0,
        dtype=jnp.float32,
    ).astype(jnp.bfloat16)
    pooled_rows = merged.reshape(merged.shape[0], local_features * embed_dim)
    rank_part = jnp.dot(pooled_rows, down_proj, preferred_element_type=jnp.float32)
    rank_act = lax.psum(rank_part.astype(jnp.bfloat16), "mp")
    scale_map = jnp.dot(rank_act, up_proj, preferred_element_type=jnp.float32)
    pooled_f = pooled_rows.astype(jnp.float32)
    cross_out = (pooled_f * scale_map + pooled_f).astype(jnp.bfloat16)
    upstream = cotangent.astype(jnp.float32)
    scale_grad = (upstream * pooled_f).astype(jnp.bfloat16)
    up_part = lax.dot_general(
        rank_act, scale_grad, (((0,), (0,)), ((), ())), preferred_element_type=jnp.float32
    )
    rank_back = lax.dot_general(
        scale_grad, up_proj, (((1,), (1,)), ((), ())), preferred_element_type=jnp.float32
    )
    rank_grad = lax.psum(rank_back.astype(jnp.bfloat16), "mp")
    down_part = lax.dot_general(
        pooled_rows, rank_grad, (((0,), (0,)), ((), ())), preferred_element_type=jnp.float32
    )
    back = lax.dot_general(
        rank_grad, down_proj, (((1,), (1,)), ((), ())), preferred_element_type=jnp.float32
    )
    pooled_grad = (upstream * scale_map + upstream + back).astype(jnp.bfloat16)
    grad_blocks = pooled_grad.reshape(sample_count, local_features, embed_dim)
    table_grads = jnp.einsum(
        "fbr,bfe->fre",
        counts,
        lax.all_gather(grad_blocks, "mp", axis=1, tiled=True),
        preferred_element_type=jnp.float32,
    ).astype(jnp.bfloat16)
    up_grad, down_grad = lax.psum((up_part, down_part), "dp")
    return (cross_out, table_grads[None], down_grad, up_grad)


def solution(mesh):
    placed = (P("dp", None, None), P(None, "mp", None), P("mp", None), P(None, "mp"), P("dp", "mp"))
    return jax.shard_map(
        shards,
        mesh=mesh,
        in_specs=placed,
        out_specs=(P("dp", "mp"), P("dp", None, "mp", None), P("mp", None), P(None, "mp")),
        check_vma=False,
    )
```

profile of v0, /device:TPU:6, one launch (start us, length us, event | category | flops | bytes accessed | tf_op | source)
XLA Modules:
  0.0 892.6 jit_solution(9598149412079210580)
XLA Ops:
  7.2 1.4 copy.12
  8.7 64.3 %while.14 = (s32[]{:T(128)}, f32[64,64,64]{2,1,0:T(8,128)}, s32[64,64,16]{1,0,2:T(8,128)S(1)}, s32[]{:T(128)}, s32[]{:T(128)}) while((s32[]{:T(128)}, f32[64,64,64]{2,1,0:T(8,128)}, s32[64,64,16]{1,0,2:T(8,128)S(1)}, s32[]{:T(128)}, s32[]{:T(128)}) %tuple.37), condition=%wide.region_1.2_spmd.clone, body=%wide.region_0.1_spmd.clone.sunk | while | flops 1048579 | bytes 2146387 | solution.py:17
  8.7 2.3 select_add_fusion.2
  11.1 4.1 select_add_fusion.2
  15.2 4.1 select_add_fusion.2
  19.3 4.1 select_add_fusion.2
  23.4 4.1 select_add_fusion.2
  27.6 4.1 select_add_fusion.2
  31.7 4.1 select_add_fusion.2
  35.8 4.1 select_add_fusion.2
  40.0 4.1 select_add_fusion.2
  44.1 4.1 select_add_fusion.2
  48.2 4.1 select_add_fusion.2
  52.3 4.1 select_add_fusion.2
  56.5 4.1 select_add_fusion.2
  60.6 4.1 select_add_fusion.2
  64.7 4.1 select_add_fusion.2
  68.8 4.1 select_add_fusion.2
  73.0 2.3 convert_bitcast_fusion.1
  75.3 42.7 %all_to_all.12 = bf16[1,64,64,256]{3,1,0,2:T(8,128)(2,1)} all-to-all(bf16[1,64,64,256]{3,1,0,2:T(8,128)(2,1)S(1)} %convert_bitcast_fusion.1), channel_id=1, replica_groups=mesh['dp'=64,'mp'=16] {'mp'}, dimensions={2} | all-to-all | bytes 4194304 | tf_op jit(solution)/shard_map/all_to_all | solution.py:32
  117.9 2.1 reduce_sum.12
  120.9 0.9 convolution_convert_fusion
  121.9 156.4 %all-reduce.7.cloned.1.call-done = (bf16[64,256]{1,0:T(8,128)(2,1)}, bf16[64,256]{1,0:T(8,128)(2,1)}) async-done(((bf16[64,256]{1,0:T(8,128)(2,1)}, bf16[64,256]{1,0:T(8,128)(2,1)}), (bf16[64,256]{1,0:T(8,128)(2,1)}, bf16[64,256]{1,0:T(8,128)(2,1)})) %all-reduce.7.cloned.1.call-update) | async-done | bytes 65552 | tf_op jit(solution)/shard_map/psum | solution.py:38
  278.2 1.7 fusion.6
  279.9 1.0 fusion.2
  281.7 1.3 fusion.10
  283.0 1.3 fusion.7
  284.4 87.5 %all-gather.2.cloned.1.call-done = bf16[64,64,256]{2,0,1:T(8,128)(2,1)} async-done(((bf16[64,4,256]{2,0,1:T(8,128)(2,1)}), bf16[64,64,256]{2,0,1:T(8,128)(2,1)}) %all-gather.2.cloned.1.call-update) | async-done | bytes 2097168 | tf_op jit(solution)/shard_map/all_gather | solution.py:62
  371.9 4.3 convert_bitcast_fusion
  376.2 506.6 %all-reduce.5.cloned.1.call-done = (f32[1024,256]{1,0:T(8,128)}, f32[256,1024]{1,0:T(8,128)}) async-done(((f32[1024,256]{1,0:T(8,128)}, f32[256,1024]{1,0:T(8,128)}), (f32[1024,256]{1,0:T(8,128)}, f32[256,1024]{1,0:T(8,128)})) %all-reduce.5.cloned.1.call-update) | async-done | bytes 2097168 | tf_op jit(solution)/shard_map/psum | solution.py:65
  882.7 2.4 copy.32
  885.1 1.0 copy.33
  (41 shorter events, 1.8 us)
Async XLA Ops:
  7.2 65.8 %copy-start = (bf16[64,64,256]{2,1,0:T(8,128)(2,1)S(1)}, bf16[64,64,256]{2,1,0:T(8,128)(2,1)}, u32[]{:S(2)}) copy-start(bf16[64,64,256]{2,1,0:T(8,128)(2,1)} %param.8) | copy-start | bytes 6291460
  7.2 271.1 %all-reduce.7.cloned.1.call-start = ((), (), s32[]{:S(2)}) async-start(), calls=%async_computation.3 | async-start | bytes 131072 | tf_op jit(solution)/shard_map/psum | solution.py:38
  117.9 2.1 copy-start.2
  117.9 2.9 copy-start.1
  117.9 2.9 copy-start.3
  121.8 250.0 %all-gather.2.cloned.1.call-start = ((), (), s32[]{:S(2)}) async-start(), calls=%async_computation.1 | async-start | bytes 2228224 | tf_op jit(solution)/shard_map/all_gather | solution.py:62
  278.2 3.5 copy-start.5
  278.2 4.8 copy-start.6
  281.7 601.0 %all-reduce.5.cloned.1.call-start = ((), (), s32[]{:S(2)}) async-start(), calls=%async_computation.2 | async-start | bytes 4194304 | tf_op jit(solution)/shard_map/psum | solution.py:65
  882.7 2.4 copy-start.4
Sparse Core Ops, SparseCore 0:
  121.9 156.2 all-reduce.6
  284.1 87.7 all-gather.1
  376.4 506.3 all-reduce.4
where the time goes:
time: 894 us; the launch traced here: 893 us
  waiting for transfers between devices  751 us (84%)
  other arithmetic  66.3 us (7%)
  blocking collectives  42.7 us (5%)
  between operations  13.8 us (2%)
  matrix products  13.6 us (2%)
    psum x1, waiting for transfers between devices, shards(): up_grad, down_grad = lax.psum((up_part, down_part), 'dp')  507 us
    psum x1, waiting for transfers between devices, shards(): rank_act = lax.psum(rank_part.astype(jnp.bfloat16), 'mp')  156 us
    all_gather x1, waiting for transfers between devices, shards(): lax.all_gather(grad_blocks, 'mp', axis=1, tiled=True)  87.5 us
    add x16, other arithmetic, add_slot(): return running + (column[:, :, None] == row_slots).astype(jnp.float32)  64.2 us
    all_to_all x1, blocking collectives, shards(): lax.all_to_all(partial_value[None], 'mp', split_axis=2, concat_axis=0, ti...  42.7 us
  transfers between devices with their start and end apart: 3, of which 3 were waited for; matrix products, arithmetic and copies ran while one was open for 1% of the time, Pallas kernels for 0%

commit v1 on v0

v1 whole, which is shorter than its diff:
```python
import jax
import jax.numpy as jnp
from jax import lax
from jax.experimental import pallas as pl
from jax.experimental.pallas import tpu as pltpu
from jax.sharding import PartitionSpec as P

BF16 = jnp.bfloat16
F32 = jnp.float32
VMEM_LIMIT = 48 * 1024 * 1024

QUAD = 4


def layout_of(dp_count, mp_count):
    depth = dp_count // 2
    pairs = depth // 2

    def member(pair, quad):
        return (quad // 2) * depth + pair * 2 + quad % 2

    quads = [[member(pair, quad) for quad in range(QUAD)] for pair in range(pairs)]
    lines = [[member(pair, quad) for pair in range(pairs)] for quad in range(QUAD)]
    blocks = [
        [member(pair, quad) * mp_count + index for index in range(mp_count) for quad in range(QUAD)]
        for pair in range(pairs)
    ]
    return quads, lines, blocks


def call(body, out_shape, *operands):
    return pl.pallas_call(
        body,
        out_shape=out_shape,
        compiler_params=pltpu.CompilerParams(vmem_limit_bytes=VMEM_LIMIT),
    )(*operands)


def contract(left, right, left_dim, right_dim):
    return lax.dot_general(
        left, right, (((left_dim,), (right_dim,)), ((), ())), preferred_element_type=F32
    )


def count_body(ids_ref, counts_ref):
    bag_size, columns = ids_ref.shape
    step = 64

    def rows_at(index, carry):
        base = pl.multiple_of(index * step, step)
        rows = lax.broadcasted_iota(jnp.int32, (step, columns), 0) + base
        total = jnp.zeros((step, columns), F32)
        for slot in range(bag_size):
            total = total + jnp.where(rows == ids_ref[slot : slot + 1, :], 1.0, 0.0)
        counts_ref[pl.ds(base, step), :] = total.astype(BF16)
        return carry

    lax.fori_loop(0, counts_ref.shape[0] // step, rows_at, 0)


def forward_body(counts_ref, table_ref, grad_ref, down_ref, up_ref, pooled_ref, scaled_ref, part_ref):
    samples = grad_ref.shape[0]
    pooled = contract(counts_ref[...], table_ref[...], 0, 0).astype(BF16)
    pooled_ref[...] = pooled
    scaled = (grad_ref[...].astype(F32) * pooled.astype(F32)).astype(BF16)
    scaled_ref[...] = scaled
    part_ref[:samples, :] = contract(pooled, down_ref[...], 1, 0).astype(BF16)
    part_ref[samples:, :] = contract(scaled, up_ref[...], 1, 1).astype(BF16)


def cross_body(ranks_ref, pooled_ref, scaled_ref, grad_ref, down_ref, up_ref, parts_ref, back_ref):
    samples = grad_ref.shape[0]
    rank_act = ranks_ref[:samples, :]
    rank_grad = ranks_ref[samples:, :]
    pooled = pooled_ref[...]
    parts_ref[0] = contract(rank_act, scaled_ref[...], 0, 0).astype(BF16)
    parts_ref[1] = contract(pooled, rank_grad, 0, 0).astype(BF16)
    scale_map = contract(rank_act, up_ref[...], 1, 0)
    pooled_f = pooled.astype(F32)
    cross = (pooled_f * scale_map + pooled_f).astype(BF16)
    upstream = grad_ref[...].astype(F32)
    back = contract(rank_grad, down_ref[...], 1, 1)
    pooled_grad = (upstream * scale_map + upstream + back).astype(BF16)
    group = samples // QUAD
    for quad in range(QUAD):
        back_ref[quad, 0] = cross[quad * group : (quad + 1) * group]
        back_ref[quad, 1] = pooled_grad[quad * group : (quad + 1) * group]


def table_body(counts_ref, back_ref, cross_ref, grads_ref):
    ways, _, rows, embed = grads_ref.shape
    group = back_ref.shape[2]
    blocks = []
    for quad in range(QUAD):
        cross_ref[:, quad * embed : (quad + 1) * embed] = back_ref[quad, 0]
        blocks.append(back_ref[quad, 1])
    zero = jnp.zeros((group, embed), BF16)
    spread = jnp.concatenate(
        [
            jnp.concatenate([blocks[quad] if quad == other else zero for other in range(QUAD)], axis=1)
            for quad in range(QUAD)
        ],
        axis=0,
    )
    step = 4 * rows

    def rows_at(index, carry):
        base = pl.multiple_of(index * step, step)
        grads = contract(counts_ref[pl.ds(base, step), :], spread, 1, 0).astype(BF16)
        for part in range(4):
            for quad in range(QUAD):
                grads_ref[index * 4 + part, quad] = grads[
                    part * rows : (part + 1) * rows, quad * embed : (quad + 1) * embed
                ]
        return carry

    lax.fori_loop(0, ways // 4, rows_at, 0)


def weights_body(sums_ref, down_ref, up_ref):
    width = sums_ref.shape[3]
    for quad in range(QUAD):
        up_ref[:, quad * width : (quad + 1) * width] = sums_ref[quad, 0].astype(F32)
        down_ref[quad * width : (quad + 1) * width, :] = sums_ref[quad, 1].astype(F32)


def shape_of(shape, dtype=BF16):
    return jax.ShapeDtypeStruct(shape, dtype)


def shards(bag_ids, tables, down_proj, up_proj, cotangent):
    dp_count, ways = lax.axis_size("dp"), lax.axis_size("mp")
    quads, lines, blocks = layout_of(dp_count, ways)
    place = lax.axis_index("dp")
    quad = (place // (dp_count // 2)) * 2 + place % 2
    shard_index = lax.axis_index("mp")
    group, feature_count, bag_size = bag_ids.shape
    _, rows, embed = tables.shape
    rank = down_proj.shape[1]
    samples = QUAD * group

    def exchange(value, axis, groups=None):
        return lax.all_to_all(value, axis, 0, 0, axis_index_groups=groups, tiled=True)

    def spread_over(value, count):
        return jnp.broadcast_to(value[None], (count,) + value.shape)

    with jax.named_scope("inputs"):
        own_ids = lax.dynamic_slice_in_dim(bag_ids, shard_index * QUAD, QUAD, 1)
        own_ids = jnp.transpose(own_ids, (1, 2, 0))
        table_parts = lax.dynamic_index_in_dim(
            tables.reshape(ways, QUAD, rows, embed), quad, 1, keepdims=False
        )
        grad_parts = jnp.transpose(cotangent.reshape(group, QUAD, embed), (1, 0, 2))
        quad_ids = exchange(own_ids, "dp", quads)
        table = exchange(table_parts, "mp").reshape(ways * rows, embed)
        quad_grad = exchange(grad_parts, "dp", quads).reshape(samples, embed)
        down = lax.dynamic_slice_in_dim(down_proj, quad * embed, embed, 0)
        up = lax.dynamic_slice_in_dim(up_proj, quad * embed, embed, 1)

    def count(ids):
        columns = jnp.transpose(ids, (1, 0, 2)).reshape(bag_size, samples)
        return call(count_body, shape_of((ways * rows, samples)), columns)

    with jax.named_scope("counts"):
        quad_counts = count(quad_ids)
        own_counts = count(own_ids)

    with jax.named_scope("forward"):
        pooled, scaled, part = call(
            forward_body,
            (shape_of((samples, embed)), shape_of((samples, embed)), shape_of((2 * samples, rank))),
            quad_counts, table, quad_grad, down, up,
        )
    with jax.named_scope("ranks"):
        members = QUAD * ways
        pieces = exchange(part.reshape(members, 2 * samples // members, rank), ("dp", "mp"), blocks)
        piece = jnp.sum(pieces.astype(F32), axis=0).astype(BF16)
        ranks = exchange(spread_over(piece, members), ("dp", "mp"), blocks).reshape(2 * samples, rank)

    with jax.named_scope("cross"):
        parts, back = call(
            cross_body,
            (shape_of((2, embed, rank)), shape_of((QUAD, 2, group, embed))),
            ranks, pooled, scaled, quad_grad, down, up,
        )
    with jax.named_scope("weights"):
        pairs = dp_count // QUAD
        slices = exchange(parts.reshape(pairs, 2 * embed // pairs, rank), "dp", lines)
        own_slice = jnp.sum(slices.astype(F32), axis=0).astype(BF16)
        sums = exchange(spread_over(own_slice, pairs), "dp", lines).reshape(2, embed, rank)
        every = exchange(spread_over(sums, QUAD), "dp", quads)
        down_grad, up_grad = call(
            weights_body, (shape_of(down_proj.shape, F32), shape_of(up_proj.shape, F32)), every
        )
    with jax.named_scope("tables"):
        own_back = exchange(back, "dp", quads)
        cross_out, grads = call(
            table_body,
            (shape_of((group, QUAD * embed)), shape_of((ways, QUAD, rows, embed))),
            own_counts, own_back,
        )
        table_grads = exchange(grads, "mp").reshape(1, feature_count, rows, embed)
    return (cross_out, table_grads, down_grad, up_grad)


def solution(mesh):
    placed = (P("dp", None, None), P(None, "mp", None), P("mp", None), P(None, "mp"), P("dp", "mp"))
    return jax.shard_map(
        shards,
        mesh=mesh,
        in_specs=placed,
        out_specs=(P("dp", "mp"), P("dp", None, "mp", None), P("mp", None), P(None, "mp")),
        check_vma=False,
    )
```

time: 894 us -> 246 us (0.28)
  the two profiles are of different devices: /device:TPU:6 before, /device:TPU:1 now
where the time goes in v1:
time: 246 us; the launch traced here: 242 us
  blocking collectives  75.2 us (31%)
  waiting for transfers between devices  73.9 us (30%)
  starting transfers between devices  67.5 us (27%)
  local copies, waits for them, and re-layouts  14.8 us (6%)
  Pallas kernels  8 us (3%)
    all_to_all x4, blocking collectives, exchange(): lax.all_to_all(value, axis, 0, 0, axis_index_groups=groups, tiled=True)  75.2 us
    all_to_all x6, waiting for transfers between devices, exchange(): lax.all_to_all(value, axis, 0, 0, axis_index_groups=groups, tiled=True)  73.9 us
    all_to_all x6, starting transfers between devices, exchange(): lax.all_to_all(value, axis, 0, 0, axis_index_groups=groups, tiled=True)  67.5 us
    unnamed x20, local copies, waits for them, and re-layouts  8.66 us
    pallas_call x6, Pallas kernels, call(): pl.pallas_call(body, out_shape=out_shape, compiler_params=pltpu.CompilerP...  8 us
  transfers between devices with their start and end apart: 6, of which 5 were waited for; matrix products, arithmetic and copies ran while one was open for 2% of the time, Pallas kernels for 2%

profile of v1, /device:TPU:1, one launch (start us, length us, event | category | flops | bytes accessed | tf_op | source)
XLA Modules:
  0.0 241.9 jit_solution(5818856277070747228)
XLA Ops:
  0.7 1.4 constant_dynamic-slice_fusion.2
  2.3 0.7 reshape.52
  3.0 4.7 %all-to-all-start = ((s32[4,1,1024]{2,1,0:T(1,128)}), s32[4,1,1024]{2,1,0:T(1,128)S(1)}, u32[]{:S(2)}, u32[]{:S(2)}) async-start(s32[4,1,1024]{2,1,0:T(1,128)} %reshape.52), calls=%async_computation | async-start | bytes 32768 | tf_op jit(solution)/shard_map/inputs/all_to_all | solution.py:143
  7.8 0.8 dynamic-slice_bitcast_fusion
  8.6 2.7 %all-to-all-done = s32[4,1,1024]{2,1,0:T(1,128)S(1)} async-done(((s32[4,1,1024]{2,1,0:T(1,128)}), s32[4,1,1024]{2,1,0:T(1,128)S(1)}, u32[]{:S(2)}, u32[]{:S(2)}) %all-to-all-start) | async-done | bytes 16416 | tf_op jit(solution)/shard_map/inputs/all_to_all | solution.py:143
  11.3 17.1 %all-to-all-start.1 = ((bf16[16,64,256]{2,1,0:T(8,128)(2,1)}), bf16[16,64,256]{2,1,0:T(8,128)(2,1)S(1)}, u32[]{:S(2)}, u32[]{:S(2)}) async-start(bf16[16,64,256]{2,1,0:T(8,128)(2,1)} %dynamic-slice_bitcast_fusion), calls=%async_computation.1 | async-start | bytes 1048576 | tf_op jit(solution)/shard_map/inputs/all_to_all | solution.py:143
  28.5 0.7 copy.20
  29.2 10.8 %all-to-all-done.1 = bf16[16,64,256]{2,1,0:T(8,128)(2,1)S(1)} async-done(((bf16[16,64,256]{2,1,0:T(8,128)(2,1)}), bf16[16,64,256]{2,1,0:T(8,128)(2,1)S(1)}, u32[]{:S(2)}, u32[]{:S(2)}) %all-to-all-start.1) | async-done | bytes 524320 | tf_op jit(solution)/shard_map/inputs/all_to_all | solution.py:143
  40.0 3.3 %all-to-all-start.2 = ((bf16[4,64,256]{2,1,0:T(8,128)(2,1)}), bf16[4,64,256]{2,1,0:T(8,128)(2,1)S(1)}, u32[]{:S(2)}, u32[]{:S(2)}) async-start(bf16[4,64,256]{2,1,0:T(8,128)(2,1)} %bitcast.21), calls=%async_computation.2 | async-start | bytes 262144 | tf_op jit(solution)/shard_map/inputs/all_to_all | solution.py:143
  43.3 1.0 constant_dynamic-slice_fusion
  44.8 0.7 reduce.2
  45.7 1.8 counts.3.counts_ref
  49.4 15.7 %all_to_all.50 = bf16[64,8,256]{2,1,0:T(8,128)(2,1)S(1)} all-to-all(bf16[64,8,256]{2,1,0:T(8,128)(2,1)S(1)} %bitcast.27), channel_id=1, replica_groups={{0,16,512,528,1,17,513,529,2,18,514,530,3,19,515,531,4,20,516,532,5,21,..., dimensions={0} | all-to-all | bytes 524288 | tf_op jit(solution)/shard_map/ranks/all_to_all | solution.py:143
  65.1 14.0 %all_to_all.51 = bf16[64,8,256]{2,1,0:T(8,128)(2,1)S(1)} all-to-all(bf16[64,8,256]{2,1,0:T(8,128)(2,1)S(1)} %broadcast_in_dim.8), channel_id=1, replica_groups={{0,16,512,528,1,17,513,529,2,18,514,530,3,19,515,531,4,20,516,532,5,21,..., dimensions={0} | all-to-all | bytes 524288 | tf_op jit(solution)/shard_map/ranks/all_to_all | solution.py:143
  79.1 0.9 copy-done.3
  80.0 0.9 copy-done.5
  80.9 1.0 cross.1
  81.9 7.5 %all_to_all.52.back_ref = bf16[4,2,64,256]{3,2,1,0:T(8,128)(2,1)S(1)} all-to-all(bf16[4,2,64,256]{3,2,1,0:T(8,128)(2,1)S(1)} %get-tuple-element.16), channel_id=1, replica_groups={{0,16,512,528},{32,48,544,560},{64,80,576,592},{96,112,608,624},{128,14..., dimensions={0} | all-to-all | bytes 524288 | tf_op jit(solution)/shard_map/tables/all_to_all | solution.py:143
  89.4 19.1 %all-to-all-start.7 = ((bf16[16,32,256]{2,1,0:T(8,128)(2,1)}), bf16[16,32,256]{2,1,0:T(8,128)(2,1)}, u32[]{:S(2)}, u32[]{:S(2)}) async-start(bf16[16,32,256]{2,1,0:T(8,128)(2,1)} %bitcast.11), calls=%async_computation.7 | async-start | bytes 524288 | tf_op jit(solution)/shard_map/weights/all_to_all | solution.py:143
  109.1 1.8 counts.2.counts_ref
  110.9 1.5 tables.1
  112.4 1.3 copy-done.1
  113.7 19.5 %all-to-all-done.7 = bf16[16,32,256]{2,1,0:T(8,128)(2,1)} async-done(((bf16[16,32,256]{2,1,0:T(8,128)(2,1)}), bf16[16,32,256]{2,1,0:T(8,128)(2,1)}, u32[]{:S(2)}, u32[]{:S(2)}) %all-to-all-start.7) | async-done | bytes 262176 | tf_op jit(solution)/shard_map/weights/all_to_all | solution.py:143
  133.3 12.0 %all-to-all-start.6 = ((bf16[16,4,64,256]{3,2,1,0:T(8,128)(2,1)}), bf16[16,4,64,256]{3,2,1,0:T(8,128)(2,1)}, u32[]{:S(2)}, u32[]{:S(2)}) async-start(bf16[16,4,64,256]{3,2,1,0:T(8,128)(2,1)} %copy-done.1), calls=%async_computation.6 | async-start | bytes 4194304 | tf_op jit(solution)/shard_map/tables/all_to_all | solution.py:143
  145.2 1.0 reduce_sum.25
  146.2 27.7 %all-to-all-done.6 = bf16[16,4,64,256]{3,2,1,0:T(8,128)(2,1)} async-done(((bf16[16,4,64,256]{3,2,1,0:T(8,128)(2,1)}), bf16[16,4,64,256]{3,2,1,0:T(8,128)(2,1)}, u32[]{:S(2)}, u32[]{:S(2)}) %all-to-all-start.6) | async-done | bytes 2097184 | tf_op jit(solution)/shard_map/tables/all_to_all | solution.py:143
  174.0 38.0 %all_to_all.53 = bf16[16,32,256]{2,1,0:T(8,128)(2,1)S(1)} all-to-all(bf16[16,32,256]{2,1,0:T(8,128)(2,1)S(1)} %broadcast_in_dim.9), channel_id=1, replica_groups={{0,32,64,96,128,160,192,224,256,288,320,352,384,416,448,480},{16,48,80,..., dimensions={0} | all-to-all | bytes 524288 | tf_op jit(solution)/shard_map/weights/all_to_all | solution.py:143
  211.9 1.0 broadcast_in_dim.22
  213.0 11.3 %all-to-all-start.9 = ((bf16[4,2,256,256]{3,2,1,0:T(8,128)(2,1)}), bf16[4,2,256,256]{3,2,1,0:T(8,128)(2,1)S(1)}, u32[]{:S(2)}, u32[]{:S(2)}) async-start(bf16[4,2,256,256]{3,2,1,0:T(8,128)(2,1)} %broadcast_in_dim.22), calls=%async_computation.9 | async-start | bytes 2097152 | tf_op jit(solution)/shard_map/weights/all_to_all | solution.py:143
  224.3 13.1 %all-to-all-done.9.sums_ref = bf16[4,2,256,256]{3,2,1,0:T(8,128)(2,1)S(1)} async-done(((bf16[4,2,256,256]{3,2,1,0:T(8,128)(2,1)}), bf16[4,2,256,256]{3,2,1,0:T(8,128)(2,1)S(1)}, u32[]{:S(2)}, u32[]{:S(2)}) %all-to-all-start.9) | async-done | bytes 1048608 | tf_op jit(solution)/shard_map/weights/all_to_all | solution.py:143
  237.3 1.4 weights.1
  238.8 3.2 %copy.22 = bf16[1,64,64,256]{3,2,1,0:T(8,128)(2,1)} copy(bf16[1,64,64,256]{3,2,1,0:T(8,128)(2,1)} %bitcast.10) | data formatting | bytes 4194304
  (26 shorter events, 3.5 us)
Async XLA Ops:
  0.6 7.1 %copy-start = (bf16[64,64,256]{2,1,0:T(8,128)(2,1)S(1)}, bf16[64,64,256]{2,1,0:T(8,128)(2,1)}, u32[]{:S(2)}) copy-start(bf16[64,64,256]{2,1,0:T(8,128)(2,1)} %param.6) | copy-start | bytes 6291460
  0.6 27.8 %copy-start.7 = (bf16[64,1024]{1,0:T(8,128)(2,1)S(1)}, bf16[64,1024]{1,0:T(8,128)(2,1)}, u32[]{:S(2)}) copy-start(bf16[64,1024]{1,0:T(8,128)(2,1)} %param.9) | copy-start | bytes 393220
  3.0 8.3 %all-to-all-start = ((s32[4,1,1024]{2,1,0:T(1,128)}), s32[4,1,1024]{2,1,0:T(1,128)S(1)}, u32[]{:S(2)}, u32[]{:S(2)}) async-start(s32[4,1,1024]{2,1,0:T(1,128)} %reshape.52), calls=%async_computation | async-start | bytes 32768 | tf_op jit(solution)/shard_map/inputs/all_to_all | solution.py:143
  11.3 28.6 %all-to-all-start.1 = ((bf16[16,64,256]{2,1,0:T(8,128)(2,1)}), bf16[16,64,256]{2,1,0:T(8,128)(2,1)S(1)}, u32[]{:S(2)}, u32[]{:S(2)}) async-start(bf16[16,64,256]{2,1,0:T(8,128)(2,1)} %dynamic-slice_bitcast_fusion), calls=%async_computation.1 | async-start | bytes 1048576 | tf_op jit(solution)/shard_map/inputs/all_to_all | solution.py:143
  40.0 7.5 %all-to-all-start.2 = ((bf16[4,64,256]{2,1,0:T(8,128)(2,1)}), bf16[4,64,256]{2,1,0:T(8,128)(2,1)S(1)}, u32[]{:S(2)}, u32[]{:S(2)}) async-start(bf16[4,64,256]{2,1,0:T(8,128)(2,1)} %bitcast.21), calls=%async_computation.2 | async-start | bytes 262144 | tf_op jit(solution)/shard_map/inputs/all_to_all | solution.py:143
  48.1 0.7 copy-start.2
  48.7 0.7 copy-start.4
  49.4 59.2 %copy-start.6 = (s32[64,64,16]{1,2,0:T(8,128)S(1)}, s32[64,64,16]{1,2,0:T(8,128)}, u32[]{:S(2)}) copy-start(s32[64,64,16]{1,2,0:T(8,128)} %param.5) | copy-start | bytes 786436
  79.1 0.9 copy-start.3
  80.0 0.9 copy-start.5
  89.4 43.8 %all-to-all-start.7 = ((bf16[16,32,256]{2,1,0:T(8,128)(2,1)}), bf16[16,32,256]{2,1,0:T(8,128)(2,1)}, u32[]{:S(2)}, u32[]{:S(2)}) async-start(bf16[16,32,256]{2,1,0:T(8,128)(2,1)} %bitcast.11), calls=%async_computation.7 | async-start | bytes 524288 | tf_op jit(solution)/shard_map/weights/all_to_all | solution.py:143
  112.4 1.3 copy-start.1
  133.3 40.7 %all-to-all-start.6 = ((bf16[16,4,64,256]{3,2,1,0:T(8,128)(2,1)}), bf16[16,4,64,256]{3,2,1,0:T(8,128)(2,1)}, u32[]{:S(2)}, u32[]{:S(2)}) async-start(bf16[16,4,64,256]{3,2,1,0:T(8,128)(2,1)} %copy-done.1), calls=%async_computation.6 | async-start | bytes 4194304 | tf_op jit(solution)/shard_map/tables/all_to_all | solution.py:143
  213.0 24.4 %all-to-all-start.9 = ((bf16[4,2,256,256]{3,2,1,0:T(8,128)(2,1)}), bf16[4,2,256,256]{3,2,1,0:T(8,128)(2,1)S(1)}, u32[]{:S(2)}, u32[]{:S(2)}) async-start(bf16[4,2,256,256]{3,2,1,0:T(8,128)(2,1)} %broadcast_in_dim.22), calls=%async_computation.9 | async-start | bytes 2097152 | tf_op jit(solution)/shard_map/weights/all_to_all | solution.py:143

commit v2 on v1

v2 whole, which is shorter than its diff:
```python
import math

import jax
import jax.numpy as jnp
from jax import lax
from jax.experimental import pallas as pl
from jax.experimental.pallas import tpu as pltpu
from jax.sharding import PartitionSpec as P

BF16 = jnp.bfloat16
F32 = jnp.float32
VMEM_LIMIT = 12 * 1024 * 1024

QUAD = 4


def layout_of(dp_count, mp_count):
    depth = dp_count // 2
    pairs = depth // 2

    def member(pair, quad):
        return (quad // 2) * depth + pair * 2 + quad % 2

    window = math.isqrt(pairs)
    quads = [[member(pair, quad) for quad in range(QUAD)] for pair in range(pairs)]
    near = [
        [member(start + index, quad) for index in range(window)]
        for quad in range(QUAD)
        for start in range(0, pairs, window)
    ]
    far = [
        [member(pair, quad) for pair in range(index, pairs, window)]
        for quad in range(QUAD)
        for index in range(window)
    ]
    blocks = [
        [member(pair, quad) * mp_count + index for index in range(mp_count) for quad in range(QUAD)]
        for pair in range(pairs)
    ]
    return quads, near, far, blocks


def call(body, out_shape, *operands, after=()):
    def run(*refs):
        body(*refs[: len(operands)], *refs[len(operands) + len(after) :])

    return pl.pallas_call(
        run,
        out_shape=out_shape,
        in_specs=[
            pl.BlockSpec(memory_space=pltpu.SMEM if operand.ndim == 1 else pltpu.VMEM)
            for operand in operands
        ]
        + [pl.BlockSpec(memory_space=pl.ANY)] * len(after),
        compiler_params=pltpu.CompilerParams(vmem_limit_bytes=VMEM_LIMIT),
    )(*operands, *after)


def contract(left, right, left_dim, right_dim):
    return lax.dot_general(
        left, right, (((left_dim,), (right_dim,)), ((), ())), preferred_element_type=F32
    )


def place_of(quad_ref, step, extent):
    return pl.ds(pl.multiple_of(lax.bitwise_xor(quad_ref[0], step) * extent, extent), extent)


def count_body(ids_ref, counts_ref):
    bag_size, columns = ids_ref.shape
    rows_step, columns_step = 64, 256

    def rows_at(index, carry):
        base = pl.multiple_of(index * rows_step, rows_step)
        rows = lax.broadcasted_iota(jnp.int32, (rows_step, columns_step), 0) + base
        for start in range(0, columns, columns_step):
            span = slice(start, start + columns_step)
            total = jnp.zeros((rows_step, columns_step), F32)
            for slot in range(bag_size):
                total = total + jnp.where(rows == ids_ref[slot : slot + 1, span], 1.0, 0.0)
            counts_ref[pl.ds(base, rows_step), span] = total.astype(BF16)
        return carry

    lax.fori_loop(0, counts_ref.shape[0] // rows_step, rows_at, 0)


def forward_body(
    quad_ref, counts_ref, table_ref, grad0_ref, grad1_ref, grad2_ref, grad3_ref, down_ref, up_ref,
    state_ref, part_ref,
):
    samples = counts_ref.shape[1]
    group = samples // QUAD
    pooled = contract(counts_ref[...], table_ref[...], 0, 0).astype(BF16)
    state_ref[0] = pooled
    for step, one_ref in enumerate((grad0_ref, grad1_ref, grad2_ref, grad3_ref)):
        state_ref[1, step * group : (step + 1) * group, :] = one_ref[...]
    scaled = (state_ref[1].astype(F32) * pooled.astype(F32)).astype(BF16)
    rank_part = contract(pooled, down_ref[...], 1, 0).astype(BF16)
    back_part = contract(scaled, up_ref[...], 1, 1).astype(BF16)
    for step in range(QUAD):
        rows = place_of(quad_ref, step, group)
        part_ref[0, rows, :] = rank_part[step * group : (step + 1) * group]
        part_ref[1, rows, :] = back_part[step * group : (step + 1) * group]


def cross_body(
    quad_ref, ranks_ref, state_ref, down_ref, up_ref,
    parts_ref, back0_ref, back1_ref, back2_ref, back3_ref,
):
    group = state_ref.shape[1] // QUAD

    def in_steps(index):
        return jnp.concatenate(
            [ranks_ref[index, place_of(quad_ref, step, group), :] for step in range(QUAD)], axis=0
        )

    rank_act = in_steps(0)
    rank_grad = in_steps(1)
    pooled = state_ref[0]
    pooled_f = pooled.astype(F32)
    upstream = state_ref[1].astype(F32)
    scaled = (upstream * pooled_f).astype(BF16)
    parts_ref[0] = contract(rank_act, scaled, 0, 0).astype(BF16)
    parts_ref[1] = contract(pooled, rank_grad, 0, 0).astype(BF16)
    scale_map = contract(rank_act, up_ref[...], 1, 0)
    cross = (pooled_f * scale_map + pooled_f).astype(BF16)
    back = contract(rank_grad, down_ref[...], 1, 1)
    pooled_grad = (upstream * scale_map + upstream + back).astype(BF16)
    for step, one_ref in enumerate((back0_ref, back1_ref, back2_ref, back3_ref)):
        one_ref[0] = cross[step * group : (step + 1) * group]
        one_ref[1] = pooled_grad[step * group : (step + 1) * group]


def add_body(slices_ref, copies_ref):
    total = jnp.sum(slices_ref[...].astype(F32), axis=0).astype(BF16)
    for index in range(copies_ref.shape[0]):
        copies_ref[index] = total


def copy_body(value_ref, copies_ref):
    for index in range(copies_ref.shape[0]):
        copies_ref[index] = value_ref[...]


def arrange_body(quad_ref, back0_ref, back1_ref, back2_ref, back3_ref, cross_ref, pooled_grad_ref):
    embed = back0_ref.shape[2]
    for step, one_ref in enumerate((back0_ref, back1_ref, back2_ref, back3_ref)):
        cross_ref[:, place_of(quad_ref, step, embed)] = one_ref[0]
        pooled_grad_ref[lax.bitwise_xor(quad_ref[0], step)] = one_ref[1]


def table_body(order_ref, counts_ref, grads_ref, out_ref):
    count, rows, embed = out_ref.shape
    columns = counts_ref.shape[1]
    group = columns // count
    counts = counts_ref[...].astype(F32)
    tall = jnp.concatenate([counts] * count, axis=0)
    row_of = lax.broadcasted_iota(jnp.int32, tall.shape, 0) // rows
    column_of = lax.broadcasted_iota(jnp.int32, tall.shape, 1) // group
    blocks = jnp.where(row_of == column_of, tall, 0.0).astype(BF16)
    sums = contract(blocks, grads_ref[...].reshape(columns, embed), 1, 0)
    out_ref[...] = sums.astype(BF16).reshape(count, rows, embed)


def sum_tables(order, counts, grads):
    features, group, embed = grads.shape
    rows = counts.shape[0]
    return pl.pallas_call(
        table_body,
        out_shape=shape_of((features, rows, embed)),
        grid_spec=pltpu.PrefetchScalarGridSpec(
            num_scalar_prefetch=1,
            grid=(features // QUAD,),
            in_specs=[
                pl.BlockSpec((rows, QUAD * group), lambda index, order: (0, order[index])),
                pl.BlockSpec((QUAD, group, embed), lambda index, order: (index, 0, 0)),
            ],
            out_specs=pl.BlockSpec((QUAD, rows, embed), lambda index, order: (order[index], 0, 0)),
        ),
        compiler_params=pltpu.CompilerParams(vmem_limit_bytes=VMEM_LIMIT),
    )(order, counts, grads)


def weights_body(sums_ref, down_ref, up_ref):
    width = sums_ref.shape[3]
    for quad in range(QUAD):
        span = slice(quad * width, (quad + 1) * width)
        up_ref[:, span] = sums_ref[quad, 0].astype(F32)
        down_ref[span, :] = sums_ref[quad, 1].astype(F32)


def shape_of(shape, dtype=BF16):
    return jax.ShapeDtypeStruct(shape, dtype)


def shards(bag_ids, tables, down_proj, up_proj, cotangent):
    dp_count, ways = lax.axis_size("dp"), lax.axis_size("mp")
    depth = dp_count // 2
    quads, near, far, blocks = layout_of(dp_count, ways)
    window, windows, members = len(near[0]), len(far[0]), len(blocks[0])
    place = lax.axis_index("dp")
    quad = (place // depth) * 2 + place % 2
    quad_at = quad.reshape(1)
    shard_index = lax.axis_index("mp")
    group, feature_count, bag_size = bag_ids.shape
    _, rows, embed = tables.shape
    rank = down_proj.shape[1]
    samples = QUAD * group

    def exchange(value, axis, groups=None):
        return lax.all_to_all(value, axis, 0, 0, axis_index_groups=groups, tiled=True)

    def swap(values):
        got = [values[0]]
        for step in range(1, QUAD):
            mask = (step // 2) * depth + step % 2
            pairs = [(index, index ^ mask) for index in range(dp_count)]
            got.append(lax.ppermute(values[step], "dp", pairs))
        return got

    def double(value, mask):
        other = lax.ppermute(value, "mp", [(index, index ^ mask) for index in range(ways)])
        return jnp.concatenate([value, other], axis=0)

    with jax.named_scope("inputs"):
        table_parts = lax.dynamic_index_in_dim(
            tables.reshape(ways, QUAD, rows, embed), quad, 1, keepdims=False
        )
        table = exchange(table_parts, "mp").reshape(ways * rows, embed)
        shard_ids = jnp.transpose(
            lax.dynamic_slice_in_dim(bag_ids, shard_index * QUAD, QUAD, 1), (1, 2, 0)
        )
        quad_ids = swap(
            [lax.dynamic_index_in_dim(shard_ids, quad ^ step, 0, keepdims=False) for step in range(QUAD)]
        )
        quad_grads = swap(
            [
                lax.dynamic_slice_in_dim(cotangent, (quad ^ step) * embed, embed, 1)
                for step in range(QUAD)
            ]
        )
        down = lax.dynamic_slice_in_dim(down_proj, quad * embed, embed, 0)
        up = lax.dynamic_slice_in_dim(up_proj, quad * embed, embed, 1)

    with jax.named_scope("counts"):
        quad_counts = call(
            count_body, shape_of((ways * rows, samples)), jnp.concatenate(quad_ids, axis=1)
        )
        row_ids = jnp.transpose(bag_ids, (2, 1, 0)).reshape(bag_size, feature_count * group)
        row_counts = call(
            count_body, shape_of((rows, feature_count * group)), row_ids - shard_index * rows
        )

    with jax.named_scope("forward"):
        state, part = call(
            forward_body, (shape_of((2, samples, embed)), shape_of((2, samples, rank))),
            quad_at, quad_counts, table, *quad_grads, down, up,
        )
    with jax.named_scope("ranks"):
        piece = 2 * samples // members
        pieces = exchange(part.reshape(members, piece, rank), ("dp", "mp"), blocks)
        copies = call(add_body, shape_of((members, piece, rank)), pieces, after=(row_counts,))
        ranks = exchange(copies, ("dp", "mp"), blocks).reshape(2, samples, rank)

    with jax.named_scope("cross"):
        parts, *backs = call(
            cross_body, (shape_of((2, embed, rank)),) + (shape_of((2, group, embed)),) * QUAD,
            quad_at, ranks, state, down, up,
        )

    slab = (2 * embed // window, rank)
    with jax.named_scope("near_sums"):
        near_parts = exchange(parts.reshape((window,) + slab), "dp", near)
        cross_out, grads = call(
            arrange_body, (shape_of((group, QUAD * embed)), shape_of((QUAD, group, embed))),
            quad_at, *swap(backs),
        )
        near_copies = call(add_body, shape_of((windows,) + slab), near_parts, after=(grads,))
    with jax.named_scope("far_sums"):
        far_parts = exchange(near_copies, "dp", far)
        steps = [ways >> (index + 1) for index in range(ways.bit_length() - 1)]
        for mask in steps[:-2]:
            grads = double(grads, mask)
        far_copies = call(add_body, shape_of((window,) + slab), far_parts, after=(grads,))
    with jax.named_scope("near_gather"):
        sums = exchange(far_copies, "dp", near)
        grads = double(grads, steps[-2])
        quad_copies = call(
            copy_body, shape_of((QUAD, window) + slab), sums, after=(grads,)
        )
    with jax.named_scope("quad_gather"):
        every = exchange(quad_copies, "dp", quads).reshape(QUAD, 2, embed, rank)
        grads = double(grads, steps[-1])
        order = [shard_index]
        for mask in steps:
            order = order + [index ^ mask for index in order]
        table_grads = sum_tables(jnp.stack(order), row_counts, grads)[None]
        down_grad, up_grad = call(
            weights_body, (shape_of(down_proj.shape, F32), shape_of(up_proj.shape, F32)), every
        )
    return (cross_out, table_grads, down_grad, up_grad)


def solution(mesh):
    placed = (P("dp", None, None), P(None, "mp", None), P("mp", None), P(None, "mp"), P("dp", "mp"))
    return jax.shard_map(
        shards,
        mesh=mesh,
        in_specs=placed,
        out_specs=(P("dp", "mp"), P("dp", None, "mp", None), P("mp", None), P(None, "mp")),
        check_vma=False,
    )
```

time: 246 us -> 213 us (0.87)
  blocking collectives: 75.2 us -> 14 us
  starting transfers between devices: 67.5 us -> 108 us
  waiting for transfers between devices: 73.9 us -> 44.1 us
  Pallas kernels: 8 us -> 21 us
  local copies, waits for them, and re-layouts: 14.8 us -> 21.5 us
    all_to_all x4 -> x1, blocking collectives: 75.2 us -> 14 us  [exchange(): lax.all_to_all(value, axis, 0, 0, axis_index_groups=groups, tiled=True)]
    all_to_all x6, waiting for transfers between devices: 73.9 us -> 21.2 us  [exchange(): lax.all_to_all(value, axis, 0, 0, axis_index_groups=groups, tiled=True)]
    ppermute x0 -> x13, starting transfers between devices: none -> 41.6 us  [the longest x9 25 us: swap(): got.append(lax.ppermute(values[step], 'dp', pairs))]
    ppermute x0 -> x13, waiting for transfers between devices: none -> 23 us  [the longest x4 21.3 us: double(): lax.ppermute(value, 'mp', [(index, index ^ mask) for index in range(ways)])]
    pallas_call x6 -> x11, Pallas kernels: 8 us -> 21 us  [the longest x1 11.2 us: sum_tables(): pl.pallas_call(table_body, out_shape=shape_of((features, rows, embed)), g...]
    concatenate x0 -> x2, local copies, waits for them, and re-layouts: none -> 3.42 us  [double(): return jnp.concatenate([value, other], axis=0)]
    unnamed x20 -> x23, local copies, waits for them, and re-layouts: 8.66 us -> 11.4 us
  transfers between devices with their start and end apart: 6 -> 19, of which waited for: 5 -> 8; matrix products, arithmetic and copies ran while one was open for 2% -> 8% of each run, Pallas kernels for 2% -> 7%
where the time goes in v2:
time: 213 us; the launch traced here: 211 us
  starting transfers between devices  108 us (51%)
  waiting for transfers between devices  44.1 us (21%)
  local copies, waits for them, and re-layouts  21.5 us (10%)
  Pallas kernels  21 us (10%)
  blocking collectives  14 us (7%)
    all_to_all x6, starting transfers between devices, exchange(): lax.all_to_all(value, axis, 0, 0, axis_index_groups=groups, tiled=True)  66 us
    ppermute x9, starting transfers between devices, swap(): got.append(lax.ppermute(values[step], 'dp', pairs))  25 us
    ppermute x4, waiting for transfers between devices, double(): lax.ppermute(value, 'mp', [(index, index ^ mask) for index in range(ways)])  21.3 us
    all_to_all x6, waiting for transfers between devices, exchange(): lax.all_to_all(value, axis, 0, 0, axis_index_groups=groups, tiled=True)  21.2 us
    ppermute x4, starting transfers between devices, double(): lax.ppermute(value, 'mp', [(index, index ^ mask) for index in range(ways)])  16.6 us
    all_to_all x1, blocking collectives, exchange(): lax.all_to_all(value, axis, 0, 0, axis_index_groups=groups, tiled=True)  14 us
    unnamed x23, local copies, waits for them, and re-layouts  11.4 us
    pallas_call x1, Pallas kernels, sum_tables(): pl.pallas_call(table_body, out_shape=shape_of((features, rows, embed)), g...  11.2 us
  transfers between devices with their start and end apart: 19, of which 8 were waited for; matrix products, arithmetic and copies ran while one was open for 8% of the time, Pallas kernels for 7%

profile of v2, /device:TPU:1, one launch (start us, length us, event | category | flops | bytes accessed | tf_op | source)
XLA Modules:
  0.0 211.2 jit_solution(5906738576422462222)
XLA Ops:
  3.1 17.5 %all-to-all-start = ((bf16[16,64,256]{2,1,0:T(8,128)(2,1)}), bf16[16,64,256]{2,1,0:T(8,128)(2,1)S(1)}, u32[]{:S(2)}, u32[]{:S(2)}) async-start(bf16[16,64,256]{2,1,0:T(8,128)(2,1)} %dynamic-slice_bitcast_fusion), calls=%async_computation | async-start | bytes 1048576 | tf_op jit(solution)/shard_map/inputs/all_to_all | solution.py:211
  21.2 1.9 collective-permute-start.5
  23.1 1.9 collective-permute-start.3
  25.1 1.9 constant_dynamic-slice_fusion.9
  28.4 4.2 %collective-permute-start.2 = (s32[16,64]{1,0:T(8,128)S(1)}, s32[16,64]{1,0:T(8,128)S(1)}, u32[]{:S(2)}, u32[]{:S(2)}) collective-permute-start(s32[16,64]{1,0:T(8,128)S(1)} %bitcast.47), channel_id=1, source_target_pairs={{0,528},{16,512},{32,560},{48,544},{64,592},{80,576},{96,624},{112... | collective-permute-start | bytes 12296 | tf_op jit(solution)/shard_map/inputs/ppermute | solution.py:218
  33.9 3.4 %collective-permute-start = (s32[16,64]{1,0:T(8,128)S(1)}, s32[16,64]{1,0:T(8,128)S(1)}, u32[]{:S(2)}, u32[]{:S(2)}) collective-permute-start(s32[16,64]{1,0:T(8,128)S(1)} %bitcast.46), channel_id=1, source_target_pairs={{0,16},{16,0},{32,48},{48,32},{64,80},{80,64},{96,112},{112,96},{1... | collective-permute-start | bytes 12296 | tf_op jit(solution)/shard_map/inputs/ppermute | solution.py:218
  38.6 1.9 collective-permute-start.1
  41.8 3.4 %collective-permute-start.4 = (bf16[64,256]{1,0:T(8,128)(2,1)}, bf16[64,256]{1,0:T(8,128)(2,1)S(1)}, u32[]{:S(2)}, u32[]{:S(2)}) collective-permute-start(bf16[64,256]{1,0:T(8,128)(2,1)} %get-tuple-element.44), channel_id=1, source_target_pairs={{0,512},{16,528},{32,544},{48,560},{64,576},{80,592},{96,608},{112... | collective-permute-start | bytes 98312 | tf_op jit(solution)/shard_map/inputs/ppermute | solution.py:218
  45.9 1.8 counts.2.refs_1_
  49.7 9.6 %all-to-all-start.1 = ((bf16[64,8,256]{2,1,0:T(8,128)(2,1)}), bf16[64,8,256]{2,1,0:T(8,128)(2,1)S(1)}, u32[]{:S(2)}, u32[]{:S(2)}) async-start(bf16[64,8,256]{2,1,0:T(8,128)(2,1)} %bitcast.43), calls=%async_computation.1 | async-start | bytes 524288 | tf_op jit(solution)/shard_map/ranks/all_to_all | solution.py:211
  64.2 5.0 %all-to-all-done.1.refs_0_ = bf16[64,8,256]{2,1,0:T(8,128)(2,1)S(1)} async-done(((bf16[64,8,256]{2,1,0:T(8,128)(2,1)}), bf16[64,8,256]{2,1,0:T(8,128)(2,1)S(1)}, u32[]{:S(2)}, u32[]{:S(2)}) %all-to-all-start.1) | async-done | bytes 262176 | tf_op jit(solution)/shard_map/ranks/all_to_all | solution.py:211
  69.3 14.0 %all_to_all.35 = bf16[64,8,256]{2,1,0:T(8,128)(2,1)S(1)} all-to-all(bf16[64,8,256]{2,1,0:T(8,128)(2,1)S(1)} %ranks.1), channel_id=1, replica_groups={{0,16,512,528,1,17,513,529,2,18,514,530,3,19,515,531,4,20,516,532,5,21,..., dimensions={0} | all-to-all | bytes 524288 | tf_op jit(solution)/shard_map/ranks/all_to_all | solution.py:211
  85.3 3.8 %all-to-all-start.3 = ((bf16[4,128,256]{2,1,0:T(8,128)(2,1)}), bf16[4,128,256]{2,1,0:T(8,128)(2,1)S(1)}, u32[]{:S(2)}, u32[]{:S(2)}) async-start(bf16[4,128,256]{2,1,0:T(8,128)(2,1)} %bitcast.32), calls=%async_computation.3 | async-start | bytes 524288 | tf_op jit(solution)/shard_map/near_sums/all_to_all | solution.py:211
  89.1 2.2 %collective-permute-start.6 = (bf16[2,64,256]{2,1,0:T(8,128)(2,1)S(1)}, bf16[2,64,256]{2,1,0:T(8,128)(2,1)S(1)}, u32[]{:S(2)}, u32[]{:S(2)}) collective-permute-start(bf16[2,64,256]{2,1,0:T(8,128)(2,1)S(1)} %get-tuple-element.18), channel_id=1, source_target_pairs={{0,16},{16,0},{32,48},{48,32},{64,80},{80,64},{96,112},{112,96},{1... | collective-permute-start | bytes 196616 | tf_op jit(solution)/shard_map/near_sums/ppermute | solution.py:218
  91.3 1.9 collective-permute-start.7
  93.2 4.2 %collective-permute-start.8 = (bf16[2,64,256]{2,1,0:T(8,128)(2,1)S(1)}, bf16[2,64,256]{2,1,0:T(8,128)(2,1)S(1)}, u32[]{:S(2)}, u32[]{:S(2)}) collective-permute-start(bf16[2,64,256]{2,1,0:T(8,128)(2,1)S(1)} %get-tuple-element.20), channel_id=1, source_target_pairs={{0,528},{16,512},{32,560},{48,544},{64,592},{80,576},{96,624},{112... | collective-permute-start | bytes 196616 | tf_op jit(solution)/shard_map/near_sums/ppermute | solution.py:218
  99.8 7.3 %all-to-all-done.3.refs_0_ = bf16[4,128,256]{2,1,0:T(8,128)(2,1)S(1)} async-done(((bf16[4,128,256]{2,1,0:T(8,128)(2,1)}), bf16[4,128,256]{2,1,0:T(8,128)(2,1)S(1)}, u32[]{:S(2)}, u32[]{:S(2)}) %all-to-all-start.3) | async-done | bytes 262176 | tf_op jit(solution)/shard_map/near_sums/all_to_all | solution.py:211
  107.8 20.6 %all-to-all-start.4 = ((bf16[4,128,256]{2,1,0:T(8,128)(2,1)}), bf16[4,128,256]{2,1,0:T(8,128)(2,1)S(1)}, u32[]{:S(2)}, u32[]{:S(2)}) async-start(bf16[4,128,256]{2,1,0:T(8,128)(2,1)} %near_sums.3), calls=%async_computation.4 | async-start | bytes 524288 | tf_op jit(solution)/shard_map/far_sums/all_to_all | solution.py:211
  128.4 1.9 collective-permute-start.9
  130.3 5.6 %collective-permute-done.9 = bf16[4,64,256]{2,1,0:T(8,128)(2,1)S(1)} collective-permute-done((bf16[4,64,256]{2,1,0:T(8,128)(2,1)S(1)}, bf16[4,64,256]{2,1,0:T(8,128)(2,1)S(1)}, u32[]{:S(2)}, u32[]{:S(2)}) %collective-permute-start.9) | collective-permute-done | bytes 131104 | tf_op jit(solution)/shard_map/far_sums/ppermute | solution.py:222
  135.9 2.6 %collective-permute-start.10 = (bf16[8,64,256]{2,1,0:T(8,128)(2,1)S(1)}, bf16[8,64,256]{2,1,0:T(8,128)(2,1)S(1)}, u32[]{:S(2)}, u32[]{:S(2)}) collective-permute-start(bf16[8,64,256]{2,1,0:T(8,128)(2,1)S(1)} %pad_maximum_fusion), channel_id=1, source_target_pairs={{0,4},{1,5},{2,6},{3,7},{4,0},{5,1},{6,2},{7,3},{8,12},{9,13},{10,... | collective-permute-start | bytes 786440 | tf_op jit(solution)/shard_map/far_sums/ppermute | solution.py:222
  140.0 5.4 %collective-permute-done.10 = bf16[8,64,256]{2,1,0:T(8,128)(2,1)S(1)} collective-permute-done((bf16[8,64,256]{2,1,0:T(8,128)(2,1)S(1)}, bf16[8,64,256]{2,1,0:T(8,128)(2,1)S(1)}, u32[]{:S(2)}, u32[]{:S(2)}) %collective-permute-start.10) | collective-permute-done | bytes 262176 | tf_op jit(solution)/shard_map/far_sums/ppermute | solution.py:222
  146.3 8.9 %all-to-all-done.4.refs_0_ = bf16[4,128,256]{2,1,0:T(8,128)(2,1)S(1)} async-done(((bf16[4,128,256]{2,1,0:T(8,128)(2,1)}), bf16[4,128,256]{2,1,0:T(8,128)(2,1)S(1)}, u32[]{:S(2)}, u32[]{:S(2)}) %all-to-all-start.4) | async-done | bytes 262176 | tf_op jit(solution)/shard_map/far_sums/all_to_all | solution.py:211
  155.9 10.3 %all-to-all-start.5 = ((bf16[4,128,256]{2,1,0:T(8,128)(2,1)}), bf16[4,128,256]{2,1,0:T(8,128)(2,1)S(1)}, u32[]{:S(2)}, u32[]{:S(2)}) async-start(bf16[4,128,256]{2,1,0:T(8,128)(2,1)} %far_sums.1), calls=%async_computation.5 | async-start | bytes 524288 | tf_op jit(solution)/shard_map/near_gather/all_to_all | solution.py:211
  166.3 2.1 %collective-permute-start.11 = (bf16[16,64,256]{2,1,0:T(8,128)(2,1)S(1)}, bf16[16,64,256]{2,1,0:T(8,128)(2,1)S(1)}, u32[]{:S(2)}, u32[]{:S(2)}) collective-permute-start(bf16[16,64,256]{2,1,0:T(8,128)(2,1)S(1)} %get-tuple-element.34.refs_1_), channel_id=1, source_target_pairs={{0,2},{1,3},{2,0},{3,1},{4,6},{5,7},{6,4},{7,5},{8,10},{9,11},{10,... | collective-permute-start | bytes 1572872 | tf_op jit(solution)/shard_map/near_gather/ppermute | solution.py:222
  168.4 7.8 %collective-permute-done.11 = bf16[16,64,256]{2,1,0:T(8,128)(2,1)S(1)} collective-permute-done((bf16[16,64,256]{2,1,0:T(8,128)(2,1)S(1)}, bf16[16,64,256]{2,1,0:T(8,128)(2,1)S(1)}, u32[]{:S(2)}, u32[]{:S(2)}) %collective-permute-start.11) | collective-permute-done | bytes 524320 | tf_op jit(solution)/shard_map/near_gather/ppermute | solution.py:222
  178.3 4.3 %all-to-all-start.6 = ((bf16[4,4,128,256]{3,2,1,0:T(8,128)(2,1)}), bf16[4,4,128,256]{3,2,1,0:T(8,128)(2,1)}, u32[]{:S(2)}, u32[]{:S(2)}) async-start(bf16[4,4,128,256]{3,2,1,0:T(8,128)(2,1)} %copy-done.1), calls=%async_computation.6 | async-start | bytes 2097152 | tf_op jit(solution)/shard_map/quad_gather/all_to_all | solution.py:211
  182.6 9.9 %collective-permute-start.12 = (bf16[32,64,256]{2,1,0:T(8,128)(2,1)}, bf16[32,64,256]{2,1,0:T(8,128)(2,1)}, u32[]{:S(2)}, u32[]{:S(2)}) collective-permute-start(bf16[32,64,256]{2,1,0:T(8,128)(2,1)} %get-tuple-element.26.refs_1_), channel_id=1, source_target_pairs={{0,1},{1,0},{2,3},{3,2},{4,5},{5,4},{6,7},{7,6},{8,9},{9,8},{10,11... | collective-permute-start | bytes 3145736 | tf_op jit(solution)/shard_map/quad_gather/ppermute | solution.py:222
  192.6 2.5 %collective-permute-done.12 = bf16[32,64,256]{2,1,0:T(8,128)(2,1)} collective-permute-done((bf16[32,64,256]{2,1,0:T(8,128)(2,1)}, bf16[32,64,256]{2,1,0:T(8,128)(2,1)}, u32[]{:S(2)}, u32[]{:S(2)}) %collective-permute-start.12) | collective-permute-done | bytes 1048608 | tf_op jit(solution)/shard_map/quad_gather/ppermute | solution.py:222
  195.1 2.3 %constant_dynamic-update-slice_fusion.7.grads_ref = bf16[64,64,256]{2,1,0:T(8,128)(2,1)} fusion(bf16[64,64,256]{2,1,0:T(8,128)(2,1)} %get-tuple-element.27, bf16[32,64,256]{2,1,0:T(8,128)(2,1)} %collective-permute-done.12), kind=kLoop, calls=%fused_computation.10 | loop fusion | bytes 2097152 | tf_op jit(solution)/shard_map/quad_gather/concatenate | solution.py:223
  197.4 11.2 %quad_gather.2 = bf16[64,64,256]{2,1,0:T(8,128)(2,1)} custom-call(s32[16]{0:T(128)S(1)} %stack.67.order_ref, bf16[64,4096]{1,0:T(8,128)(2,1)S(1)} %counts.3.refs_1_.counts_ref, bf16[64,64,256]{2,1,0:T(8,128)(2,1)} %constant_dynamic-update-slice_fusion.7.grads_ref), custom_call_target="tpu_custom_call" | custom-call | tf_op jit(solution)/shard_map/quad_gather/pallas_call | solution.py:168
  208.6 2.7 %quad_gather.3 = (f32[1024,256]{1,0:T(8,128)}, f32[256,1024]{1,0:T(8,128)}) custom-call(bf16[4,2,256,256]{3,2,1,0:T(8,128)(2,1)} %bitcast.33.refs_0_), custom_call_target="tpu_custom_call" | custom-call | tf_op jit(solution)/shard_map/quad_gather/pallas_call | solution.py:47
  (53 shorter events, 26.3 us)
Async XLA Ops:
  0.6 1.6 copy-start
  0.6 19.9 %copy-start.7 = (bf16[64,1024]{1,0:T(8,128)(2,1)S(1)}, bf16[64,1024]{1,0:T(8,128)(2,1)}, u32[]{:S(2)}) copy-start(bf16[64,1024]{1,0:T(8,128)(2,1)} %param.9) | copy-start | bytes 393220
  0.7 24.5 %copy-start.5 = (s32[64,64,16]{1,2,0:T(8,128)S(1)}, s32[64,64,16]{1,2,0:T(8,128)}, u32[]{:S(2)}) copy-start(s32[64,64,16]{1,2,0:T(8,128)} %param.5) | copy-start | bytes 786436
  3.1 44.7 %all-to-all-start = ((bf16[16,64,256]{2,1,0:T(8,128)(2,1)}), bf16[16,64,256]{2,1,0:T(8,128)(2,1)S(1)}, u32[]{:S(2)}, u32[]{:S(2)}) async-start(bf16[16,64,256]{2,1,0:T(8,128)(2,1)} %dynamic-slice_bitcast_fusion), calls=%async_computation | async-start | bytes 1048576 | tf_op jit(solution)/shard_map/inputs/all_to_all | solution.py:211
  21.2 26.5 %collective-permute-start.5 = (bf16[64,256]{1,0:T(8,128)(2,1)}, bf16[64,256]{1,0:T(8,128)(2,1)S(1)}, u32[]{:S(2)}, u32[]{:S(2)}) collective-permute-start(bf16[64,256]{1,0:T(8,128)(2,1)} %get-tuple-element.41), channel_id=1, source_target_pairs={{0,528},{16,512},{32,560},{48,544},{64,592},{80,576},{96,624},{112... | collective-permute-start | bytes 98312 | tf_op jit(solution)/shard_map/inputs/ppermute | solution.py:218
  23.1 24.6 %collective-permute-start.3 = (bf16[64,256]{1,0:T(8,128)(2,1)}, bf16[64,256]{1,0:T(8,128)(2,1)S(1)}, u32[]{:S(2)}, u32[]{:S(2)}) collective-permute-start(bf16[64,256]{1,0:T(8,128)(2,1)} %get-tuple-element.42), channel_id=1, source_target_pairs={{0,16},{16,0},{32,48},{48,32},{64,80},{80,64},{96,112},{112,96},{1... | collective-permute-start | bytes 98312 | tf_op jit(solution)/shard_map/inputs/ppermute | solution.py:218
  27.0 14.5 %copy-start.6 = (s32[64,1,16]{1,2,0:T(8,128)S(1)}, s32[64,1,16]{1,2,0:T(8,128)}, u32[]{:S(2)}) copy-start(s32[64,1,16]{1,2,0:T(8,128)} %get-tuple-element.28) | copy-start | bytes 12292
  28.4 13.4 %collective-permute-start.2 = (s32[16,64]{1,0:T(8,128)S(1)}, s32[16,64]{1,0:T(8,128)S(1)}, u32[]{:S(2)}, u32[]{:S(2)}) collective-permute-start(s32[16,64]{1,0:T(8,128)S(1)} %bitcast.47), channel_id=1, source_target_pairs={{0,528},{16,512},{32,560},{48,544},{64,592},{80,576},{96,624},{112... | collective-permute-start | bytes 12296 | tf_op jit(solution)/shard_map/inputs/ppermute | solution.py:218
  33.9 11.2 %collective-permute-start = (s32[16,64]{1,0:T(8,128)S(1)}, s32[16,64]{1,0:T(8,128)S(1)}, u32[]{:S(2)}, u32[]{:S(2)}) collective-permute-start(s32[16,64]{1,0:T(8,128)S(1)} %bitcast.46), channel_id=1, source_target_pairs={{0,16},{16,0},{32,48},{48,32},{64,80},{80,64},{96,112},{112,96},{1... | collective-permute-start | bytes 12296 | tf_op jit(solution)/shard_map/inputs/ppermute | solution.py:218
  38.6 6.6 %collective-permute-start.1 = (s32[16,64]{1,0:T(8,128)S(1)}, s32[16,64]{1,0:T(8,128)}, u32[]{:S(2)}, u32[]{:S(2)}) collective-permute-start(s32[16,64]{1,0:T(8,128)S(1)} %bitcast.48), channel_id=1, source_target_pairs={{0,512},{16,528},{32,544},{48,560},{64,576},{80,592},{96,608},{112... | collective-permute-start | bytes 12296 | tf_op jit(solution)/shard_map/inputs/ppermute | solution.py:218
  41.8 5.9 %collective-permute-start.4 = (bf16[64,256]{1,0:T(8,128)(2,1)}, bf16[64,256]{1,0:T(8,128)(2,1)S(1)}, u32[]{:S(2)}, u32[]{:S(2)}) collective-permute-start(bf16[64,256]{1,0:T(8,128)(2,1)} %get-tuple-element.44), channel_id=1, source_target_pairs={{0,512},{16,528},{32,544},{48,560},{64,576},{80,592},{96,608},{112... | collective-permute-start | bytes 98312 | tf_op jit(solution)/shard_map/inputs/ppermute | solution.py:218
  48.3 0.7 copy-start.2
  49.0 0.7 copy-start.3
  49.7 19.5 %all-to-all-start.1 = ((bf16[64,8,256]{2,1,0:T(8,128)(2,1)}), bf16[64,8,256]{2,1,0:T(8,128)(2,1)S(1)}, u32[]{:S(2)}, u32[]{:S(2)}) async-start(bf16[64,8,256]{2,1,0:T(8,128)(2,1)} %bitcast.43), calls=%async_computation.1 | async-start | bytes 524288 | tf_op jit(solution)/shard_map/ranks/all_to_all | solution.py:211
  83.3 1.0 copy-start.4
  85.3 21.8 %all-to-all-start.3 = ((bf16[4,128,256]{2,1,0:T(8,128)(2,1)}), bf16[4,128,256]{2,1,0:T(8,128)(2,1)S(1)}, u32[]{:S(2)}, u32[]{:S(2)}) async-start(bf16[4,128,256]{2,1,0:T(8,128)(2,1)} %bitcast.32), calls=%async_computation.3 | async-start | bytes 524288 | tf_op jit(solution)/shard_map/near_sums/all_to_all | solution.py:211
  89.1 8.4 %collective-permute-start.6 = (bf16[2,64,256]{2,1,0:T(8,128)(2,1)S(1)}, bf16[2,64,256]{2,1,0:T(8,128)(2,1)S(1)}, u32[]{:S(2)}, u32[]{:S(2)}) collective-permute-start(bf16[2,64,256]{2,1,0:T(8,128)(2,1)S(1)} %get-tuple-element.18), channel_id=1, source_target_pairs={{0,16},{16,0},{32,48},{48,32},{64,80},{80,64},{96,112},{112,96},{1... | collective-permute-start | bytes 196616 | tf_op jit(solution)/shard_map/near_sums/ppermute | solution.py:218
  91.3 6.2 %collective-permute-start.7 = (bf16[2,64,256]{2,1,0:T(8,128)(2,1)S(1)}, bf16[2,64,256]{2,1,0:T(8,128)(2,1)S(1)}, u32[]{:S(2)}, u32[]{:S(2)}) collective-permute-start(bf16[2,64,256]{2,1,0:T(8,128)(2,1)S(1)} %get-tuple-element.19), channel_id=1, source_target_pairs={{0,512},{16,528},{32,544},{48,560},{64,576},{80,592},{96,608},{112... | collective-permute-start | bytes 196616 | tf_op jit(solution)/shard_map/near_sums/ppermute | solution.py:218
  93.2 5.9 %collective-permute-start.8 = (bf16[2,64,256]{2,1,0:T(8,128)(2,1)S(1)}, bf16[2,64,256]{2,1,0:T(8,128)(2,1)S(1)}, u32[]{:S(2)}, u32[]{:S(2)}) collective-permute-start(bf16[2,64,256]{2,1,0:T(8,128)(2,1)S(1)} %get-tuple-element.20), channel_id=1, source_target_pairs={{0,528},{16,512},{32,560},{48,544},{64,592},{80,576},{96,624},{112... | collective-permute-start | bytes 196616 | tf_op jit(solution)/shard_map/near_sums/ppermute | solution.py:218
  107.8 47.4 %all-to-all-start.4 = ((bf16[4,128,256]{2,1,0:T(8,128)(2,1)}), bf16[4,128,256]{2,1,0:T(8,128)(2,1)S(1)}, u32[]{:S(2)}, u32[]{:S(2)}) async-start(bf16[4,128,256]{2,1,0:T(8,128)(2,1)} %near_sums.3), calls=%async_computation.4 | async-start | bytes 524288 | tf_op jit(solution)/shard_map/far_sums/all_to_all | solution.py:211
  128.4 7.6 %collective-permute-start.9 = (bf16[4,64,256]{2,1,0:T(8,128)(2,1)S(1)}, bf16[4,64,256]{2,1,0:T(8,128)(2,1)S(1)}, u32[]{:S(2)}, u32[]{:S(2)}) collective-permute-start(bf16[4,64,256]{2,1,0:T(8,128)(2,1)S(1)} %get-tuple-element.22.refs_1_), channel_id=1, source_target_pairs={{0,8},{1,9},{2,10},{3,11},{4,12},{5,13},{6,14},{7,15},{8,0},{9,1},... | collective-permute-start | bytes 393224 | tf_op jit(solution)/shard_map/far_sums/ppermute | solution.py:222
  135.9 9.5 %collective-permute-start.10 = (bf16[8,64,256]{2,1,0:T(8,128)(2,1)S(1)}, bf16[8,64,256]{2,1,0:T(8,128)(2,1)S(1)}, u32[]{:S(2)}, u32[]{:S(2)}) collective-permute-start(bf16[8,64,256]{2,1,0:T(8,128)(2,1)S(1)} %pad_maximum_fusion), channel_id=1, source_target_pairs={{0,4},{1,5},{2,6},{3,7},{4,0},{5,1},{6,2},{7,3},{8,12},{9,13},{10,... | collective-permute-start | bytes 786440 | tf_op jit(solution)/shard_map/far_sums/ppermute | solution.py:222
  155.9 21.4 %all-to-all-start.5 = ((bf16[4,128,256]{2,1,0:T(8,128)(2,1)}), bf16[4,128,256]{2,1,0:T(8,128)(2,1)S(1)}, u32[]{:S(2)}, u32[]{:S(2)}) async-start(bf16[4,128,256]{2,1,0:T(8,128)(2,1)} %far_sums.1), calls=%async_computation.5 | async-start | bytes 524288 | tf_op jit(solution)/shard_map/near_gather/all_to_all | solution.py:211
  166.3 9.9 %collective-permute-start.11 = (bf16[16,64,256]{2,1,0:T(8,128)(2,1)S(1)}, bf16[16,64,256]{2,1,0:T(8,128)(2,1)S(1)}, u32[]{:S(2)}, u32[]{:S(2)}) collective-permute-start(bf16[16,64,256]{2,1,0:T(8,128)(2,1)S(1)} %get-tuple-element.34.refs_1_), channel_id=1, source_target_pairs={{0,2},{1,3},{2,0},{3,1},{4,6},{5,7},{6,4},{7,5},{8,10},{9,11},{10,... | collective-permute-start | bytes 1572872 | tf_op jit(solution)/shard_map/near_gather/ppermute | solution.py:222
  177.4 1.0 copy-start.1
  178.3 30.2 %all-to-all-start.6 = ((bf16[4,4,128,256]{3,2,1,0:T(8,128)(2,1)}), bf16[4,4,128,256]{3,2,1,0:T(8,128)(2,1)}, u32[]{:S(2)}, u32[]{:S(2)}) async-start(bf16[4,4,128,256]{3,2,1,0:T(8,128)(2,1)} %copy-done.1), calls=%async_computation.6 | async-start | bytes 2097152 | tf_op jit(solution)/shard_map/quad_gather/all_to_all | solution.py:211
  182.6 12.5 %collective-permute-start.12 = (bf16[32,64,256]{2,1,0:T(8,128)(2,1)}, bf16[32,64,256]{2,1,0:T(8,128)(2,1)}, u32[]{:S(2)}, u32[]{:S(2)}) collective-permute-start(bf16[32,64,256]{2,1,0:T(8,128)(2,1)} %get-tuple-element.26.refs_1_), channel_id=1, source_target_pairs={{0,1},{1,0},{2,3},{3,2},{4,5},{5,4},{6,7},{7,6},{8,9},{9,8},{10,11... | collective-permute-start | bytes 3145736 | tf_op jit(solution)/shard_map/quad_gather/ppermute | solution.py:222

commit v3 on v2

--- a/solution.py
+++ b/solution.py
@@ -12,6 +12,7 @@
 VMEM_LIMIT = 12 * 1024 * 1024
 
 QUAD = 4
+ID_BITS = 5
 
 
 def layout_of(dp_count, mp_count):
@@ -66,35 +67,79 @@
     return pl.ds(pl.multiple_of(lax.bitwise_xor(quad_ref[0], step) * extent, extent), extent)
 
 
-def count_body(ids_ref, counts_ref):
-    bag_size, columns = ids_ref.shape
-    rows_step, columns_step = 64, 256
+def count_of(ids, base, rows):
+    slots = lax.broadcasted_iota(jnp.int32, (rows, ids.shape[1]), 0) + base
+    total = jnp.zeros(slots.shape, F32)
+    for slot in range(ids.shape[0]):
+        total = total + jnp.where(slots == ids[slot : slot + 1, :], 1.0, 0.0)
+    return total
+
+
+def pack_body(quad_ref, shard_ref, ids_ref, grad_ref, *packed_refs):
+    group, width = grad_ref.shape
+    bag_size = ids_ref.shape[0]
+    embed = width // QUAD
+    span = QUAD * group
+    own = ids_ref[:, pl.ds(pl.multiple_of(shard_ref[0] * span, span), span)]
+    high = lax.shift_right_logical(own, ID_BITS).astype(F32).astype(BF16)
+    low = lax.bitwise_and(own, (1 << ID_BITS) - 1).astype(F32).astype(BF16)
+    for step, packed_ref in enumerate(packed_refs):
+        packed_ref[:group, :] = grad_ref[:, place_of(quad_ref, step, embed)]
+        packed_ref[group : group + bag_size, :] = high
+        packed_ref[group + bag_size :, :] = low
+
+
+def count_body(quad_ref, *refs):
+    packed_refs, counts_ref, grad_ref = refs[:-2], refs[-2], refs[-1]
+    columns = counts_ref.shape[1]
+    group = columns // QUAD
+    bag_size = (packed_refs[0].shape[0] - group) // 2
+    lanes = lax.broadcasted_iota(jnp.int32, (bag_size, columns), 1)
+    ids = jnp.zeros((bag_size, columns), jnp.int32)
+    for step, packed_ref in enumerate(packed_refs):
+        grad_ref[step * group : (step + 1) * group, :] = packed_ref[:group, :]
+        high = packed_ref[group : group + bag_size, :].astype(F32)
+        low = packed_ref[group + bag_size :, :].astype(F32)
+        every = (high * (1 << ID_BITS) + low).astype(jnp.int32)
+        turn = lax.bitwise_and(step - quad_ref[0], QUAD - 1) * group
+        here = (lanes >= step * group) & (lanes < (step + 1) * group)
+        ids = jnp.where(here, pltpu.roll(every, turn, 1), ids)
+    rows = 64
 
     def rows_at(index, carry):
-        base = pl.multiple_of(index * rows_step, rows_step)
-        rows = lax.broadcasted_iota(jnp.int32, (rows_step, columns_step), 0) + base
-        for start in range(0, columns, columns_step):
-            span = slice(start, start + columns_step)
-            total = jnp.zeros((rows_step, columns_step), F32)
-            for slot in range(bag_size):
-                total = total + jnp.where(rows == ids_ref[slot : slot + 1, span], 1.0, 0.0)
-            counts_ref[pl.ds(base, rows_step), span] = total.astype(BF16)
+        base = pl.multiple_of(index * rows, rows)
+        counts_ref[pl.ds(base, rows), :] = count_of(ids, base, rows).astype(BF16)
         return carry
 
-    lax.fori_loop(0, counts_ref.shape[0] // rows_step, rows_at, 0)
+    lax.fori_loop(0, counts_ref.shape[0] // rows, rows_at, 0)
+
+
+def block_body(order_ref, ids_ref, blocks_ref, done_ref):
+    shards_of, width, _ = blocks_ref.shape
+    rows = width // QUAD
+    row_of = lax.broadcasted_iota(jnp.int32, (width, width), 0) // rows
+    column_of = lax.broadcasted_iota(jnp.int32, (width, width), 1) // rows
+
+    def shard_at(index, carry):
+        start = pl.multiple_of(order_ref[index] * width, width)
+        counts = count_of(ids_ref[:, pl.ds(start, width)], order_ref[0] * rows, rows)
+        tall = jnp.concatenate([counts] * QUAD, axis=0)
+        blocks_ref[index] = jnp.where(row_of == column_of, tall, 0.0).astype(BF16)
+        return carry
+
+    lax.fori_loop(0, shards_of, shard_at, 0)
+    done_ref[...] = jnp.zeros(done_ref.shape, done_ref.dtype)
 
 
 def forward_body(
-    quad_ref, counts_ref, table_ref, grad0_ref, grad1_ref, grad2_ref, grad3_ref, down_ref, up_ref,
-    state_ref, part_ref,
+    quad_ref, counts_ref, grad_ref, table_ref, down_ref, up_ref, state_ref, part_ref,
 ):
     samples = counts_ref.shape[1]
     group = samples // QUAD
     pooled = contract(counts_ref[...], table_ref[...], 0, 0).astype(BF16)
     state_ref[0] = pooled
-    for step, one_ref in enumerate((grad0_ref, grad1_ref, grad2_ref, grad3_ref)):
-        state_ref[1, step * group : (step + 1) * group, :] = one_ref[...]
-    scaled = (state_ref[1].astype(F32) * pooled.astype(F32)).astype(BF16)
+    state_ref[1] = grad_ref[...]
+    scaled = (grad_ref[...].astype(F32) * pooled.astype(F32)).astype(BF16)
     rank_part = contract(pooled, down_ref[...], 1, 0).astype(BF16)
     back_part = contract(scaled, up_ref[...], 1, 1).astype(BF16)
     for step in range(QUAD):
@@ -149,36 +194,37 @@
         pooled_grad_ref[lax.bitwise_xor(quad_ref[0], step)] = one_ref[1]
 
 
-def table_body(order_ref, counts_ref, grads_ref, out_ref):
-    count, rows, embed = out_ref.shape
-    columns = counts_ref.shape[1]
-    group = columns // count
-    counts = counts_ref[...].astype(F32)
-    tall = jnp.concatenate([counts] * count, axis=0)
-    row_of = lax.broadcasted_iota(jnp.int32, tall.shape, 0) // rows
-    column_of = lax.broadcasted_iota(jnp.int32, tall.shape, 1) // group
-    blocks = jnp.where(row_of == column_of, tall, 0.0).astype(BF16)
-    sums = contract(blocks, grads_ref[...].reshape(columns, embed), 1, 0)
-    out_ref[...] = sums.astype(BF16).reshape(count, rows, embed)
-
-
-def sum_tables(order, counts, grads):
+def table_body(order_ref, blocks_ref, grads_ref, out_ref):
+    count, width, _ = blocks_ref.shape
+    _, rows, embed = out_ref.shape
+    first = pl.program_id(0) * count
+    for index in range(count):
+        grads = grads_ref[index * QUAD : (index + 1) * QUAD].reshape(width, embed)
+        sums = contract(blocks_ref[index], grads, 1, 0).astype(BF16)
+        start = order_ref[first + index] * QUAD
+        for feature in range(QUAD):
+            out_ref[start + feature] = sums[feature * rows : (feature + 1) * rows]
+
+
+def sum_tables(order, blocks, grads):
     features, group, embed = grads.shape
-    rows = counts.shape[0]
+    shards_of, width, _ = blocks.shape
+    count = shards_of // 4
+    out = (features, width // QUAD, embed)
     return pl.pallas_call(
         table_body,
-        out_shape=shape_of((features, rows, embed)),
+        out_shape=shape_of(out),
         grid_spec=pltpu.PrefetchScalarGridSpec(
             num_scalar_prefetch=1,
-            grid=(features // QUAD,),
+            grid=(4,),
             in_specs=[
-                pl.BlockSpec((rows, QUAD * group), lambda index, order: (0, order[index])),
-                pl.BlockSpec((QUAD, group, embed), lambda index, order: (index, 0, 0)),
+                pl.BlockSpec((count, width, width), lambda index, order: (index, 0, 0)),
+                pl.BlockSpec((count * QUAD, group, embed), lambda index, order: (index, 0, 0)),
             ],
-            out_specs=pl.BlockSpec((QUAD, rows, embed), lambda index, order: (order[index], 0, 0)),
+            out_specs=pl.BlockSpec(out, lambda index, order: (0, 0, 0)),
         ),
         compiler_params=pltpu.CompilerParams(vmem_limit_bytes=VMEM_LIMIT),
-    )(order, counts, grads)
+    )(order, blocks, grads)
 
 
 def weights_body(sums_ref, down_ref, up_ref):
@@ -227,39 +273,36 @@
             tables.reshape(ways, QUAD, rows, embed), quad, 1, keepdims=False
         )
         table = exchange(table_parts, "mp").reshape(ways * rows, embed)
-        shard_ids = jnp.transpose(
-            lax.dynamic_slice_in_dim(bag_ids, shard_index * QUAD, QUAD, 1), (1, 2, 0)
-        )
-        quad_ids = swap(
-            [lax.dynamic_index_in_dim(shard_ids, quad ^ step, 0, keepdims=False) for step in range(QUAD)]
-        )
-        quad_grads = swap(
-            [
-                lax.dynamic_slice_in_dim(cotangent, (quad ^ step) * embed, embed, 1)
-                for step in range(QUAD)
-            ]
+        ids = jnp.transpose(bag_ids, (2, 1, 0)).reshape(bag_size, feature_count * group)
+        packed_shape = shape_of((group + 2 * bag_size, embed))
+        packed = swap(
+            call(pack_body, (packed_shape,) * QUAD, quad_at, shard_index.reshape(1), ids, cotangent)
         )
         down = lax.dynamic_slice_in_dim(down_proj, quad * embed, embed, 0)
         up = lax.dynamic_slice_in_dim(up_proj, quad * embed, embed, 1)
 
     with jax.named_scope("counts"):
-        quad_counts = call(
-            count_body, shape_of((ways * rows, samples)), jnp.concatenate(quad_ids, axis=1)
-        )
-        row_ids = jnp.transpose(bag_ids, (2, 1, 0)).reshape(bag_size, feature_count * group)
-        row_counts = call(
-            count_body, shape_of((rows, feature_count * group)), row_ids - shard_index * rows
+        quad_counts, grad = call(
+            count_body, (shape_of((ways * rows, samples)), shape_of((samples, embed))), quad_at, *packed
+        )
+        steps = [ways >> (index + 1) for index in range(ways.bit_length() - 1)]
+        order = [shard_index]
+        for mask in steps:
+            order = order + [index ^ mask for index in order]
+        order = jnp.stack(order)
+        row_blocks, done = call(
+            block_body, (shape_of((ways, QUAD * rows, QUAD * group)), shape_of((8, 128), F32)), order, ids
         )
 
     with jax.named_scope("forward"):
         state, part = call(
             forward_body, (shape_of((2, samples, embed)), shape_of((2, samples, rank))),
-            quad_at, quad_counts, table, *quad_grads, down, up,
+            quad_at, quad_counts, grad, table, down, up,
         )
     with jax.named_scope("ranks"):
         piece = 2 * samples // members
         pieces = exchange(part.reshape(members, piece, rank), ("dp", "mp"), blocks)
-        copies = call(add_body, shape_of((members, piece, rank)), pieces, after=(row_counts,))
+        copies = call(add_body, shape_of((members, piece, rank)), pieces, after=(done,))
         ranks = exchange(copies, ("dp", "mp"), blocks).reshape(2, samples, rank)
 
     with jax.named_scope("cross"):
@@ -278,23 +321,18 @@
         near_copies = call(add_body, shape_of((windows,) + slab), near_parts, after=(grads,))
     with jax.named_scope("far_sums"):
         far_parts = exchange(near_copies, "dp", far)
-        steps = [ways >> (index + 1) for index in range(ways.bit_length() - 1)]
-        for mask in steps[:-2]:
+        for mask in steps[:-1]:
             grads = double(grads, mask)
         far_copies = call(add_body, shape_of((window,) + slab), far_parts, after=(grads,))
     with jax.named_scope("near_gather"):
         sums = exchange(far_copies, "dp", near)
-        grads = double(grads, steps[-2])
+        grads = double(grads, steps[-1])
         quad_copies = call(
             copy_body, shape_of((QUAD, window) + slab), sums, after=(grads,)
         )
     with jax.named_scope("quad_gather"):
         every = exchange(quad_copies, "dp", quads).reshape(QUAD, 2, embed, rank)
-        grads = double(grads, steps[-1])
-        order = [shard_index]
-        for mask in steps:
-            order = order + [index ^ mask for index in order]
-        table_grads = sum_tables(jnp.stack(order), row_counts, grads)[None]
+        table_grads = sum_tables(order, row_blocks, grads)[None]
         down_grad, up_grad = call(
             weights_body, (shape_of(down_proj.shape, F32), shape_of(up_proj.shape, F32)), every
         )

time: 213 us -> 188 us (0.88)
  the two profiles are of different devices: /device:TPU:1 before, /device:TPU:2 now
where the time goes in v3:
time: 188 us; the launch traced here: 186 us
  starting transfers between devices  93.3 us (50%)
  waiting for transfers between devices  46.1 us (25%)
  local copies, waits for them, and re-layouts  17.2 us (9%)
  Pallas kernels  14.7 us (8%)
  blocking collectives  14 us (7%)
    all_to_all x6, starting transfers between devices, exchange(): lax.all_to_all(value, axis, 0, 0, axis_index_groups=groups, tiled=True)  64.4 us
    ppermute x4, waiting for transfers between devices, double(): lax.ppermute(value, 'mp', [(index, index ^ mask) for index in range(ways)])  24.4 us
    ppermute x6, starting transfers between devices, swap(): got.append(lax.ppermute(values[step], 'dp', pairs))  18.4 us
    all_to_all x6, waiting for transfers between devices, exchange(): lax.all_to_all(value, axis, 0, 0, axis_index_groups=groups, tiled=True)  17.3 us
    all_to_all x1, blocking collectives, exchange(): lax.all_to_all(value, axis, 0, 0, axis_index_groups=groups, tiled=True)  14 us
    ppermute x4, starting transfers between devices, double(): lax.ppermute(value, 'mp', [(index, index ^ mask) for index in range(ways)])  10.5 us
    unnamed x19, local copies, waits for them, and re-layouts  10 us
    pallas_call x11, Pallas kernels, call(): pl.pallas_call(run, out_shape=out_shape, in_specs=[pl.BlockSpec(memory_sp...  9.79 us
  transfers between devices with their start and end apart: 16, of which 10 were waited for; matrix products, arithmetic and copies ran while one was open for 5% of the time, Pallas kernels for 5%

profile of v3, /device:TPU:2, one launch (start us, length us, event | category | flops | bytes accessed | tf_op | source)
XLA Modules:
  0.0 186.4 jit_solution(16435753192080169614)
XLA Ops:
  0.7 1.5 copy-done
  3.1 16.6 %all-to-all-start = ((bf16[16,64,256]{2,1,0:T(8,128)(2,1)}), bf16[16,64,256]{2,1,0:T(8,128)(2,1)S(1)}, u32[]{:S(2)}, u32[]{:S(2)}) async-start(bf16[16,64,256]{2,1,0:T(8,128)(2,1)} %dynamic-slice_bitcast_fusion), calls=%async_computation | async-start | bytes 1048576 | tf_op jit(solution)/shard_map/inputs/all_to_all | solution.py:257
  19.6 2.1 %copy.9 = s32[16,64,64]{2,1,0:T(8,128)} copy(s32[16,64,64]{1,0,2:T(8,128)} %bitcast.32) | data formatting | bytes 524288 | tf_op jit(solution)/shard_map/inputs/transpose | solution.py:276
  23.0 1.9 %collective-permute-start = (bf16[96,256]{1,0:T(8,128)(2,1)S(1)}, bf16[96,256]{1,0:T(8,128)(2,1)S(1)}, u32[]{:S(2)}, u32[]{:S(2)}) collective-permute-start(bf16[96,256]{1,0:T(8,128)(2,1)S(1)} %get-tuple-element.24), channel_id=1, source_target_pairs={{0,16},{16,0},{32,48},{48,32},{64,80},{80,64},{96,112},{112,96},{1... | collective-permute-start | bytes 147464 | tf_op jit(solution)/shard_map/inputs/ppermute | solution.py:264
  24.9 1.9 %collective-permute-start.1 = (bf16[96,256]{1,0:T(8,128)(2,1)S(1)}, bf16[96,256]{1,0:T(8,128)(2,1)S(1)}, u32[]{:S(2)}, u32[]{:S(2)}) collective-permute-start(bf16[96,256]{1,0:T(8,128)(2,1)S(1)} %get-tuple-element.25), channel_id=1, source_target_pairs={{0,512},{16,528},{32,544},{48,560},{64,576},{80,592},{96,608},{112... | collective-permute-start | bytes 147464 | tf_op jit(solution)/shard_map/inputs/ppermute | solution.py:264
  26.8 5.4 %collective-permute-start.2 = (bf16[96,256]{1,0:T(8,128)(2,1)S(1)}, bf16[96,256]{1,0:T(8,128)(2,1)S(1)}, u32[]{:S(2)}, u32[]{:S(2)}) collective-permute-start(bf16[96,256]{1,0:T(8,128)(2,1)S(1)} %get-tuple-element.26), channel_id=1, source_target_pairs={{0,528},{16,512},{32,560},{48,544},{64,592},{80,576},{96,624},{112... | collective-permute-start | bytes 147464 | tf_op jit(solution)/shard_map/inputs/ppermute | solution.py:264
  34.2 1.9 %counts.2 = (bf16[1024,256]{1,0:T(8,128)(2,1)S(1)}, bf16[256,256]{1,0:T(8,128)(2,1)S(1)}) custom-call(s32[1]{0:T(128)} %bitcast.refs_0_, bf16[96,256]{1,0:T(8,128)(2,1)S(1)} %get-tuple-element.23.refs_1_, bf16[96,256]{1,0:T(8,128)(2,1)S(1)} %collective-permute-done.refs_2_, bf16[96,256]{1,0:T(8,128)(2,1)S(1)} %collective-permute-done.1.refs_3_, ...), custom_call_target="tpu_custom_call" | custom-call | tf_op jit(solution)/shard_map/counts/pallas_call | solution.py:48
  39.2 9.3 %all-to-all-start.1 = ((bf16[64,8,256]{2,1,0:T(8,128)(2,1)}), bf16[64,8,256]{2,1,0:T(8,128)(2,1)S(1)}, u32[]{:S(2)}, u32[]{:S(2)}) async-start(bf16[64,8,256]{2,1,0:T(8,128)(2,1)} %bitcast.6), calls=%async_computation.1 | async-start | bytes 524288 | tf_op jit(solution)/shard_map/ranks/all_to_all | solution.py:257
  48.7 2.6 %counts.3 = (bf16[16,256,256]{2,1,0:T(8,128)(2,1)S(1)}, f32[8,128]{1,0:T(8,128)S(1)}) custom-call(s32[16]{0:T(128)S(1)} %stack.64.refs_0_.order_ref, s32[16,4096]{1,0:T(8,128)S(1)} %reshape.37.refs_2_.refs_1_), custom_call_target="tpu_custom_call" | custom-call | tf_op jit(solution)/shard_map/counts/pallas_call | solution.py:48
  52.6 4.8 %all-to-all-done.1.refs_0_ = bf16[64,8,256]{2,1,0:T(8,128)(2,1)S(1)} async-done(((bf16[64,8,256]{2,1,0:T(8,128)(2,1)}), bf16[64,8,256]{2,1,0:T(8,128)(2,1)S(1)}, u32[]{:S(2)}, u32[]{:S(2)}) %all-to-all-start.1) | async-done | bytes 262176 | tf_op jit(solution)/shard_map/ranks/all_to_all | solution.py:257
  57.4 14.0 %all_to_all.35 = bf16[64,8,256]{2,1,0:T(8,128)(2,1)S(1)} all-to-all(bf16[64,8,256]{2,1,0:T(8,128)(2,1)S(1)} %ranks.1), channel_id=1, replica_groups={{0,16,512,528,1,17,513,529,2,18,514,530,3,19,515,531,4,20,516,532,5,21,..., dimensions={0} | all-to-all | bytes 524288 | tf_op jit(solution)/shard_map/ranks/all_to_all | solution.py:257
  72.4 3.4 %all-to-all-start.3 = ((bf16[4,128,256]{2,1,0:T(8,128)(2,1)}), bf16[4,128,256]{2,1,0:T(8,128)(2,1)S(1)}, u32[]{:S(2)}, u32[]{:S(2)}) async-start(bf16[4,128,256]{2,1,0:T(8,128)(2,1)} %bitcast.24), calls=%async_computation.3 | async-start | bytes 524288 | tf_op jit(solution)/shard_map/near_sums/all_to_all | solution.py:257
  75.8 2.7 %collective-permute-start.3 = (bf16[2,64,256]{2,1,0:T(8,128)(2,1)S(1)}, bf16[2,64,256]{2,1,0:T(8,128)(2,1)S(1)}, u32[]{:S(2)}, u32[]{:S(2)}) collective-permute-start(bf16[2,64,256]{2,1,0:T(8,128)(2,1)S(1)} %get-tuple-element.33), channel_id=1, source_target_pairs={{0,16},{16,0},{32,48},{48,32},{64,80},{80,64},{96,112},{112,96},{1... | collective-permute-start | bytes 196616 | tf_op jit(solution)/shard_map/near_sums/ppermute | solution.py:264
  78.5 2.5 %collective-permute-start.4 = (bf16[2,64,256]{2,1,0:T(8,128)(2,1)S(1)}, bf16[2,64,256]{2,1,0:T(8,128)(2,1)S(1)}, u32[]{:S(2)}, u32[]{:S(2)}) collective-permute-start(bf16[2,64,256]{2,1,0:T(8,128)(2,1)S(1)} %get-tuple-element.34), channel_id=1, source_target_pairs={{0,512},{16,528},{32,544},{48,560},{64,576},{80,592},{96,608},{112... | collective-permute-start | bytes 196616 | tf_op jit(solution)/shard_map/near_sums/ppermute | solution.py:264
  81.1 4.0 %collective-permute-start.5 = (bf16[2,64,256]{2,1,0:T(8,128)(2,1)S(1)}, bf16[2,64,256]{2,1,0:T(8,128)(2,1)S(1)}, u32[]{:S(2)}, u32[]{:S(2)}) collective-permute-start(bf16[2,64,256]{2,1,0:T(8,128)(2,1)S(1)} %get-tuple-element.35), channel_id=1, source_target_pairs={{0,528},{16,512},{32,560},{48,544},{64,592},{80,576},{96,624},{112... | collective-permute-start | bytes 196616 | tf_op jit(solution)/shard_map/near_sums/ppermute | solution.py:264
  85.1 3.4 %collective-permute-done.5.refs_4_ = bf16[2,64,256]{2,1,0:T(8,128)(2,1)S(1)} collective-permute-done((bf16[2,64,256]{2,1,0:T(8,128)(2,1)S(1)}, bf16[2,64,256]{2,1,0:T(8,128)(2,1)S(1)}, u32[]{:S(2)}, u32[]{:S(2)}) %collective-permute-start.5) | collective-permute-done | bytes 65568 | tf_op jit(solution)/shard_map/near_sums/ppermute | solution.py:264
  89.1 4.9 %all-to-all-done.3.refs_0_ = bf16[4,128,256]{2,1,0:T(8,128)(2,1)S(1)} async-done(((bf16[4,128,256]{2,1,0:T(8,128)(2,1)}), bf16[4,128,256]{2,1,0:T(8,128)(2,1)S(1)}, u32[]{:S(2)}, u32[]{:S(2)}) %all-to-all-start.3) | async-done | bytes 262176 | tf_op jit(solution)/shard_map/near_sums/all_to_all | solution.py:257
  94.7 20.9 %all-to-all-start.4 = ((bf16[4,128,256]{2,1,0:T(8,128)(2,1)}), bf16[4,128,256]{2,1,0:T(8,128)(2,1)S(1)}, u32[]{:S(2)}, u32[]{:S(2)}) async-start(bf16[4,128,256]{2,1,0:T(8,128)(2,1)} %near_sums.3), calls=%async_computation.4 | async-start | bytes 524288 | tf_op jit(solution)/shard_map/far_sums/all_to_all | solution.py:257
  115.7 2.5 %collective-permute-start.6 = (bf16[4,64,256]{2,1,0:T(8,128)(2,1)S(1)}, bf16[4,64,256]{2,1,0:T(8,128)(2,1)S(1)}, u32[]{:S(2)}, u32[]{:S(2)}) collective-permute-start(bf16[4,64,256]{2,1,0:T(8,128)(2,1)S(1)} %get-tuple-element.38.refs_1_), channel_id=1, source_target_pairs={{0,8},{1,9},{2,10},{3,11},{4,12},{5,13},{6,14},{7,15},{8,0},{9,1},... | collective-permute-start | bytes 393224 | tf_op jit(solution)/shard_map/far_sums/ppermute | solution.py:268
  118.1 6.0 %collective-permute-done.6 = bf16[4,64,256]{2,1,0:T(8,128)(2,1)S(1)} collective-permute-done((bf16[4,64,256]{2,1,0:T(8,128)(2,1)S(1)}, bf16[4,64,256]{2,1,0:T(8,128)(2,1)S(1)}, u32[]{:S(2)}, u32[]{:S(2)}) %collective-permute-start.6) | collective-permute-done | bytes 131104 | tf_op jit(solution)/shard_map/far_sums/ppermute | solution.py:268
  124.1 2.8 %collective-permute-start.7 = (bf16[8,64,256]{2,1,0:T(8,128)(2,1)S(1)}, bf16[8,64,256]{2,1,0:T(8,128)(2,1)S(1)}, u32[]{:S(2)}, u32[]{:S(2)}) collective-permute-start(bf16[8,64,256]{2,1,0:T(8,128)(2,1)S(1)} %pad_maximum_fusion.1), channel_id=1, source_target_pairs={{0,4},{1,5},{2,6},{3,7},{4,0},{5,1},{6,2},{7,3},{8,12},{9,13},{10,... | collective-permute-start | bytes 786440 | tf_op jit(solution)/shard_map/far_sums/ppermute | solution.py:268
  127.0 7.6 %collective-permute-done.7 = bf16[8,64,256]{2,1,0:T(8,128)(2,1)S(1)} collective-permute-done((bf16[8,64,256]{2,1,0:T(8,128)(2,1)S(1)}, bf16[8,64,256]{2,1,0:T(8,128)(2,1)S(1)}, u32[]{:S(2)}, u32[]{:S(2)}) %collective-permute-start.7) | collective-permute-done | bytes 262176 | tf_op jit(solution)/shard_map/far_sums/ppermute | solution.py:268
  134.6 3.3 %collective-permute-start.8 = (bf16[16,64,256]{2,1,0:T(8,128)(2,1)S(1)}, bf16[16,64,256]{2,1,0:T(8,128)(2,1)S(1)}, u32[]{:S(2)}, u32[]{:S(2)}) collective-permute-start(bf16[16,64,256]{2,1,0:T(8,128)(2,1)S(1)} %pad_maximum_fusion), channel_id=1, source_target_pairs={{0,2},{1,3},{2,0},{3,1},{4,6},{5,7},{6,4},{7,5},{8,10},{9,11},{10,... | collective-permute-start | bytes 1572872 | tf_op jit(solution)/shard_map/far_sums/ppermute | solution.py:268
  140.0 8.2 %collective-permute-done.8 = bf16[16,64,256]{2,1,0:T(8,128)(2,1)S(1)} collective-permute-done((bf16[16,64,256]{2,1,0:T(8,128)(2,1)S(1)}, bf16[16,64,256]{2,1,0:T(8,128)(2,1)S(1)}, u32[]{:S(2)}, u32[]{:S(2)}) %collective-permute-start.8) | collective-permute-done | bytes 524320 | tf_op jit(solution)/shard_map/far_sums/ppermute | solution.py:268
  149.9 10.7 %all-to-all-start.5 = ((bf16[4,128,256]{2,1,0:T(8,128)(2,1)}), bf16[4,128,256]{2,1,0:T(8,128)(2,1)S(1)}, u32[]{:S(2)}, u32[]{:S(2)}) async-start(bf16[4,128,256]{2,1,0:T(8,128)(2,1)} %copy-done.4), calls=%async_computation.5 | async-start | bytes 524288 | tf_op jit(solution)/shard_map/near_gather/all_to_all | solution.py:257
  160.6 1.9 %collective-permute-start.9 = (bf16[32,64,256]{2,1,0:T(8,128)(2,1)S(1)}, bf16[32,64,256]{2,1,0:T(8,128)(2,1)S(1)}, u32[]{:S(2)}, u32[]{:S(2)}) collective-permute-start(bf16[32,64,256]{2,1,0:T(8,128)(2,1)S(1)} %get-tuple-element.42.refs_1_), channel_id=1, source_target_pairs={{0,1},{1,0},{2,3},{3,2},{4,5},{5,4},{6,7},{7,6},{8,9},{9,8},{10,11... | collective-permute-start | bytes 3145736 | tf_op jit(solution)/shard_map/near_gather/ppermute | solution.py:268
  162.5 2.6 %collective-permute-done.9 = bf16[32,64,256]{2,1,0:T(8,128)(2,1)S(1)} collective-permute-done((bf16[32,64,256]{2,1,0:T(8,128)(2,1)S(1)}, bf16[32,64,256]{2,1,0:T(8,128)(2,1)S(1)}, u32[]{:S(2)}, u32[]{:S(2)}) %collective-permute-start.9) | collective-permute-done | bytes 1048608 | tf_op jit(solution)/shard_map/near_gather/ppermute | solution.py:268
  166.2 4.6 %all-to-all-done.5.refs_0_ = bf16[4,128,256]{2,1,0:T(8,128)(2,1)S(1)} async-done(((bf16[4,128,256]{2,1,0:T(8,128)(2,1)}), bf16[4,128,256]{2,1,0:T(8,128)(2,1)S(1)}, u32[]{:S(2)}, u32[]{:S(2)}) %all-to-all-start.5) | async-done | bytes 262176 | tf_op jit(solution)/shard_map/near_gather/all_to_all | solution.py:257
  171.8 3.5 %all-to-all-start.6 = ((bf16[4,4,128,256]{3,2,1,0:T(8,128)(2,1)}), bf16[4,4,128,256]{3,2,1,0:T(8,128)(2,1)S(1)}, u32[]{:S(2)}, u32[]{:S(2)}) async-start(bf16[4,4,128,256]{3,2,1,0:T(8,128)(2,1)} %copy-done.1), calls=%async_computation.6 | async-start | bytes 2097152 | tf_op jit(solution)/shard_map/quad_gather/all_to_all | solution.py:257
  175.3 1.6 copy-done.3
  176.9 4.9 %quad_gather.2 = bf16[64,64,256]{2,1,0:T(8,128)(2,1)} custom-call(s32[16]{0:T(128)S(1)} %stack.64.refs_0_.order_ref, bf16[16,256,256]{2,1,0:T(8,128)(2,1)S(1)} %copy-done.3, bf16[64,64,256]{2,1,0:T(8,128)(2,1)} %constant_dynamic-update-slice_fusion.4.grads_ref.refs_1_), custom_call_target="tpu_custom_call" | custom-call | tf_op jit(solution)/shard_map/quad_gather/pallas_call | solution.py:214
  181.9 3.1 %all-to-all-done.6 = bf16[4,4,128,256]{3,2,1,0:T(8,128)(2,1)S(1)} async-done(((bf16[4,4,128,256]{3,2,1,0:T(8,128)(2,1)}), bf16[4,4,128,256]{3,2,1,0:T(8,128)(2,1)S(1)}, u32[]{:S(2)}, u32[]{:S(2)}) %all-to-all-start.6) | async-done | bytes 1048608 | tf_op jit(solution)/shard_map/quad_gather/all_to_all | solution.py:257
  (41 shorter events, 18.5 us)
Async XLA Ops:
  0.6 1.6 copy-start
  0.6 22.3 %copy-start.7 = (bf16[64,1024]{1,0:T(8,128)(2,1)S(1)}, bf16[64,1024]{1,0:T(8,128)(2,1)}, u32[]{:S(2)}) copy-start(bf16[64,1024]{1,0:T(8,128)(2,1)} %refs_3_.1) | copy-start | bytes 393220
  3.1 33.9 %all-to-all-start = ((bf16[16,64,256]{2,1,0:T(8,128)(2,1)}), bf16[16,64,256]{2,1,0:T(8,128)(2,1)S(1)}, u32[]{:S(2)}, u32[]{:S(2)}) async-start(bf16[16,64,256]{2,1,0:T(8,128)(2,1)} %dynamic-slice_bitcast_fusion), calls=%async_computation | async-start | bytes 1048576 | tf_op jit(solution)/shard_map/inputs/all_to_all | solution.py:257
  23.0 10.2 %collective-permute-start = (bf16[96,256]{1,0:T(8,128)(2,1)S(1)}, bf16[96,256]{1,0:T(8,128)(2,1)S(1)}, u32[]{:S(2)}, u32[]{:S(2)}) collective-permute-start(bf16[96,256]{1,0:T(8,128)(2,1)S(1)} %get-tuple-element.24), channel_id=1, source_target_pairs={{0,16},{16,0},{32,48},{48,32},{64,80},{80,64},{96,112},{112,96},{1... | collective-permute-start | bytes 147464 | tf_op jit(solution)/shard_map/inputs/ppermute | solution.py:264
  24.9 8.3 %collective-permute-start.1 = (bf16[96,256]{1,0:T(8,128)(2,1)S(1)}, bf16[96,256]{1,0:T(8,128)(2,1)S(1)}, u32[]{:S(2)}, u32[]{:S(2)}) collective-permute-start(bf16[96,256]{1,0:T(8,128)(2,1)S(1)} %get-tuple-element.25), channel_id=1, source_target_pairs={{0,512},{16,528},{32,544},{48,560},{64,576},{80,592},{96,608},{112... | collective-permute-start | bytes 147464 | tf_op jit(solution)/shard_map/inputs/ppermute | solution.py:264
  26.8 7.4 %collective-permute-start.2 = (bf16[96,256]{1,0:T(8,128)(2,1)S(1)}, bf16[96,256]{1,0:T(8,128)(2,1)S(1)}, u32[]{:S(2)}, u32[]{:S(2)}) collective-permute-start(bf16[96,256]{1,0:T(8,128)(2,1)S(1)} %get-tuple-element.26), channel_id=1, source_target_pairs={{0,528},{16,512},{32,560},{48,544},{64,592},{80,576},{96,624},{112... | collective-permute-start | bytes 147464 | tf_op jit(solution)/shard_map/inputs/ppermute | solution.py:264
  36.1 0.8 copy-start.5
  36.9 1.0 copy-start.6
  39.2 18.1 %all-to-all-start.1 = ((bf16[64,8,256]{2,1,0:T(8,128)(2,1)}), bf16[64,8,256]{2,1,0:T(8,128)(2,1)S(1)}, u32[]{:S(2)}, u32[]{:S(2)}) async-start(bf16[64,8,256]{2,1,0:T(8,128)(2,1)} %bitcast.6), calls=%async_computation.1 | async-start | bytes 524288 | tf_op jit(solution)/shard_map/ranks/all_to_all | solution.py:257
  51.3 1.3 copy-start.2
  72.4 21.6 %all-to-all-start.3 = ((bf16[4,128,256]{2,1,0:T(8,128)(2,1)}), bf16[4,128,256]{2,1,0:T(8,128)(2,1)S(1)}, u32[]{:S(2)}, u32[]{:S(2)}) async-start(bf16[4,128,256]{2,1,0:T(8,128)(2,1)} %bitcast.24), calls=%async_computation.3 | async-start | bytes 524288 | tf_op jit(solution)/shard_map/near_sums/all_to_all | solution.py:257
  75.8 9.2 %collective-permute-start.3 = (bf16[2,64,256]{2,1,0:T(8,128)(2,1)S(1)}, bf16[2,64,256]{2,1,0:T(8,128)(2,1)S(1)}, u32[]{:S(2)}, u32[]{:S(2)}) collective-permute-start(bf16[2,64,256]{2,1,0:T(8,128)(2,1)S(1)} %get-tuple-element.33), channel_id=1, source_target_pairs={{0,16},{16,0},{32,48},{48,32},{64,80},{80,64},{96,112},{112,96},{1... | collective-permute-start | bytes 196616 | tf_op jit(solution)/shard_map/near_sums/ppermute | solution.py:264
  78.5 6.5 %collective-permute-start.4 = (bf16[2,64,256]{2,1,0:T(8,128)(2,1)S(1)}, bf16[2,64,256]{2,1,0:T(8,128)(2,1)S(1)}, u32[]{:S(2)}, u32[]{:S(2)}) collective-permute-start(bf16[2,64,256]{2,1,0:T(8,128)(2,1)S(1)} %get-tuple-element.34), channel_id=1, source_target_pairs={{0,512},{16,528},{32,544},{48,560},{64,576},{80,592},{96,608},{112... | collective-permute-start | bytes 196616 | tf_op jit(solution)/shard_map/near_sums/ppermute | solution.py:264
  81.1 7.4 %collective-permute-start.5 = (bf16[2,64,256]{2,1,0:T(8,128)(2,1)S(1)}, bf16[2,64,256]{2,1,0:T(8,128)(2,1)S(1)}, u32[]{:S(2)}, u32[]{:S(2)}) collective-permute-start(bf16[2,64,256]{2,1,0:T(8,128)(2,1)S(1)} %get-tuple-element.35), channel_id=1, source_target_pairs={{0,528},{16,512},{32,560},{48,544},{64,592},{80,576},{96,624},{112... | collective-permute-start | bytes 196616 | tf_op jit(solution)/shard_map/near_sums/ppermute | solution.py:264
  94.7 54.4 %all-to-all-start.4 = ((bf16[4,128,256]{2,1,0:T(8,128)(2,1)}), bf16[4,128,256]{2,1,0:T(8,128)(2,1)S(1)}, u32[]{:S(2)}, u32[]{:S(2)}) async-start(bf16[4,128,256]{2,1,0:T(8,128)(2,1)} %near_sums.3), calls=%async_computation.4 | async-start | bytes 524288 | tf_op jit(solution)/shard_map/far_sums/all_to_all | solution.py:257
  115.7 8.5 %collective-permute-start.6 = (bf16[4,64,256]{2,1,0:T(8,128)(2,1)S(1)}, bf16[4,64,256]{2,1,0:T(8,128)(2,1)S(1)}, u32[]{:S(2)}, u32[]{:S(2)}) collective-permute-start(bf16[4,64,256]{2,1,0:T(8,128)(2,1)S(1)} %get-tuple-element.38.refs_1_), channel_id=1, source_target_pairs={{0,8},{1,9},{2,10},{3,11},{4,12},{5,13},{6,14},{7,15},{8,0},{9,1},... | collective-permute-start | bytes 393224 | tf_op jit(solution)/shard_map/far_sums/ppermute | solution.py:268
  124.1 10.4 %collective-permute-start.7 = (bf16[8,64,256]{2,1,0:T(8,128)(2,1)S(1)}, bf16[8,64,256]{2,1,0:T(8,128)(2,1)S(1)}, u32[]{:S(2)}, u32[]{:S(2)}) collective-permute-start(bf16[8,64,256]{2,1,0:T(8,128)(2,1)S(1)} %pad_maximum_fusion.1), channel_id=1, source_target_pairs={{0,4},{1,5},{2,6},{3,7},{4,0},{5,1},{6,2},{7,3},{8,12},{9,13},{10,... | collective-permute-start | bytes 786440 | tf_op jit(solution)/shard_map/far_sums/ppermute | solution.py:268
  134.6 13.6 %collective-permute-start.8 = (bf16[16,64,256]{2,1,0:T(8,128)(2,1)S(1)}, bf16[16,64,256]{2,1,0:T(8,128)(2,1)S(1)}, u32[]{:S(2)}, u32[]{:S(2)}) collective-permute-start(bf16[16,64,256]{2,1,0:T(8,128)(2,1)S(1)} %pad_maximum_fusion), channel_id=1, source_target_pairs={{0,2},{1,3},{2,0},{3,1},{4,6},{5,7},{6,4},{7,5},{8,10},{9,11},{10,... | collective-permute-start | bytes 1572872 | tf_op jit(solution)/shard_map/far_sums/ppermute | solution.py:268
  149.2 0.7 copy-start.4
  149.9 20.9 %all-to-all-start.5 = ((bf16[4,128,256]{2,1,0:T(8,128)(2,1)}), bf16[4,128,256]{2,1,0:T(8,128)(2,1)S(1)}, u32[]{:S(2)}, u32[]{:S(2)}) async-start(bf16[4,128,256]{2,1,0:T(8,128)(2,1)} %copy-done.4), calls=%async_computation.5 | async-start | bytes 524288 | tf_op jit(solution)/shard_map/near_gather/all_to_all | solution.py:257
  160.6 4.5 %collective-permute-start.9 = (bf16[32,64,256]{2,1,0:T(8,128)(2,1)S(1)}, bf16[32,64,256]{2,1,0:T(8,128)(2,1)S(1)}, u32[]{:S(2)}, u32[]{:S(2)}) collective-permute-start(bf16[32,64,256]{2,1,0:T(8,128)(2,1)S(1)} %get-tuple-element.42.refs_1_), channel_id=1, source_target_pairs={{0,1},{1,0},{2,3},{3,2},{4,5},{5,4},{6,7},{7,6},{8,9},{9,8},{10,11... | collective-permute-start | bytes 3145736 | tf_op jit(solution)/shard_map/near_gather/ppermute | solution.py:268
  170.8 1.0 copy-start.1
  171.8 13.2 %all-to-all-start.6 = ((bf16[4,4,128,256]{3,2,1,0:T(8,128)(2,1)}), bf16[4,4,128,256]{3,2,1,0:T(8,128)(2,1)S(1)}, u32[]{:S(2)}, u32[]{:S(2)}) async-start(bf16[4,4,128,256]{3,2,1,0:T(8,128)(2,1)} %copy-done.1), calls=%async_computation.6 | async-start | bytes 2097152 | tf_op jit(solution)/shard_map/quad_gather/all_to_all | solution.py:257
  175.3 1.6 copy-start.3

commit v4 on v3

--- a/solution.py
+++ b/solution.py
@@ -57,6 +57,32 @@
     )(*operands, *after)
 
 
+def call_sliced(body, out_shape, quad_at, operands, sliced, scratch=(), limit=VMEM_LIMIT):
+    def whole(array):
+        return pl.BlockSpec(array.shape, lambda index, quad: (0,) * len(array.shape))
+
+    def part(array, dim):
+        shape = list(array.shape)
+        shape[dim] //= QUAD
+        return pl.BlockSpec(
+            tuple(shape),
+            lambda index, quad: tuple(quad[0] if axis == dim else 0 for axis in range(len(shape))),
+        )
+
+    return pl.pallas_call(
+        body,
+        out_shape=out_shape,
+        grid_spec=pltpu.PrefetchScalarGridSpec(
+            num_scalar_prefetch=1,
+            grid=(1,),
+            in_specs=[whole(operand) for operand in operands] + [part(*pair) for pair in sliced],
+            out_specs=jax.tree.map(whole, out_shape),
+            scratch_shapes=scratch,
+        ),
+        compiler_params=pltpu.CompilerParams(vmem_limit_bytes=limit),
+    )(quad_at, *operands, *(array for array, _ in sliced))
+
+
 def contract(left, right, left_dim, right_dim):
     return lax.dot_general(
         left, right, (((left_dim,), (right_dim,)), ((), ())), preferred_element_type=F32
@@ -73,6 +99,10 @@
     for slot in range(ids.shape[0]):
         total = total + jnp.where(slots == ids[slot : slot + 1, :], 1.0, 0.0)
     return total
+
+
+def slice_body(quad_ref, source_ref, slice_ref):
+    slice_ref[...] = source_ref[:, 0]
 
 
 def pack_body(quad_ref, shard_ref, ids_ref, grad_ref, *packed_refs):
@@ -89,40 +119,30 @@
         packed_ref[group + bag_size :, :] = low
 
 
-def count_body(quad_ref, *refs):
-    packed_refs, counts_ref, grad_ref = refs[:-2], refs[-2], refs[-1]
-    columns = counts_ref.shape[1]
+def ids_of(quad_ref, packed_refs, columns):
     group = columns // QUAD
     bag_size = (packed_refs[0].shape[0] - group) // 2
     lanes = lax.broadcasted_iota(jnp.int32, (bag_size, columns), 1)
     ids = jnp.zeros((bag_size, columns), jnp.int32)
     for step, packed_ref in enumerate(packed_refs):
-        grad_ref[step * group : (step + 1) * group, :] = packed_ref[:group, :]
         high = packed_ref[group : group + bag_size, :].astype(F32)
         low = packed_ref[group + bag_size :, :].astype(F32)
         every = (high * (1 << ID_BITS) + low).astype(jnp.int32)
         turn = lax.bitwise_and(step - quad_ref[0], QUAD - 1) * group
         here = (lanes >= step * group) & (lanes < (step + 1) * group)
         ids = jnp.where(here, pltpu.roll(every, turn, 1), ids)
-    rows = 64
-
-    def rows_at(index, carry):
-        base = pl.multiple_of(index * rows, rows)
-        counts_ref[pl.ds(base, rows), :] = count_of(ids, base, rows).astype(BF16)
-        return carry
-
-    lax.fori_loop(0, counts_ref.shape[0] // rows, rows_at, 0)
-
-
-def block_body(order_ref, ids_ref, blocks_ref, done_ref):
+    return ids
+
+
+def block_body(shard_ref, ids_ref, blocks_ref, done_ref):
     shards_of, width, _ = blocks_ref.shape
     rows = width // QUAD
     row_of = lax.broadcasted_iota(jnp.int32, (width, width), 0) // rows
     column_of = lax.broadcasted_iota(jnp.int32, (width, width), 1) // rows
 
     def shard_at(index, carry):
-        start = pl.multiple_of(order_ref[index] * width, width)
-        counts = count_of(ids_ref[:, pl.ds(start, width)], order_ref[0] * rows, rows)
+        start = pl.multiple_of(index * width, width)
+        counts = count_of(ids_ref[:, pl.ds(start, width)], shard_ref[0] * rows, rows)
         tall = jnp.concatenate([counts] * QUAD, axis=0)
         blocks_ref[index] = jnp.where(row_of == column_of, tall, 0.0).astype(BF16)
         return carry
@@ -132,20 +152,32 @@
 
 
 def forward_body(
-    quad_ref, counts_ref, grad_ref, table_ref, down_ref, up_ref, state_ref, part_ref,
+    quad_ref, table_ref, packed0_ref, packed1_ref, packed2_ref, packed3_ref, down_ref, up_ref,
+    state_ref, part_ref, ids_ref, counts_ref,
 ):
-    samples = counts_ref.shape[1]
+    packed_refs = (packed0_ref, packed1_ref, packed2_ref, packed3_ref)
+    samples = state_ref.shape[1]
     group = samples // QUAD
+    rows = 64
+    ids_ref[...] = ids_of(quad_ref, packed_refs, samples)
+
+    def rows_at(index, carry):
+        base = pl.multiple_of(index * rows, rows)
+        counts_ref[pl.ds(base, rows), :] = count_of(ids_ref[...], base, rows).astype(BF16)
+        return carry
+
+    lax.fori_loop(0, counts_ref.shape[0] // rows, rows_at, 0)
     pooled = contract(counts_ref[...], table_ref[...], 0, 0).astype(BF16)
     state_ref[0] = pooled
-    state_ref[1] = grad_ref[...]
-    scaled = (grad_ref[...].astype(F32) * pooled.astype(F32)).astype(BF16)
+    for step, packed_ref in enumerate(packed_refs):
+        state_ref[1, step * group : (step + 1) * group, :] = packed_ref[:group, :]
+    scaled = (state_ref[1].astype(F32) * pooled.astype(F32)).astype(BF16)
     rank_part = contract(pooled, down_ref[...], 1, 0).astype(BF16)
     back_part = contract(scaled, up_ref[...], 1, 1).astype(BF16)
     for step in range(QUAD):
-        rows = place_of(quad_ref, step, group)
-        part_ref[0, rows, :] = rank_part[step * group : (step + 1) * group]
-        part_ref[1, rows, :] = back_part[step * group : (step + 1) * group]
+        rows_of = place_of(quad_ref, step, group)
+        part_ref[0, rows_of, :] = rank_part[step * group : (step + 1) * group]
+        part_ref[1, rows_of, :] = back_part[step * group : (step + 1) * group]
 
 
 def cross_body(
@@ -194,37 +226,33 @@
         pooled_grad_ref[lax.bitwise_xor(quad_ref[0], step)] = one_ref[1]
 
 
-def table_body(order_ref, blocks_ref, grads_ref, out_ref):
+def table_body(blocks_ref, grads_ref, out_ref):
     count, width, _ = blocks_ref.shape
     _, rows, embed = out_ref.shape
-    first = pl.program_id(0) * count
     for index in range(count):
-        grads = grads_ref[index * QUAD : (index + 1) * QUAD].reshape(width, embed)
+        features = slice(index * QUAD, (index + 1) * QUAD)
+        grads = grads_ref[features].reshape(width, embed)
         sums = contract(blocks_ref[index], grads, 1, 0).astype(BF16)
-        start = order_ref[first + index] * QUAD
-        for feature in range(QUAD):
-            out_ref[start + feature] = sums[feature * rows : (feature + 1) * rows]
-
-
-def sum_tables(order, blocks, grads):
+        out_ref[features] = sums.reshape(QUAD, rows, embed)
+
+
+def sum_tables(blocks, grads):
     features, group, embed = grads.shape
     shards_of, width, _ = blocks.shape
+    rows = width // QUAD
     count = shards_of // 4
-    out = (features, width // QUAD, embed)
+
+    def block(*shape):
+        return pl.BlockSpec(shape, lambda index: (index, 0, 0))
+
     return pl.pallas_call(
         table_body,
-        out_shape=shape_of(out),
-        grid_spec=pltpu.PrefetchScalarGridSpec(
-            num_scalar_prefetch=1,
-            grid=(4,),
-            in_specs=[
-                pl.BlockSpec((count, width, width), lambda index, order: (index, 0, 0)),
-                pl.BlockSpec((count * QUAD, group, embed), lambda index, order: (index, 0, 0)),
-            ],
-            out_specs=pl.BlockSpec(out, lambda index, order: (0, 0, 0)),
-        ),
+        out_shape=shape_of((features, rows, embed)),
+        grid=(4,),
+        in_specs=[block(count, width, width), block(count * QUAD, group, embed)],
+        out_specs=block(count * QUAD, rows, embed),
         compiler_params=pltpu.CompilerParams(vmem_limit_bytes=VMEM_LIMIT),
-    )(order, blocks, grads)
+    )(blocks, grads)
 
 
 def weights_body(sums_ref, down_ref, up_ref):
@@ -264,13 +292,10 @@
             got.append(lax.ppermute(values[step], "dp", pairs))
         return got
 
-    def double(value, mask):
-        other = lax.ppermute(value, "mp", [(index, index ^ mask) for index in range(ways)])
-        return jnp.concatenate([value, other], axis=0)
-
     with jax.named_scope("inputs"):
-        table_parts = lax.dynamic_index_in_dim(
-            tables.reshape(ways, QUAD, rows, embed), quad, 1, keepdims=False
+        table_parts = call_sliced(
+            slice_body, shape_of((ways, rows, embed)), quad_at, (),
+            ((tables.reshape(ways, QUAD, rows, embed), 1),), limit=5 * VMEM_LIMIT,
         )
         table = exchange(table_parts, "mp").reshape(ways * rows, embed)
         ids = jnp.transpose(bag_ids, (2, 1, 0)).reshape(bag_size, feature_count * group)
@@ -278,26 +303,18 @@
         packed = swap(
             call(pack_body, (packed_shape,) * QUAD, quad_at, shard_index.reshape(1), ids, cotangent)
         )
-        down = lax.dynamic_slice_in_dim(down_proj, quad * embed, embed, 0)
-        up = lax.dynamic_slice_in_dim(up_proj, quad * embed, embed, 1)
+        weights = ((down_proj, 0), (up_proj, 1))
 
     with jax.named_scope("counts"):
-        quad_counts, grad = call(
-            count_body, (shape_of((ways * rows, samples)), shape_of((samples, embed))), quad_at, *packed
-        )
-        steps = [ways >> (index + 1) for index in range(ways.bit_length() - 1)]
-        order = [shard_index]
-        for mask in steps:
-            order = order + [index ^ mask for index in order]
-        order = jnp.stack(order)
         row_blocks, done = call(
-            block_body, (shape_of((ways, QUAD * rows, QUAD * group)), shape_of((8, 128), F32)), order, ids
+            block_body, (shape_of((ways, QUAD * rows, QUAD * group)), shape_of((8, 128), F32)), shard_index.reshape(1), ids
         )
 
     with jax.named_scope("forward"):
-        state, part = call(
+        state, part = call_sliced(
             forward_body, (shape_of((2, samples, embed)), shape_of((2, samples, rank))),
-            quad_at, quad_counts, grad, table, down, up,
+            quad_at, (table, *packed), weights,
+            (pltpu.VMEM((bag_size, samples), jnp.int32), pltpu.VMEM((ways * rows, samples), BF16)),
         )
     with jax.named_scope("ranks"):
         piece = 2 * samples // members
@@ -306,9 +323,9 @@
         ranks = exchange(copies, ("dp", "mp"), blocks).reshape(2, samples, rank)
 
     with jax.named_scope("cross"):
-        parts, *backs = call(
+        parts, *backs = call_sliced(
             cross_body, (shape_of((2, embed, rank)),) + (shape_of((2, group, embed)),) * QUAD,
-            quad_at, ranks, state, down, up,
+            quad_at, (ranks, state), weights,
         )
 
     slab = (2 * embed // window, rank)
@@ -319,20 +336,18 @@
             quad_at, *swap(backs),
         )
         near_copies = call(add_body, shape_of((windows,) + slab), near_parts, after=(grads,))
+        every_grad = lax.all_gather(grads, "mp", axis=0, tiled=True)
     with jax.named_scope("far_sums"):
         far_parts = exchange(near_copies, "dp", far)
-        for mask in steps[:-1]:
-            grads = double(grads, mask)
-        far_copies = call(add_body, shape_of((window,) + slab), far_parts, after=(grads,))
+        far_copies = call(add_body, shape_of((window,) + slab), far_parts)
     with jax.named_scope("near_gather"):
         sums = exchange(far_copies, "dp", near)
-        grads = double(grads, steps[-1])
         quad_copies = call(
-            copy_body, shape_of((QUAD, window) + slab), sums, after=(grads,)
+            copy_body, shape_of((QUAD, window) + slab), sums, after=(every_grad,)
         )
     with jax.named_scope("quad_gather"):
         every = exchange(quad_copies, "dp", quads).reshape(QUAD, 2, embed, rank)
-        table_grads = sum_tables(order, row_blocks, grads)[None]
+        table_grads = sum_tables(row_blocks, every_grad)[None]
         down_grad, up_grad = call(
             weights_body, (shape_of(down_proj.shape, F32), shape_of(up_proj.shape, F32)), every
         )

time: 188 us -> 207 us (1.10)
  the two profiles are of different devices: /device:TPU:2 before, /device:TPU:1 now
where the time goes in v4:
time: 207 us; the launch traced here: 206 us
  blocking collectives  63.2 us (31%)
  starting transfers between devices  59.8 us (29%)
  waiting for transfers between devices  49.5 us (24%)
  between operations  14.2 us (7%)
  Pallas kernels  13.7 us (7%)
  local copies, waits for them, and re-layouts  5.92 us (3%)
    all_to_all x2, blocking collectives, exchange(): lax.all_to_all(value, axis, 0, 0, axis_index_groups=groups, tiled=True)  63.2 us
    all_to_all x5, starting transfers between devices, exchange(): lax.all_to_all(value, axis, 0, 0, axis_index_groups=groups, tiled=True)  43 us
    all_to_all x5, waiting for transfers between devices, exchange(): lax.all_to_all(value, axis, 0, 0, axis_index_groups=groups, tiled=True)  23.9 us
    all_gather x1, waiting for transfers between devices, shards(): every_grad = lax.all_gather(grads, 'mp', axis=0, tiled=True)  22.2 us
    ppermute x6, starting transfers between devices, swap(): got.append(lax.ppermute(values[step], 'dp', pairs))  16.7 us
    pallas_call x3, Pallas kernels, call_sliced(): pl.pallas_call(body, out_shape=out_shape, grid_spec=pltpu.PrefetchScalarG...  6.01 us
    unnamed x18, local copies, waits for them, and re-layouts  5.48 us
    pallas_call x8, Pallas kernels, call(): pl.pallas_call(run, out_shape=out_shape, in_specs=[pl.BlockSpec(memory_sp...  5.16 us
  transfers between devices with their start and end apart: 12, of which 7 were waited for; matrix products, arithmetic and copies ran while one was open for 0% of the time, Pallas kernels for 3%

profile of v4, /device:TPU:1, one launch (start us, length us, event | category | flops | bytes accessed | tf_op | source)
XLA Modules:
  0.0 206.3 jit_solution(3784595413273337003)
XLA Ops:
  7.2 1.9 inputs.2
  9.1 17.6 %all-to-all-start = ((bf16[16,64,256]{2,1,0:T(8,128)(2,1)}), bf16[16,64,256]{2,1,0:T(8,128)(2,1)S(1)}, u32[]{:S(2)}, u32[]{:S(2)}) async-start(bf16[16,64,256]{2,1,0:T(8,128)(2,1)} %inputs.2), calls=%async_computation | async-start | bytes 1048576 | tf_op jit(solution)/shard_map/inputs/all_to_all | solution.py:285
  27.3 1.9 collective-permute-start
  29.2 1.9 collective-permute-start.1
  31.1 4.5 %collective-permute-start.2 = (bf16[96,256]{1,0:T(8,128)(2,1)S(1)}, bf16[96,256]{1,0:T(8,128)(2,1)S(1)}, u32[]{:S(2)}, u32[]{:S(2)}) collective-permute-start(bf16[96,256]{1,0:T(8,128)(2,1)S(1)} %get-tuple-element.24), channel_id=1, source_target_pairs={{0,528},{16,512},{32,560},{48,544},{64,592},{80,576},{96,624},{112... | collective-permute-start | bytes 147464 | tf_op jit(solution)/shard_map/inputs/ppermute | solution.py:292
  35.7 1.7 collective-permute-done.2.packed3_ref
  37.4 0.8 all-to-all-done
  38.3 3.1 %forward.1 = (bf16[2,256,256]{2,1,0:T(8,128)(2,1)S(1)}, bf16[2,256,256]{2,1,0:T(8,128)(2,1)}) custom-call(s32[1]{0:T(128)} %bitcast.quad_ref.refs_0_, bf16[1024,256]{1,0:T(8,128)(2,1)S(1)} %bitcast.11, bf16[96,256]{1,0:T(8,128)(2,1)S(1)} %get-tuple-element.21.packed0_ref, bf16[96,256]{1,0:T(8,128)(2,1)S(1)} %collective-permute-done.packed1_ref, ...), custom_call_target="tpu_custom_call" | custom-call | tf_op jit(solution)/shard_map/forward/pallas_call | solution.py:72
  41.4 9.6 %all-to-all-start.1 = ((bf16[64,8,256]{2,1,0:T(8,128)(2,1)}), bf16[64,8,256]{2,1,0:T(8,128)(2,1)S(1)}, u32[]{:S(2)}, u32[]{:S(2)}) async-start(bf16[64,8,256]{2,1,0:T(8,128)(2,1)} %bitcast.5), calls=%async_computation.1 | async-start | bytes 524288 | tf_op jit(solution)/shard_map/ranks/all_to_all | solution.py:285
  51.0 2.0 counts.1
  53.1 1.3 copy-done.3
  54.4 6.6 %all-to-all-done.1.refs_0_ = bf16[64,8,256]{2,1,0:T(8,128)(2,1)S(1)} async-done(((bf16[64,8,256]{2,1,0:T(8,128)(2,1)}), bf16[64,8,256]{2,1,0:T(8,128)(2,1)S(1)}, u32[]{:S(2)}, u32[]{:S(2)}) %all-to-all-start.1) | async-done | bytes 262176 | tf_op jit(solution)/shard_map/ranks/all_to_all | solution.py:285
  61.1 14.0 %all_to_all.35 = bf16[64,8,256]{2,1,0:T(8,128)(2,1)S(1)} all-to-all(bf16[64,8,256]{2,1,0:T(8,128)(2,1)S(1)} %ranks.1), channel_id=1, replica_groups={{0,16,512,528,1,17,513,529,2,18,514,530,3,19,515,531,4,20,516,532,5,21,..., dimensions={0} | all-to-all | bytes 524288 | tf_op jit(solution)/shard_map/ranks/all_to_all | solution.py:285
  75.1 1.0 cross.1
  76.0 3.4 %all-to-all-start.3 = ((bf16[4,128,256]{2,1,0:T(8,128)(2,1)}), bf16[4,128,256]{2,1,0:T(8,128)(2,1)S(1)}, u32[]{:S(2)}, u32[]{:S(2)}) async-start(bf16[4,128,256]{2,1,0:T(8,128)(2,1)} %bitcast.8), calls=%async_computation.3 | async-start | bytes 524288 | tf_op jit(solution)/shard_map/near_sums/all_to_all | solution.py:285
  79.5 2.2 %collective-permute-start.3 = (bf16[2,64,256]{2,1,0:T(8,128)(2,1)S(1)}, bf16[2,64,256]{2,1,0:T(8,128)(2,1)S(1)}, u32[]{:S(2)}, u32[]{:S(2)}) collective-permute-start(bf16[2,64,256]{2,1,0:T(8,128)(2,1)S(1)} %get-tuple-element.29), channel_id=1, source_target_pairs={{0,16},{16,0},{32,48},{48,32},{64,80},{80,64},{96,112},{112,96},{1... | collective-permute-start | bytes 196616 | tf_op jit(solution)/shard_map/near_sums/ppermute | solution.py:292
  81.7 1.9 collective-permute-start.4
  83.6 4.2 %collective-permute-start.5 = (bf16[2,64,256]{2,1,0:T(8,128)(2,1)S(1)}, bf16[2,64,256]{2,1,0:T(8,128)(2,1)S(1)}, u32[]{:S(2)}, u32[]{:S(2)}) collective-permute-start(bf16[2,64,256]{2,1,0:T(8,128)(2,1)S(1)} %get-tuple-element.31), channel_id=1, source_target_pairs={{0,528},{16,512},{32,560},{48,544},{64,592},{80,576},{96,624},{112... | collective-permute-start | bytes 196616 | tf_op jit(solution)/shard_map/near_sums/ppermute | solution.py:292
  87.9 1.6 collective-permute-done.5.refs_4_
  89.5 0.7 near_sums.2
  90.3 7.1 %all-to-all-done.3.refs_0_ = bf16[4,128,256]{2,1,0:T(8,128)(2,1)S(1)} async-done(((bf16[4,128,256]{2,1,0:T(8,128)(2,1)}), bf16[4,128,256]{2,1,0:T(8,128)(2,1)S(1)}, u32[]{:S(2)}, u32[]{:S(2)}) %all-to-all-start.3) | async-done | bytes 262176 | tf_op jit(solution)/shard_map/near_sums/all_to_all | solution.py:285
  97.4 49.2 %all_to_all.36.refs_0_ = bf16[4,128,256]{2,1,0:T(8,128)(2,1)S(1)} all-to-all(bf16[4,128,256]{2,1,0:T(8,128)(2,1)S(1)} %near_sums.3), channel_id=1, replica_groups={{0,128,256,384},{32,160,288,416},{64,192,320,448},{96,224,352,480},{16,..., dimensions={0} | all-to-all | bytes 524288 | tf_op jit(solution)/shard_map/far_sums/all_to_all | solution.py:285
  146.5 0.7 far_sums.1
  147.3 8.9 %all-to-all-start.5 = ((bf16[4,128,256]{2,1,0:T(8,128)(2,1)}), bf16[4,128,256]{2,1,0:T(8,128)(2,1)S(1)}, u32[]{:S(2)}, u32[]{:S(2)}) async-start(bf16[4,128,256]{2,1,0:T(8,128)(2,1)} %far_sums.1), calls=%async_computation.5 | async-start | bytes 524288 | tf_op jit(solution)/shard_map/near_gather/all_to_all | solution.py:285
  156.2 22.2 %all-gather.2.cloned.1.call-done.grads_ref.refs_1_ = bf16[64,64,256]{2,1,0:T(8,128)(2,1)} async-done(((bf16[4,64,256]{2,1,0:T(8,128)(2,1)}), bf16[64,64,256]{2,1,0:T(8,128)(2,1)}) %all-gather.2.cloned.1.call-update) | async-done | bytes 2097168 | tf_op jit(solution)/shard_map/near_sums/all_gather | solution.py:339
  178.3 1.6 copy-done
  180.0 1.0 copy-done.2
  181.0 3.5 %all-to-all-start.6 = ((bf16[4,4,128,256]{3,2,1,0:T(8,128)(2,1)}), bf16[4,4,128,256]{3,2,1,0:T(8,128)(2,1)S(1)}, u32[]{:S(2)}, u32[]{:S(2)}) async-start(bf16[4,4,128,256]{3,2,1,0:T(8,128)(2,1)} %copy-done.2), calls=%async_computation.6 | async-start | bytes 2097152 | tf_op jit(solution)/shard_map/quad_gather/all_to_all | solution.py:285
  184.5 1.6 copy-done.4
  186.1 2.5 %quad_gather.2 = bf16[64,64,256]{2,1,0:T(8,128)(2,1)} custom-call(bf16[16,256,256]{2,1,0:T(8,128)(2,1)S(1)} %copy-done.4, bf16[64,64,256]{2,1,0:T(8,128)(2,1)S(1)} %copy-done.1), custom_call_target="tpu_custom_call" | custom-call | tf_op jit(solution)/shard_map/quad_gather/pallas_call | solution.py:248
  188.6 9.4 %all-to-all-done.6 = bf16[4,4,128,256]{3,2,1,0:T(8,128)(2,1)S(1)} async-done(((bf16[4,4,128,256]{3,2,1,0:T(8,128)(2,1)}), bf16[4,4,128,256]{3,2,1,0:T(8,128)(2,1)S(1)}, u32[]{:S(2)}, u32[]{:S(2)}) %all-to-all-start.6) | async-done | bytes 1048608 | tf_op jit(solution)/shard_map/quad_gather/all_to_all | solution.py:285
  198.0 1.4 quad_gather.3
  (27 shorter events, 0.8 us)
Async XLA Ops:
  7.2 19.6 %copy-start.8 = (s32[64,64,16]{1,2,0:T(8,128)S(1)}, s32[64,64,16]{1,2,0:T(8,128)}, u32[]{:S(2)}) copy-start(s32[64,64,16]{1,2,0:T(8,128)} %param.5) | copy-start | bytes 786436
  9.1 18.1 %copy-start.7 = (bf16[64,1024]{1,0:T(8,128)(2,1)S(1)}, bf16[64,1024]{1,0:T(8,128)(2,1)}, u32[]{:S(2)}) copy-start(bf16[64,1024]{1,0:T(8,128)(2,1)} %refs_3_.1) | copy-start | bytes 393220
  9.1 29.1 %copy-start.5 = (bf16[1024,256]{1,0:T(8,128)(2,1)S(1)}, bf16[1024,256]{1,0:T(8,128)(2,1)}, u32[]{:S(2)}) copy-start(bf16[1024,256]{1,0:T(8,128)(2,1)} %down_ref.3) | copy-start | bytes 1572868
  9.1 29.1 %copy-start.6 = (bf16[256,1024]{1,0:T(8,128)(2,1)S(1)}, bf16[256,1024]{1,0:T(8,128)(2,1)}, u32[]{:S(2)}) copy-start(bf16[256,1024]{1,0:T(8,128)(2,1)} %up_ref.3) | copy-start | bytes 1572868
  9.1 29.1 %all-to-all-start = ((bf16[16,64,256]{2,1,0:T(8,128)(2,1)}), bf16[16,64,256]{2,1,0:T(8,128)(2,1)S(1)}, u32[]{:S(2)}, u32[]{:S(2)}) async-start(bf16[16,64,256]{2,1,0:T(8,128)(2,1)} %inputs.2), calls=%async_computation | async-start | bytes 1048576 | tf_op jit(solution)/shard_map/inputs/all_to_all | solution.py:285
  27.3 8.4 %collective-permute-start = (bf16[96,256]{1,0:T(8,128)(2,1)S(1)}, bf16[96,256]{1,0:T(8,128)(2,1)S(1)}, u32[]{:S(2)}, u32[]{:S(2)}) collective-permute-start(bf16[96,256]{1,0:T(8,128)(2,1)S(1)} %get-tuple-element.22), channel_id=1, source_target_pairs={{0,16},{16,0},{32,48},{48,32},{64,80},{80,64},{96,112},{112,96},{1... | collective-permute-start | bytes 147464 | tf_op jit(solution)/shard_map/inputs/ppermute | solution.py:292
  29.2 6.5 %collective-permute-start.1 = (bf16[96,256]{1,0:T(8,128)(2,1)S(1)}, bf16[96,256]{1,0:T(8,128)(2,1)S(1)}, u32[]{:S(2)}, u32[]{:S(2)}) collective-permute-start(bf16[96,256]{1,0:T(8,128)(2,1)S(1)} %get-tuple-element.23), channel_id=1, source_target_pairs={{0,512},{16,528},{32,544},{48,560},{64,576},{80,592},{96,608},{112... | collective-permute-start | bytes 147464 | tf_op jit(solution)/shard_map/inputs/ppermute | solution.py:292
  31.1 6.3 %collective-permute-start.2 = (bf16[96,256]{1,0:T(8,128)(2,1)S(1)}, bf16[96,256]{1,0:T(8,128)(2,1)S(1)}, u32[]{:S(2)}, u32[]{:S(2)}) collective-permute-start(bf16[96,256]{1,0:T(8,128)(2,1)S(1)} %get-tuple-element.24), channel_id=1, source_target_pairs={{0,528},{16,512},{32,560},{48,544},{64,592},{80,576},{96,624},{112... | collective-permute-start | bytes 147464 | tf_op jit(solution)/shard_map/inputs/ppermute | solution.py:292
  41.4 19.6 %all-to-all-start.1 = ((bf16[64,8,256]{2,1,0:T(8,128)(2,1)}), bf16[64,8,256]{2,1,0:T(8,128)(2,1)S(1)}, u32[]{:S(2)}, u32[]{:S(2)}) async-start(bf16[64,8,256]{2,1,0:T(8,128)(2,1)} %bitcast.5), calls=%async_computation.1 | async-start | bytes 524288 | tf_op jit(solution)/shard_map/ranks/all_to_all | solution.py:285
  53.0 1.3 copy-start.3
  76.0 21.3 %all-to-all-start.3 = ((bf16[4,128,256]{2,1,0:T(8,128)(2,1)}), bf16[4,128,256]{2,1,0:T(8,128)(2,1)S(1)}, u32[]{:S(2)}, u32[]{:S(2)}) async-start(bf16[4,128,256]{2,1,0:T(8,128)(2,1)} %bitcast.8), calls=%async_computation.3 | async-start | bytes 524288 | tf_op jit(solution)/shard_map/near_sums/all_to_all | solution.py:285
  79.4 98.9 %all-gather.2.cloned.1.call-start = ((), (), s32[]{:S(2)}) async-start(), calls=%async_computation.7 | async-start | bytes 2228224 | tf_op jit(solution)/shard_map/near_sums/all_gather | solution.py:339
  79.5 8.4 %collective-permute-start.3 = (bf16[2,64,256]{2,1,0:T(8,128)(2,1)S(1)}, bf16[2,64,256]{2,1,0:T(8,128)(2,1)S(1)}, u32[]{:S(2)}, u32[]{:S(2)}) collective-permute-start(bf16[2,64,256]{2,1,0:T(8,128)(2,1)S(1)} %get-tuple-element.29), channel_id=1, source_target_pairs={{0,16},{16,0},{32,48},{48,32},{64,80},{80,64},{96,112},{112,96},{1... | collective-permute-start | bytes 196616 | tf_op jit(solution)/shard_map/near_sums/ppermute | solution.py:292
  81.7 6.2 %collective-permute-start.4 = (bf16[2,64,256]{2,1,0:T(8,128)(2,1)S(1)}, bf16[2,64,256]{2,1,0:T(8,128)(2,1)S(1)}, u32[]{:S(2)}, u32[]{:S(2)}) collective-permute-start(bf16[2,64,256]{2,1,0:T(8,128)(2,1)S(1)} %get-tuple-element.30), channel_id=1, source_target_pairs={{0,512},{16,528},{32,544},{48,560},{64,576},{80,592},{96,608},{112... | collective-permute-start | bytes 196616 | tf_op jit(solution)/shard_map/near_sums/ppermute | solution.py:292
  83.6 5.9 %collective-permute-start.5 = (bf16[2,64,256]{2,1,0:T(8,128)(2,1)S(1)}, bf16[2,64,256]{2,1,0:T(8,128)(2,1)S(1)}, u32[]{:S(2)}, u32[]{:S(2)}) collective-permute-start(bf16[2,64,256]{2,1,0:T(8,128)(2,1)S(1)} %get-tuple-element.31), channel_id=1, source_target_pairs={{0,528},{16,512},{32,560},{48,544},{64,592},{80,576},{96,624},{112... | collective-permute-start | bytes 196616 | tf_op jit(solution)/shard_map/near_sums/ppermute | solution.py:292
  147.3 31.1 %all-to-all-start.5 = ((bf16[4,128,256]{2,1,0:T(8,128)(2,1)}), bf16[4,128,256]{2,1,0:T(8,128)(2,1)S(1)}, u32[]{:S(2)}, u32[]{:S(2)}) async-start(bf16[4,128,256]{2,1,0:T(8,128)(2,1)} %far_sums.1), calls=%async_computation.5 | async-start | bytes 524288 | tf_op jit(solution)/shard_map/near_gather/all_to_all | solution.py:285
  178.3 1.6 copy-start
  179.9 4.6 %copy-start.1 = (bf16[64,64,256]{2,1,0:T(8,128)(2,1)S(1)}, bf16[64,64,256]{2,1,0:T(8,128)(2,1)}, u32[]{:S(2)}) copy-start(bf16[64,64,256]{2,1,0:T(8,128)(2,1)} %all-gather.2.cloned.1.call-done.grads_ref.refs_1_) | copy-start | bytes 6291460
  180.0 1.0 copy-start.2
  181.0 17.0 %all-to-all-start.6 = ((bf16[4,4,128,256]{3,2,1,0:T(8,128)(2,1)}), bf16[4,4,128,256]{3,2,1,0:T(8,128)(2,1)S(1)}, u32[]{:S(2)}, u32[]{:S(2)}) async-start(bf16[4,4,128,256]{3,2,1,0:T(8,128)(2,1)} %copy-done.2), calls=%async_computation.6 | async-start | bytes 2097152 | tf_op jit(solution)/shard_map/quad_gather/all_to_all | solution.py:285
  184.5 1.6 copy-start.4
Sparse Core Ops, SparseCore 0:
  90.4 87.8 all-gather.1

commit v5 on v4

--- a/solution.py
+++ b/solution.py
@@ -1,5 +1,3 @@
-import math
-
 import jax
 import jax.numpy as jnp
 from jax import lax
@@ -22,23 +20,13 @@
     def member(pair, quad):
         return (quad // 2) * depth + pair * 2 + quad % 2
 
-    window = math.isqrt(pairs)
     quads = [[member(pair, quad) for quad in range(QUAD)] for pair in range(pairs)]
-    near = [
-        [member(start + index, quad) for index in range(window)]
-        for quad in range(QUAD)
-        for start in range(0, pairs, window)
-    ]
-    far = [
-        [member(pair, quad) for pair in range(index, pairs, window)]
-        for quad in range(QUAD)
-        for index in range(window)
-    ]
+    lines = [[member(pair, quad) for pair in range(pairs)] for quad in range(QUAD)]
     blocks = [
         [member(pair, quad) * mp_count + index for index in range(mp_count) for quad in range(QUAD)]
         for pair in range(pairs)
     ]
-    return quads, near, far, blocks
+    return quads, lines, blocks
 
 
 def call(body, out_shape, *operands, after=()):
@@ -134,15 +122,15 @@
     return ids
 
 
-def block_body(shard_ref, ids_ref, blocks_ref, done_ref):
+def block_body(order_ref, ids_ref, blocks_ref, done_ref):
     shards_of, width, _ = blocks_ref.shape
     rows = width // QUAD
     row_of = lax.broadcasted_iota(jnp.int32, (width, width), 0) // rows
     column_of = lax.broadcasted_iota(jnp.int32, (width, width), 1) // rows
 
     def shard_at(index, carry):
-        start = pl.multiple_of(index * width, width)
-        counts = count_of(ids_ref[:, pl.ds(start, width)], shard_ref[0] * rows, rows)
+        start = pl.multiple_of(order_ref[index] * width, width)
+        counts = count_of(ids_ref[:, pl.ds(start, width)], order_ref[0] * rows, rows)
         tall = jnp.concatenate([counts] * QUAD, axis=0)
         blocks_ref[index] = jnp.where(row_of == column_of, tall, 0.0).astype(BF16)
         return carry
@@ -226,33 +214,37 @@
         pooled_grad_ref[lax.bitwise_xor(quad_ref[0], step)] = one_ref[1]
 
 
-def table_body(blocks_ref, grads_ref, out_ref):
+def table_body(order_ref, blocks_ref, grads_ref, out_ref):
     count, width, _ = blocks_ref.shape
     _, rows, embed = out_ref.shape
+    first = pl.program_id(0) * count
     for index in range(count):
-        features = slice(index * QUAD, (index + 1) * QUAD)
-        grads = grads_ref[features].reshape(width, embed)
+        grads = grads_ref[index * QUAD : (index + 1) * QUAD].reshape(width, embed)
         sums = contract(blocks_ref[index], grads, 1, 0).astype(BF16)
-        out_ref[features] = sums.reshape(QUAD, rows, embed)
-
-
-def sum_tables(blocks, grads):
+        start = order_ref[first + index] * QUAD
+        for feature in range(QUAD):
+            out_ref[start + feature] = sums[feature * rows : (feature + 1) * rows]
+
+
+def sum_tables(order, blocks, grads):
     features, group, embed = grads.shape
     shards_of, width, _ = blocks.shape
-    rows = width // QUAD
     count = shards_of // 4
-
-    def block(*shape):
-        return pl.BlockSpec(shape, lambda index: (index, 0, 0))
-
+    out = (features, width // QUAD, embed)
     return pl.pallas_call(
         table_body,
-        out_shape=shape_of((features, rows, embed)),
-        grid=(4,),
-        in_specs=[block(count, width, width), block(count * QUAD, group, embed)],
-        out_specs=block(count * QUAD, rows, embed),
+        out_shape=shape_of(out),
+        grid_spec=pltpu.PrefetchScalarGridSpec(
+            num_scalar_prefetch=1,
+            grid=(4,),
+            in_specs=[
+                pl.BlockSpec((count, width, width), lambda index, order: (index, 0, 0)),
+                pl.BlockSpec((count * QUAD, group, embed), lambda index, order: (index, 0, 0)),
+            ],
+            out_specs=pl.BlockSpec(out, lambda index, order: (0, 0, 0)),
+        ),
         compiler_params=pltpu.CompilerParams(vmem_limit_bytes=VMEM_LIMIT),
-    )(blocks, grads)
+    )(order, blocks, grads)
 
 
 def weights_body(sums_ref, down_ref, up_ref):
@@ -270,8 +262,8 @@
 def shards(bag_ids, tables, down_proj, up_proj, cotangent):
     dp_count, ways = lax.axis_size("dp"), lax.axis_size("mp")
     depth = dp_count // 2
-    quads, near, far, blocks = layout_of(dp_count, ways)
-    window, windows, members = len(near[0]), len(far[0]), len(blocks[0])
+    quads, lines, blocks = layout_of(dp_count, ways)
+    pairs, members = len(lines[0]), len(blocks[0])
     place = lax.axis_index("dp")
     quad = (place // depth) * 2 + place % 2
     quad_at = quad.reshape(1)
@@ -292,6 +284,10 @@
             got.append(lax.ppermute(values[step], "dp", pairs))
         return got
 
+    def double(value, mask):
+        other = lax.ppermute(value, "mp", [(index, index ^ mask) for index in range(ways)])
+        return jnp.concatenate([value, other], axis=0), other
+
     with jax.named_scope("inputs"):
         table_parts = call_sliced(
             slice_body, shape_of((ways, rows, embed)), quad_at, (),
@@ -306,8 +302,13 @@
         weights = ((down_proj, 0), (up_proj, 1))
 
     with jax.named_scope("counts"):
+        steps = [ways >> (index + 1) for index in range(ways.bit_length() - 1)]
+        order = [shard_index]
+        for mask in steps:
+            order = order + [index ^ mask for index in order]
+        order = jnp.stack(order)
         row_blocks, done = call(
-            block_body, (shape_of((ways, QUAD * rows, QUAD * group)), shape_of((8, 128), F32)), shard_index.reshape(1), ids
+            block_body, (shape_of((ways, QUAD * rows, QUAD * group)), shape_of((8, 128), F32)), order, ids
         )
 
     with jax.named_scope("forward"):
@@ -328,26 +329,24 @@
             quad_at, (ranks, state), weights,
         )
 
-    slab = (2 * embed // window, rank)
-    with jax.named_scope("near_sums"):
-        near_parts = exchange(parts.reshape((window,) + slab), "dp", near)
+    slab = (2 * embed // pairs, rank)
+    with jax.named_scope("line_sums"):
+        line_parts = exchange(parts.reshape((pairs,) + slab), "dp", lines)
         cross_out, grads = call(
             arrange_body, (shape_of((group, QUAD * embed)), shape_of((QUAD, group, embed))),
             quad_at, *swap(backs),
         )
-        near_copies = call(add_body, shape_of((windows,) + slab), near_parts, after=(grads,))
-        every_grad = lax.all_gather(grads, "mp", axis=0, tiled=True)
-    with jax.named_scope("far_sums"):
-        far_parts = exchange(near_copies, "dp", far)
-        far_copies = call(add_body, shape_of((window,) + slab), far_parts)
-    with jax.named_scope("near_gather"):
-        sums = exchange(far_copies, "dp", near)
-        quad_copies = call(
-            copy_body, shape_of((QUAD, window) + slab), sums, after=(every_grad,)
-        )
+        grads, arrived = double(grads, steps[0])
+        copies = call(add_body, shape_of((pairs,) + slab), line_parts, after=(arrived,))
+    with jax.named_scope("line_gather"):
+        sums = exchange(copies, "dp", lines)
+        for mask in steps[1:-1]:
+            grads, arrived = double(grads, mask)
+        quad_copies = call(copy_body, shape_of((QUAD, pairs) + slab), sums, after=(arrived,))
     with jax.named_scope("quad_gather"):
         every = exchange(quad_copies, "dp", quads).reshape(QUAD, 2, embed, rank)
-        table_grads = sum_tables(row_blocks, every_grad)[None]
+        grads, _ = double(grads, steps[-1])
+        table_grads = sum_tables(order, row_blocks, grads)[None]
         down_grad, up_grad = call(
             weights_body, (shape_of(down_proj.shape, F32), shape_of(up_proj.shape, F32)), every
         )

time: 207 us -> 203 us (0.981)
  blocking collectives: 63.2 us -> 14 us
  starting transfers between devices: 59.8 us -> 107 us
  between operations: 14.2 us -> 0.92 us
  waiting for transfers between devices: 49.5 us -> 61.7 us
  local copies, waits for them, and re-layouts: 5.92 us -> 2.07 us
  Pallas kernels: 13.7 us -> 15.8 us
    all_to_all x2 -> x1, blocking collectives: 63.2 us -> 14 us  [exchange(): lax.all_to_all(value, axis, 0, 0, axis_index_groups=groups, tiled=True)]
    all_to_all x5, starting transfers between devices: 43 us -> 76.3 us  [exchange(): lax.all_to_all(value, axis, 0, 0, axis_index_groups=groups, tiled=True)]
    ppermute x0 -> x4, waiting for transfers between devices: none -> 24.6 us  [double(): lax.ppermute(value, 'mp', [(index, index ^ mask) for index in range(ways)])]
    all_gather x1 -> x0, waiting for transfers between devices: 22.2 us -> none  [shards(): every_grad = lax.all_gather(grads, 'mp', axis=0, tiled=True)]
    ppermute x0 -> x4, starting transfers between devices: none -> 13.6 us  [double(): lax.ppermute(value, 'mp', [(index, index ^ mask) for index in range(ways)])]
    ppermute x6, waiting for transfers between devices: 3.38 us -> 16.3 us  [swap(): got.append(lax.ppermute(values[step], 'dp', pairs))]
    unnamed x18 -> x16, local copies, waits for them, and re-layouts: 5.48 us -> 1.42 us
    all_to_all x5, waiting for transfers between devices: 23.9 us -> 20.9 us  [exchange(): lax.all_to_all(value, axis, 0, 0, axis_index_groups=groups, tiled=True)]
  transfers between devices with their start and end apart: 12 -> 15, of which waited for: 7 -> 11; matrix products, arithmetic and copies ran while one was open for 0% -> 0% of each run, Pallas kernels for 3% -> 3%
where the time goes in v5:
time: 203 us; the launch traced here: 201 us
  starting transfers between devices  107 us (53%)
  waiting for transfers between devices  61.7 us (30%)
  Pallas kernels  15.8 us (8%)
  blocking collectives  14 us (7%)
  local copies, waits for them, and re-layouts  2.07 us (1%)
    all_to_all x5, starting transfers between devices, exchange(): lax.all_to_all(value, axis, 0, 0, axis_index_groups=groups, tiled=True)  76.3 us
    ppermute x4, waiting for transfers between devices, double(): lax.ppermute(value, 'mp', [(index, index ^ mask) for index in range(ways)])  24.6 us
    all_to_all x5, waiting for transfers between devices, exchange(): lax.all_to_all(value, axis, 0, 0, axis_index_groups=groups, tiled=True)  20.9 us
    ppermute x6, starting transfers between devices, swap(): got.append(lax.ppermute(values[step], 'dp', pairs))  16.7 us
    ppermute x6, waiting for transfers between devices, swap(): got.append(lax.ppermute(values[step], 'dp', pairs))  16.3 us
    all_to_all x1, blocking collectives, exchange(): lax.all_to_all(value, axis, 0, 0, axis_index_groups=groups, tiled=True)  14 us
    ppermute x4, starting transfers between devices, double(): lax.ppermute(value, 'mp', [(index, index ^ mask) for index in range(ways)])  13.6 us
    pallas_call x7, Pallas kernels, call(): pl.pallas_call(run, out_shape=out_shape, in_specs=[pl.BlockSpec(memory_sp...  6.62 us
  transfers between devices with their start and end apart: 15, of which 11 were waited for; matrix products, arithmetic and copies ran while one was open for 0% of the time, Pallas kernels for 3%

profile of v5, /device:TPU:1, one launch (start us, length us, event | category | flops | bytes accessed | tf_op | source)
XLA Modules:
  0.0 201.3 jit_solution(16730101306986787204)
XLA Ops:
  0.7 1.9 inputs.2
  2.6 17.6 %all-to-all-start = ((bf16[16,64,256]{2,1,0:T(8,128)(2,1)}), bf16[16,64,256]{2,1,0:T(8,128)(2,1)S(1)}, u32[]{:S(2)}, u32[]{:S(2)}) async-start(bf16[16,64,256]{2,1,0:T(8,128)(2,1)} %inputs.2), calls=%async_computation | async-start | bytes 1048576 | tf_op jit(solution)/shard_map/inputs/all_to_all | solution.py:277
  20.8 1.9 collective-permute-start
  22.7 1.9 collective-permute-start.1
  24.6 4.5 %collective-permute-start.2 = (bf16[96,256]{1,0:T(8,128)(2,1)S(1)}, bf16[96,256]{1,0:T(8,128)(2,1)S(1)}, u32[]{:S(2)}, u32[]{:S(2)}) collective-permute-start(bf16[96,256]{1,0:T(8,128)(2,1)S(1)} %get-tuple-element.24), channel_id=1, source_target_pairs={{0,528},{16,512},{32,560},{48,544},{64,592},{80,576},{96,624},{112... | collective-permute-start | bytes 147464 | tf_op jit(solution)/shard_map/inputs/ppermute | solution.py:284
  29.2 1.7 collective-permute-done.2.packed3_ref
  31.7 3.1 %forward.1 = (bf16[2,256,256]{2,1,0:T(8,128)(2,1)S(1)}, bf16[2,256,256]{2,1,0:T(8,128)(2,1)}) custom-call(s32[1]{0:T(128)} %bitcast.quad_ref.refs_0_, bf16[1024,256]{1,0:T(8,128)(2,1)S(1)} %bitcast.26, bf16[96,256]{1,0:T(8,128)(2,1)S(1)} %get-tuple-element.21.packed0_ref, bf16[96,256]{1,0:T(8,128)(2,1)S(1)} %collective-permute-done.packed1_ref, ...), custom_call_target="tpu_custom_call" | custom-call | tf_op jit(solution)/shard_map/forward/pallas_call | solution.py:60
  34.9 9.6 %all-to-all-start.1 = ((bf16[64,8,256]{2,1,0:T(8,128)(2,1)}), bf16[64,8,256]{2,1,0:T(8,128)(2,1)S(1)}, u32[]{:S(2)}, u32[]{:S(2)}) async-start(bf16[64,8,256]{2,1,0:T(8,128)(2,1)} %bitcast.5), calls=%async_computation.1 | async-start | bytes 524288 | tf_op jit(solution)/shard_map/ranks/all_to_all | solution.py:277
  44.6 2.6 %counts.1 = (bf16[16,256,256]{2,1,0:T(8,128)(2,1)S(1)}, f32[8,128]{1,0:T(8,128)S(1)}) custom-call(s32[16]{0:T(128)S(1)} %stack.64.refs_0_.order_ref, s32[16,4096]{1,0:T(8,128)S(1)} %reshape.39.refs_2_.refs_1_), custom_call_target="tpu_custom_call" | custom-call | tf_op jit(solution)/shard_map/counts/pallas_call | solution.py:36
  47.2 1.3 copy-done
  48.5 5.9 %all-to-all-done.1.refs_0_ = bf16[64,8,256]{2,1,0:T(8,128)(2,1)S(1)} async-done(((bf16[64,8,256]{2,1,0:T(8,128)(2,1)}), bf16[64,8,256]{2,1,0:T(8,128)(2,1)S(1)}, u32[]{:S(2)}, u32[]{:S(2)}) %all-to-all-start.1) | async-done | bytes 262176 | tf_op jit(solution)/shard_map/ranks/all_to_all | solution.py:277
  54.5 14.0 %all_to_all.30 = bf16[64,8,256]{2,1,0:T(8,128)(2,1)S(1)} all-to-all(bf16[64,8,256]{2,1,0:T(8,128)(2,1)S(1)} %ranks.1), channel_id=1, replica_groups={{0,16,512,528,1,17,513,529,2,18,514,530,3,19,515,531,4,20,516,532,5,21,..., dimensions={0} | all-to-all | bytes 524288 | tf_op jit(solution)/shard_map/ranks/all_to_all | solution.py:277
  69.5 19.7 %all-to-all-start.3 = ((bf16[16,32,256]{2,1,0:T(8,128)(2,1)}), bf16[16,32,256]{2,1,0:T(8,128)(2,1)S(1)}, u32[]{:S(2)}, u32[]{:S(2)}) async-start(bf16[16,32,256]{2,1,0:T(8,128)(2,1)} %bitcast.23), calls=%async_computation.3 | async-start | bytes 524288 | tf_op jit(solution)/shard_map/line_sums/all_to_all | solution.py:277
  89.3 2.2 %collective-permute-start.3 = (bf16[2,64,256]{2,1,0:T(8,128)(2,1)S(1)}, bf16[2,64,256]{2,1,0:T(8,128)(2,1)S(1)}, u32[]{:S(2)}, u32[]{:S(2)}) collective-permute-start(bf16[2,64,256]{2,1,0:T(8,128)(2,1)S(1)} %get-tuple-element.29), channel_id=1, source_target_pairs={{0,16},{16,0},{32,48},{48,32},{64,80},{80,64},{96,112},{112,96},{1... | collective-permute-start | bytes 196616 | tf_op jit(solution)/shard_map/line_sums/ppermute | solution.py:284
  91.5 1.9 collective-permute-start.4
  93.4 4.2 %collective-permute-start.5 = (bf16[2,64,256]{2,1,0:T(8,128)(2,1)S(1)}, bf16[2,64,256]{2,1,0:T(8,128)(2,1)S(1)}, u32[]{:S(2)}, u32[]{:S(2)}) collective-permute-start(bf16[2,64,256]{2,1,0:T(8,128)(2,1)S(1)} %get-tuple-element.31), channel_id=1, source_target_pairs={{0,528},{16,512},{32,560},{48,544},{64,592},{80,576},{96,624},{112... | collective-permute-start | bytes 196616 | tf_op jit(solution)/shard_map/line_sums/ppermute | solution.py:284
  97.7 7.6 %collective-permute-done.3.refs_2_ = bf16[2,64,256]{2,1,0:T(8,128)(2,1)S(1)} collective-permute-done((bf16[2,64,256]{2,1,0:T(8,128)(2,1)S(1)}, bf16[2,64,256]{2,1,0:T(8,128)(2,1)S(1)}, u32[]{:S(2)}, u32[]{:S(2)}) %collective-permute-start.3) | collective-permute-done | bytes 65568 | tf_op jit(solution)/shard_map/line_sums/ppermute | solution.py:284
  105.2 6.9 %collective-permute-done.5.refs_4_ = bf16[2,64,256]{2,1,0:T(8,128)(2,1)S(1)} collective-permute-done((bf16[2,64,256]{2,1,0:T(8,128)(2,1)S(1)}, bf16[2,64,256]{2,1,0:T(8,128)(2,1)S(1)}, u32[]{:S(2)}, u32[]{:S(2)}) %collective-permute-start.5) | collective-permute-done | bytes 65568 | tf_op jit(solution)/shard_map/line_sums/ppermute | solution.py:284
  112.9 2.0 collective-permute-start.6
  114.8 5.5 %collective-permute-done.6.refs_1_ = bf16[4,64,256]{2,1,0:T(8,128)(2,1)S(1)} collective-permute-done((bf16[4,64,256]{2,1,0:T(8,128)(2,1)S(1)}, bf16[4,64,256]{2,1,0:T(8,128)(2,1)S(1)}, u32[]{:S(2)}, u32[]{:S(2)}) %collective-permute-start.6) | collective-permute-done | bytes 131104 | tf_op jit(solution)/shard_map/line_sums/ppermute | solution.py:288
  121.1 24.8 %all-to-all-start.4 = ((bf16[16,32,256]{2,1,0:T(8,128)(2,1)}), bf16[16,32,256]{2,1,0:T(8,128)(2,1)S(1)}, u32[]{:S(2)}, u32[]{:S(2)}) async-start(bf16[16,32,256]{2,1,0:T(8,128)(2,1)} %line_sums.3), calls=%async_computation.4 | async-start | bytes 524288 | tf_op jit(solution)/shard_map/line_gather/all_to_all | solution.py:277
  145.9 3.3 %collective-permute-start.7 = (bf16[8,64,256]{2,1,0:T(8,128)(2,1)S(1)}, bf16[8,64,256]{2,1,0:T(8,128)(2,1)S(1)}, u32[]{:S(2)}, u32[]{:S(2)}) collective-permute-start(bf16[8,64,256]{2,1,0:T(8,128)(2,1)S(1)} %pad_maximum_fusion.2), channel_id=1, source_target_pairs={{0,4},{1,5},{2,6},{3,7},{4,0},{5,1},{6,2},{7,3},{8,12},{9,13},{10,... | collective-permute-start | bytes 786440 | tf_op jit(solution)/shard_map/line_gather/ppermute | solution.py:288
  149.3 6.2 %collective-permute-done.7 = bf16[8,64,256]{2,1,0:T(8,128)(2,1)S(1)} collective-permute-done((bf16[8,64,256]{2,1,0:T(8,128)(2,1)S(1)}, bf16[8,64,256]{2,1,0:T(8,128)(2,1)S(1)}, u32[]{:S(2)}, u32[]{:S(2)}) %collective-permute-start.7) | collective-permute-done | bytes 262176 | tf_op jit(solution)/shard_map/line_gather/ppermute | solution.py:288
  155.6 2.1 %collective-permute-start.8 = (bf16[16,64,256]{2,1,0:T(8,128)(2,1)S(1)}, bf16[16,64,256]{2,1,0:T(8,128)(2,1)S(1)}, u32[]{:S(2)}, u32[]{:S(2)}) collective-permute-start(bf16[16,64,256]{2,1,0:T(8,128)(2,1)S(1)} %pad_maximum_fusion.1), channel_id=1, source_target_pairs={{0,2},{1,3},{2,0},{3,1},{4,6},{5,7},{6,4},{7,5},{8,10},{9,11},{10,... | collective-permute-start | bytes 1572872 | tf_op jit(solution)/shard_map/line_gather/ppermute | solution.py:288
  157.7 10.7 %collective-permute-done.8.refs_1_ = bf16[16,64,256]{2,1,0:T(8,128)(2,1)S(1)} collective-permute-done((bf16[16,64,256]{2,1,0:T(8,128)(2,1)S(1)}, bf16[16,64,256]{2,1,0:T(8,128)(2,1)S(1)}, u32[]{:S(2)}, u32[]{:S(2)}) %collective-permute-start.8) | collective-permute-done | bytes 524320 | tf_op jit(solution)/shard_map/line_gather/ppermute | solution.py:288
  168.3 12.3 %all-to-all-done.4.refs_0_ = bf16[16,32,256]{2,1,0:T(8,128)(2,1)S(1)} async-done(((bf16[16,32,256]{2,1,0:T(8,128)(2,1)}), bf16[16,32,256]{2,1,0:T(8,128)(2,1)S(1)}, u32[]{:S(2)}, u32[]{:S(2)}) %all-to-all-start.4) | async-done | bytes 262176 | tf_op jit(solution)/shard_map/line_gather/all_to_all | solution.py:277
  181.6 4.5 %all-to-all-start.5 = ((bf16[4,16,32,256]{3,2,1,0:T(8,128)(2,1)}), bf16[4,16,32,256]{3,2,1,0:T(8,128)(2,1)S(1)}, u32[]{:S(2)}, u32[]{:S(2)}) async-start(bf16[4,16,32,256]{3,2,1,0:T(8,128)(2,1)} %line_gather.1), calls=%async_computation.5 | async-start | bytes 2097152 | tf_op jit(solution)/shard_map/quad_gather/all_to_all | solution.py:277
  186.3 6.2 %collective-permute-start.9 = (bf16[32,64,256]{2,1,0:T(8,128)(2,1)S(1)}, bf16[32,64,256]{2,1,0:T(8,128)(2,1)S(1)}, u32[]{:S(2)}, u32[]{:S(2)}) collective-permute-start(bf16[32,64,256]{2,1,0:T(8,128)(2,1)S(1)} %pad_maximum_fusion), channel_id=1, source_target_pairs={{0,1},{1,0},{2,3},{3,2},{4,5},{5,4},{6,7},{7,6},{8,9},{9,8},{10,11... | collective-permute-start | bytes 3145736 | tf_op jit(solution)/shard_map/quad_gather/ppermute | solution.py:288
  192.6 2.2 %collective-permute-done.9 = bf16[32,64,256]{2,1,0:T(8,128)(2,1)S(1)} collective-permute-done((bf16[32,64,256]{2,1,0:T(8,128)(2,1)S(1)}, bf16[32,64,256]{2,1,0:T(8,128)(2,1)S(1)}, u32[]{:S(2)}, u32[]{:S(2)}) %collective-permute-start.9) | collective-permute-done | bytes 1048608 | tf_op jit(solution)/shard_map/quad_gather/ppermute | solution.py:288
  194.9 3.2 %quad_gather.2 = bf16[64,64,256]{2,1,0:T(8,128)(2,1)} custom-call(s32[16]{0:T(128)S(1)} %stack.64.refs_0_.order_ref, bf16[16,256,256]{2,1,0:T(8,128)(2,1)S(1)} %copy-done.1, bf16[64,64,256]{2,1,0:T(8,128)(2,1)S(1)} %constant_dynamic-update-slice_fusion.grads_ref), custom_call_target="tpu_custom_call" | custom-call | tf_op jit(solution)/shard_map/quad_gather/pallas_call | solution.py:234
  198.0 1.9 all-to-all-done.5
  199.9 1.4 quad_gather.3
  (33 shorter events, 5.3 us)
Async XLA Ops:
  0.6 19.6 %copy-start.5 = (s32[64,64,16]{1,2,0:T(8,128)S(1)}, s32[64,64,16]{1,2,0:T(8,128)}, u32[]{:S(2)}) copy-start(s32[64,64,16]{1,2,0:T(8,128)} %param.5) | copy-start | bytes 786436
  2.6 18.1 %copy-start.4 = (bf16[64,1024]{1,0:T(8,128)(2,1)S(1)}, bf16[64,1024]{1,0:T(8,128)(2,1)}, u32[]{:S(2)}) copy-start(bf16[64,1024]{1,0:T(8,128)(2,1)} %refs_3_.1) | copy-start | bytes 393220
  2.6 29.1 %copy-start.2 = (bf16[1024,256]{1,0:T(8,128)(2,1)S(1)}, bf16[1024,256]{1,0:T(8,128)(2,1)}, u32[]{:S(2)}) copy-start(bf16[1024,256]{1,0:T(8,128)(2,1)} %down_ref.3) | copy-start | bytes 1572868
  2.6 29.1 %copy-start.3 = (bf16[256,1024]{1,0:T(8,128)(2,1)S(1)}, bf16[256,1024]{1,0:T(8,128)(2,1)}, u32[]{:S(2)}) copy-start(bf16[256,1024]{1,0:T(8,128)(2,1)} %up_ref.3) | copy-start | bytes 1572868
  2.6 29.1 %all-to-all-start = ((bf16[16,64,256]{2,1,0:T(8,128)(2,1)}), bf16[16,64,256]{2,1,0:T(8,128)(2,1)S(1)}, u32[]{:S(2)}, u32[]{:S(2)}) async-start(bf16[16,64,256]{2,1,0:T(8,128)(2,1)} %inputs.2), calls=%async_computation | async-start | bytes 1048576 | tf_op jit(solution)/shard_map/inputs/all_to_all | solution.py:277
  20.8 8.4 %collective-permute-start = (bf16[96,256]{1,0:T(8,128)(2,1)S(1)}, bf16[96,256]{1,0:T(8,128)(2,1)S(1)}, u32[]{:S(2)}, u32[]{:S(2)}) collective-permute-start(bf16[96,256]{1,0:T(8,128)(2,1)S(1)} %get-tuple-element.22), channel_id=1, source_target_pairs={{0,16},{16,0},{32,48},{48,32},{64,80},{80,64},{96,112},{112,96},{1... | collective-permute-start | bytes 147464 | tf_op jit(solution)/shard_map/inputs/ppermute | solution.py:284
  22.7 6.5 %collective-permute-start.1 = (bf16[96,256]{1,0:T(8,128)(2,1)S(1)}, bf16[96,256]{1,0:T(8,128)(2,1)S(1)}, u32[]{:S(2)}, u32[]{:S(2)}) collective-permute-start(bf16[96,256]{1,0:T(8,128)(2,1)S(1)} %get-tuple-element.23), channel_id=1, source_target_pairs={{0,512},{16,528},{32,544},{48,560},{64,576},{80,592},{96,608},{112... | collective-permute-start | bytes 147464 | tf_op jit(solution)/shard_map/inputs/ppermute | solution.py:284
  24.6 6.3 %collective-permute-start.2 = (bf16[96,256]{1,0:T(8,128)(2,1)S(1)}, bf16[96,256]{1,0:T(8,128)(2,1)S(1)}, u32[]{:S(2)}, u32[]{:S(2)}) collective-permute-start(bf16[96,256]{1,0:T(8,128)(2,1)S(1)} %get-tuple-element.24), channel_id=1, source_target_pairs={{0,528},{16,512},{32,560},{48,544},{64,592},{80,576},{96,624},{112... | collective-permute-start | bytes 147464 | tf_op jit(solution)/shard_map/inputs/ppermute | solution.py:284
  34.9 19.6 %all-to-all-start.1 = ((bf16[64,8,256]{2,1,0:T(8,128)(2,1)}), bf16[64,8,256]{2,1,0:T(8,128)(2,1)S(1)}, u32[]{:S(2)}, u32[]{:S(2)}) async-start(bf16[64,8,256]{2,1,0:T(8,128)(2,1)} %bitcast.5), calls=%async_computation.1 | async-start | bytes 524288 | tf_op jit(solution)/shard_map/ranks/all_to_all | solution.py:277
  47.2 1.3 copy-start
  69.5 50.9 %all-to-all-start.3 = ((bf16[16,32,256]{2,1,0:T(8,128)(2,1)}), bf16[16,32,256]{2,1,0:T(8,128)(2,1)S(1)}, u32[]{:S(2)}, u32[]{:S(2)}) async-start(bf16[16,32,256]{2,1,0:T(8,128)(2,1)} %bitcast.23), calls=%async_computation.3 | async-start | bytes 524288 | tf_op jit(solution)/shard_map/line_sums/all_to_all | solution.py:277
  89.3 16.0 %collective-permute-start.3 = (bf16[2,64,256]{2,1,0:T(8,128)(2,1)S(1)}, bf16[2,64,256]{2,1,0:T(8,128)(2,1)S(1)}, u32[]{:S(2)}, u32[]{:S(2)}) collective-permute-start(bf16[2,64,256]{2,1,0:T(8,128)(2,1)S(1)} %get-tuple-element.29), channel_id=1, source_target_pairs={{0,16},{16,0},{32,48},{48,32},{64,80},{80,64},{96,112},{112,96},{1... | collective-permute-start | bytes 196616 | tf_op jit(solution)/shard_map/line_sums/ppermute | solution.py:284
  91.5 13.8 %collective-permute-start.4 = (bf16[2,64,256]{2,1,0:T(8,128)(2,1)S(1)}, bf16[2,64,256]{2,1,0:T(8,128)(2,1)S(1)}, u32[]{:S(2)}, u32[]{:S(2)}) collective-permute-start(bf16[2,64,256]{2,1,0:T(8,128)(2,1)S(1)} %get-tuple-element.30), channel_id=1, source_target_pairs={{0,512},{16,528},{32,544},{48,560},{64,576},{80,592},{96,608},{112... | collective-permute-start | bytes 196616 | tf_op jit(solution)/shard_map/line_sums/ppermute | solution.py:284
  93.4 18.8 %collective-permute-start.5 = (bf16[2,64,256]{2,1,0:T(8,128)(2,1)S(1)}, bf16[2,64,256]{2,1,0:T(8,128)(2,1)S(1)}, u32[]{:S(2)}, u32[]{:S(2)}) collective-permute-start(bf16[2,64,256]{2,1,0:T(8,128)(2,1)S(1)} %get-tuple-element.31), channel_id=1, source_target_pairs={{0,528},{16,512},{32,560},{48,544},{64,592},{80,576},{96,624},{112... | collective-permute-start | bytes 196616 | tf_op jit(solution)/shard_map/line_sums/ppermute | solution.py:284
  112.9 7.5 %collective-permute-start.6 = (bf16[4,64,256]{2,1,0:T(8,128)(2,1)S(1)}, bf16[4,64,256]{2,1,0:T(8,128)(2,1)S(1)}, u32[]{:S(2)}, u32[]{:S(2)}) collective-permute-start(bf16[4,64,256]{2,1,0:T(8,128)(2,1)S(1)} %get-tuple-element.34), channel_id=1, source_target_pairs={{0,8},{1,9},{2,10},{3,11},{4,12},{5,13},{6,14},{7,15},{8,0},{9,1},... | collective-permute-start | bytes 393224 | tf_op jit(solution)/shard_map/line_sums/ppermute | solution.py:288
  121.1 59.5 %all-to-all-start.4 = ((bf16[16,32,256]{2,1,0:T(8,128)(2,1)}), bf16[16,32,256]{2,1,0:T(8,128)(2,1)S(1)}, u32[]{:S(2)}, u32[]{:S(2)}) async-start(bf16[16,32,256]{2,1,0:T(8,128)(2,1)} %line_sums.3), calls=%async_computation.4 | async-start | bytes 524288 | tf_op jit(solution)/shard_map/line_gather/all_to_all | solution.py:277
  145.9 9.6 %collective-permute-start.7 = (bf16[8,64,256]{2,1,0:T(8,128)(2,1)S(1)}, bf16[8,64,256]{2,1,0:T(8,128)(2,1)S(1)}, u32[]{:S(2)}, u32[]{:S(2)}) collective-permute-start(bf16[8,64,256]{2,1,0:T(8,128)(2,1)S(1)} %pad_maximum_fusion.2), channel_id=1, source_target_pairs={{0,4},{1,5},{2,6},{3,7},{4,0},{5,1},{6,2},{7,3},{8,12},{9,13},{10,... | collective-permute-start | bytes 786440 | tf_op jit(solution)/shard_map/line_gather/ppermute | solution.py:288
  155.6 12.8 %collective-permute-start.8 = (bf16[16,64,256]{2,1,0:T(8,128)(2,1)S(1)}, bf16[16,64,256]{2,1,0:T(8,128)(2,1)S(1)}, u32[]{:S(2)}, u32[]{:S(2)}) collective-permute-start(bf16[16,64,256]{2,1,0:T(8,128)(2,1)S(1)} %pad_maximum_fusion.1), channel_id=1, source_target_pairs={{0,2},{1,3},{2,0},{3,1},{4,6},{5,7},{6,4},{7,5},{8,10},{9,11},{10,... | collective-permute-start | bytes 1572872 | tf_op jit(solution)/shard_map/line_gather/ppermute | solution.py:288
  181.6 18.3 %all-to-all-start.5 = ((bf16[4,16,32,256]{3,2,1,0:T(8,128)(2,1)}), bf16[4,16,32,256]{3,2,1,0:T(8,128)(2,1)S(1)}, u32[]{:S(2)}, u32[]{:S(2)}) async-start(bf16[4,16,32,256]{3,2,1,0:T(8,128)(2,1)} %line_gather.1), calls=%async_computation.5 | async-start | bytes 2097152 | tf_op jit(solution)/shard_map/quad_gather/all_to_all | solution.py:277
  186.3 8.6 %copy-start.1 = (bf16[16,256,256]{2,1,0:T(8,128)(2,1)S(1)}, bf16[16,256,256]{2,1,0:T(8,128)(2,1)}, u32[]{:S(2)}) copy-start(bf16[16,256,256]{2,1,0:T(8,128)(2,1)} %copy-done) | copy-start | bytes 6291460
  186.3 8.5 %collective-permute-start.9 = (bf16[32,64,256]{2,1,0:T(8,128)(2,1)S(1)}, bf16[32,64,256]{2,1,0:T(8,128)(2,1)S(1)}, u32[]{:S(2)}, u32[]{:S(2)}) collective-permute-start(bf16[32,64,256]{2,1,0:T(8,128)(2,1)S(1)} %pad_maximum_fusion), channel_id=1, source_target_pairs={{0,1},{1,0},{2,3},{3,2},{4,5},{5,4},{6,7},{7,6},{8,9},{9,8},{10,11... | collective-permute-start | bytes 3145736 | tf_op jit(solution)/shard_map/quad_gather/ppermute | solution.py:288

commit v6 on v5

--- a/solution.py
+++ b/solution.py
@@ -1,3 +1,5 @@
+import math
+
 import jax
 import jax.numpy as jnp
 from jax import lax
@@ -20,13 +22,23 @@
     def member(pair, quad):
         return (quad // 2) * depth + pair * 2 + quad % 2
 
+    window = math.isqrt(pairs)
     quads = [[member(pair, quad) for quad in range(QUAD)] for pair in range(pairs)]
-    lines = [[member(pair, quad) for pair in range(pairs)] for quad in range(QUAD)]
+    near = [
+        [member(start + index, quad) for index in range(window)]
+        for quad in range(QUAD)
+        for start in range(0, pairs, window)
+    ]
+    far = [
+        [member(pair, quad) for pair in range(index, pairs, window)]
+        for quad in range(QUAD)
+        for index in range(window)
+    ]
     blocks = [
         [member(pair, quad) * mp_count + index for index in range(mp_count) for quad in range(QUAD)]
         for pair in range(pairs)
     ]
-    return quads, lines, blocks
+    return quads, near, far, blocks
 
 
 def call(body, out_shape, *operands, after=()):
@@ -262,8 +274,8 @@
 def shards(bag_ids, tables, down_proj, up_proj, cotangent):
     dp_count, ways = lax.axis_size("dp"), lax.axis_size("mp")
     depth = dp_count // 2
-    quads, lines, blocks = layout_of(dp_count, ways)
-    pairs, members = len(lines[0]), len(blocks[0])
+    quads, near, far, blocks = layout_of(dp_count, ways)
+    window, windows, members = len(near[0]), len(far[0]), len(blocks[0])
     place = lax.axis_index("dp")
     quad = (place // depth) * 2 + place % 2
     quad_at = quad.reshape(1)
@@ -329,23 +341,27 @@
             quad_at, (ranks, state), weights,
         )
 
-    slab = (2 * embed // pairs, rank)
-    with jax.named_scope("line_sums"):
-        line_parts = exchange(parts.reshape((pairs,) + slab), "dp", lines)
+    slab = (2 * embed // window, rank)
+    with jax.named_scope("near_sums"):
+        near_parts = exchange(parts.reshape((window,) + slab), "dp", near)
         cross_out, grads = call(
             arrange_body, (shape_of((group, QUAD * embed)), shape_of((QUAD, group, embed))),
             quad_at, *swap(backs),
         )
-        grads, arrived = double(grads, steps[0])
-        copies = call(add_body, shape_of((pairs,) + slab), line_parts, after=(arrived,))
-    with jax.named_scope("line_gather"):
-        sums = exchange(copies, "dp", lines)
-        for mask in steps[1:-1]:
+        near_copies = call(add_body, shape_of((windows,) + slab), near_parts, after=(grads,))
+    with jax.named_scope("far_sums"):
+        far_parts = exchange(near_copies, "dp", far)
+        for mask in steps[:-1]:
             grads, arrived = double(grads, mask)
-        quad_copies = call(copy_body, shape_of((QUAD, pairs) + slab), sums, after=(arrived,))
+        far_copies = call(add_body, shape_of((window,) + slab), far_parts, after=(arrived,))
+    with jax.named_scope("near_gather"):
+        sums = exchange(far_copies, "dp", near)
+        grads, arrived = double(grads, steps[-1])
+        quad_copies = call(
+            copy_body, shape_of((QUAD, window) + slab), sums, after=(arrived,)
+        )
     with jax.named_scope("quad_gather"):
         every = exchange(quad_copies, "dp", quads).reshape(QUAD, 2, embed, rank)
-        grads, _ = double(grads, steps[-1])
         table_grads = sum_tables(order, row_blocks, grads)[None]
         down_grad, up_grad = call(
             weights_body, (shape_of(down_proj.shape, F32), shape_of(up_proj.shape, F32)), every

time: 203 us -> 182 us (0.90)
  the two profiles are of different devices: /device:TPU:1 before, /device:TPU:2 now
where the time goes in v6:
time: 182 us; the launch traced here: 181 us
  starting transfers between devices  94.4 us (52%)
  waiting for transfers between devices  51.7 us (28%)
  Pallas kernels  15.5 us (9%)
  blocking collectives  14 us (8%)
  local copies, waits for them, and re-layouts  4.4 us (2%)
    all_to_all x6, starting transfers between devices, exchange(): lax.all_to_all(value, axis, 0, 0, axis_index_groups=groups, tiled=True)  65.5 us
    ppermute x4, waiting for transfers between devices, double(): lax.ppermute(value, 'mp', [(index, index ^ mask) for index in range(ways)])  26.4 us
    all_to_all x6, waiting for transfers between devices, exchange(): lax.all_to_all(value, axis, 0, 0, axis_index_groups=groups, tiled=True)  19.8 us
    ppermute x6, starting transfers between devices, swap(): got.append(lax.ppermute(values[step], 'dp', pairs))  18.4 us
    all_to_all x1, blocking collectives, exchange(): lax.all_to_all(value, axis, 0, 0, axis_index_groups=groups, tiled=True)  14 us
    ppermute x4, starting transfers between devices, double(): lax.ppermute(value, 'mp', [(index, index ^ mask) for index in range(ways)])  10.5 us
    pallas_call x8, Pallas kernels, call(): pl.pallas_call(run, out_shape=out_shape, in_specs=[pl.BlockSpec(memory_sp...  6.37 us
    pallas_call x3, Pallas kernels, call_sliced(): pl.pallas_call(body, out_shape=out_shape, grid_spec=pltpu.PrefetchScalarG...  6.02 us
  transfers between devices with their start and end apart: 16, of which 10 were waited for; matrix products, arithmetic and copies ran while one was open for 1% of the time, Pallas kernels for 4%

profile of v6, /device:TPU:2, one launch (start us, length us, event | category | flops | bytes accessed | tf_op | source)
XLA Modules:
  0.0 181.1 jit_solution(14985097566498428623)
XLA Ops:
  0.7 1.9 %inputs.2 = bf16[16,64,256]{2,1,0:T(8,128)(2,1)} custom-call(s32[1]{0:T(128)} %bitcast.quad_ref.refs_0_, bf16[16,4,64,256]{3,2,1,0:T(8,128)(2,1)} %bitcast.29), custom_call_target="tpu_custom_call" | custom-call | tf_op jit(solution)/shard_map/inputs/pallas_call | solution.py:72
  2.6 16.7 %all-to-all-start = ((bf16[16,64,256]{2,1,0:T(8,128)(2,1)}), bf16[16,64,256]{2,1,0:T(8,128)(2,1)S(1)}, u32[]{:S(2)}, u32[]{:S(2)}) async-start(bf16[16,64,256]{2,1,0:T(8,128)(2,1)} %inputs.2), calls=%async_computation | async-start | bytes 1048576 | tf_op jit(solution)/shard_map/inputs/all_to_all | solution.py:289
  19.8 1.9 %collective-permute-start = (bf16[96,256]{1,0:T(8,128)(2,1)S(1)}, bf16[96,256]{1,0:T(8,128)(2,1)S(1)}, u32[]{:S(2)}, u32[]{:S(2)}) collective-permute-start(bf16[96,256]{1,0:T(8,128)(2,1)S(1)} %get-tuple-element.22), channel_id=1, source_target_pairs={{0,16},{16,0},{32,48},{48,32},{64,80},{80,64},{96,112},{112,96},{1... | collective-permute-start | bytes 147464 | tf_op jit(solution)/shard_map/inputs/ppermute | solution.py:296
  21.7 1.9 %collective-permute-start.1 = (bf16[96,256]{1,0:T(8,128)(2,1)S(1)}, bf16[96,256]{1,0:T(8,128)(2,1)S(1)}, u32[]{:S(2)}, u32[]{:S(2)}) collective-permute-start(bf16[96,256]{1,0:T(8,128)(2,1)S(1)} %get-tuple-element.23), channel_id=1, source_target_pairs={{0,512},{16,528},{32,544},{48,560},{64,576},{80,592},{96,608},{112... | collective-permute-start | bytes 147464 | tf_op jit(solution)/shard_map/inputs/ppermute | solution.py:296
  23.7 5.4 %collective-permute-start.2 = (bf16[96,256]{1,0:T(8,128)(2,1)S(1)}, bf16[96,256]{1,0:T(8,128)(2,1)S(1)}, u32[]{:S(2)}, u32[]{:S(2)}) collective-permute-start(bf16[96,256]{1,0:T(8,128)(2,1)S(1)} %get-tuple-element.24), channel_id=1, source_target_pairs={{0,528},{16,512},{32,560},{48,544},{64,592},{80,576},{96,624},{112... | collective-permute-start | bytes 147464 | tf_op jit(solution)/shard_map/inputs/ppermute | solution.py:296
  29.1 2.0 %collective-permute-done.2.packed3_ref = bf16[96,256]{1,0:T(8,128)(2,1)S(1)} collective-permute-done((bf16[96,256]{1,0:T(8,128)(2,1)S(1)}, bf16[96,256]{1,0:T(8,128)(2,1)S(1)}, u32[]{:S(2)}, u32[]{:S(2)}) %collective-permute-start.2) | collective-permute-done | bytes 49184 | tf_op jit(solution)/shard_map/inputs/ppermute | solution.py:296
  31.1 3.1 %forward.1 = (bf16[2,256,256]{2,1,0:T(8,128)(2,1)S(1)}, bf16[2,256,256]{2,1,0:T(8,128)(2,1)}) custom-call(s32[1]{0:T(128)} %bitcast.quad_ref.refs_0_, bf16[1024,256]{1,0:T(8,128)(2,1)S(1)} %bitcast.26, bf16[96,256]{1,0:T(8,128)(2,1)S(1)} %get-tuple-element.21.packed0_ref, bf16[96,256]{1,0:T(8,128)(2,1)S(1)} %collective-permute-done.packed1_ref, ...), custom_call_target="tpu_custom_call" | custom-call | tf_op jit(solution)/shard_map/forward/pallas_call | solution.py:72
  34.2 9.3 %all-to-all-start.1 = ((bf16[64,8,256]{2,1,0:T(8,128)(2,1)}), bf16[64,8,256]{2,1,0:T(8,128)(2,1)S(1)}, u32[]{:S(2)}, u32[]{:S(2)}) async-start(bf16[64,8,256]{2,1,0:T(8,128)(2,1)} %bitcast.5), calls=%async_computation.1 | async-start | bytes 524288 | tf_op jit(solution)/shard_map/ranks/all_to_all | solution.py:289
  43.6 2.6 %counts.1 = (bf16[16,256,256]{2,1,0:T(8,128)(2,1)S(1)}, f32[8,128]{1,0:T(8,128)S(1)}) custom-call(s32[16]{0:T(128)S(1)} %stack.64.refs_0_.order_ref, s32[16,4096]{1,0:T(8,128)S(1)} %reshape.39.refs_2_.refs_1_), custom_call_target="tpu_custom_call" | custom-call | tf_op jit(solution)/shard_map/counts/pallas_call | solution.py:48
  47.6 4.8 %all-to-all-done.1.refs_0_ = bf16[64,8,256]{2,1,0:T(8,128)(2,1)S(1)} async-done(((bf16[64,8,256]{2,1,0:T(8,128)(2,1)}), bf16[64,8,256]{2,1,0:T(8,128)(2,1)S(1)}, u32[]{:S(2)}, u32[]{:S(2)}) %all-to-all-start.1) | async-done | bytes 262176 | tf_op jit(solution)/shard_map/ranks/all_to_all | solution.py:289
  52.4 14.0 %all_to_all.35 = bf16[64,8,256]{2,1,0:T(8,128)(2,1)S(1)} all-to-all(bf16[64,8,256]{2,1,0:T(8,128)(2,1)S(1)} %ranks.1), channel_id=1, replica_groups={{0,16,512,528,1,17,513,529,2,18,514,530,3,19,515,531,4,20,516,532,5,21,..., dimensions={0} | all-to-all | bytes 524288 | tf_op jit(solution)/shard_map/ranks/all_to_all | solution.py:289
  67.4 3.4 %all-to-all-start.3 = ((bf16[4,128,256]{2,1,0:T(8,128)(2,1)}), bf16[4,128,256]{2,1,0:T(8,128)(2,1)S(1)}, u32[]{:S(2)}, u32[]{:S(2)}) async-start(bf16[4,128,256]{2,1,0:T(8,128)(2,1)} %bitcast.23), calls=%async_computation.3 | async-start | bytes 524288 | tf_op jit(solution)/shard_map/near_sums/all_to_all | solution.py:289
  70.8 2.7 %collective-permute-start.3 = (bf16[2,64,256]{2,1,0:T(8,128)(2,1)S(1)}, bf16[2,64,256]{2,1,0:T(8,128)(2,1)S(1)}, u32[]{:S(2)}, u32[]{:S(2)}) collective-permute-start(bf16[2,64,256]{2,1,0:T(8,128)(2,1)S(1)} %get-tuple-element.29), channel_id=1, source_target_pairs={{0,16},{16,0},{32,48},{48,32},{64,80},{80,64},{96,112},{112,96},{1... | collective-permute-start | bytes 196616 | tf_op jit(solution)/shard_map/near_sums/ppermute | solution.py:296
  73.5 2.5 %collective-permute-start.4 = (bf16[2,64,256]{2,1,0:T(8,128)(2,1)S(1)}, bf16[2,64,256]{2,1,0:T(8,128)(2,1)S(1)}, u32[]{:S(2)}, u32[]{:S(2)}) collective-permute-start(bf16[2,64,256]{2,1,0:T(8,128)(2,1)S(1)} %get-tuple-element.30), channel_id=1, source_target_pairs={{0,512},{16,528},{32,544},{48,560},{64,576},{80,592},{96,608},{112... | collective-permute-start | bytes 196616 | tf_op jit(solution)/shard_map/near_sums/ppermute | solution.py:296
  76.0 4.0 %collective-permute-start.5 = (bf16[2,64,256]{2,1,0:T(8,128)(2,1)S(1)}, bf16[2,64,256]{2,1,0:T(8,128)(2,1)S(1)}, u32[]{:S(2)}, u32[]{:S(2)}) collective-permute-start(bf16[2,64,256]{2,1,0:T(8,128)(2,1)S(1)} %get-tuple-element.31), channel_id=1, source_target_pairs={{0,528},{16,512},{32,560},{48,544},{64,592},{80,576},{96,624},{112... | collective-permute-start | bytes 196616 | tf_op jit(solution)/shard_map/near_sums/ppermute | solution.py:296
  80.0 3.4 %collective-permute-done.5.refs_4_ = bf16[2,64,256]{2,1,0:T(8,128)(2,1)S(1)} collective-permute-done((bf16[2,64,256]{2,1,0:T(8,128)(2,1)S(1)}, bf16[2,64,256]{2,1,0:T(8,128)(2,1)S(1)}, u32[]{:S(2)}, u32[]{:S(2)}) %collective-permute-start.5) | collective-permute-done | bytes 65568 | tf_op jit(solution)/shard_map/near_sums/ppermute | solution.py:296
  84.1 4.9 %all-to-all-done.3.refs_0_ = bf16[4,128,256]{2,1,0:T(8,128)(2,1)S(1)} async-done(((bf16[4,128,256]{2,1,0:T(8,128)(2,1)}), bf16[4,128,256]{2,1,0:T(8,128)(2,1)S(1)}, u32[]{:S(2)}, u32[]{:S(2)}) %all-to-all-start.3) | async-done | bytes 262176 | tf_op jit(solution)/shard_map/near_sums/all_to_all | solution.py:289
  89.7 20.9 %all-to-all-start.4 = ((bf16[4,128,256]{2,1,0:T(8,128)(2,1)}), bf16[4,128,256]{2,1,0:T(8,128)(2,1)S(1)}, u32[]{:S(2)}, u32[]{:S(2)}) async-start(bf16[4,128,256]{2,1,0:T(8,128)(2,1)} %near_sums.3), calls=%async_computation.4 | async-start | bytes 524288 | tf_op jit(solution)/shard_map/far_sums/all_to_all | solution.py:289
  110.6 2.5 %collective-permute-start.6 = (bf16[4,64,256]{2,1,0:T(8,128)(2,1)S(1)}, bf16[4,64,256]{2,1,0:T(8,128)(2,1)S(1)}, u32[]{:S(2)}, u32[]{:S(2)}) collective-permute-start(bf16[4,64,256]{2,1,0:T(8,128)(2,1)S(1)} %get-tuple-element.34.refs_1_), channel_id=1, source_target_pairs={{0,8},{1,9},{2,10},{3,11},{4,12},{5,13},{6,14},{7,15},{8,0},{9,1},... | collective-permute-start | bytes 393224 | tf_op jit(solution)/shard_map/far_sums/ppermute | solution.py:300
  113.1 6.0 %collective-permute-done.6 = bf16[4,64,256]{2,1,0:T(8,128)(2,1)S(1)} collective-permute-done((bf16[4,64,256]{2,1,0:T(8,128)(2,1)S(1)}, bf16[4,64,256]{2,1,0:T(8,128)(2,1)S(1)}, u32[]{:S(2)}, u32[]{:S(2)}) %collective-permute-start.6) | collective-permute-done | bytes 131104 | tf_op jit(solution)/shard_map/far_sums/ppermute | solution.py:300
  119.1 2.8 %collective-permute-start.7 = (bf16[8,64,256]{2,1,0:T(8,128)(2,1)S(1)}, bf16[8,64,256]{2,1,0:T(8,128)(2,1)S(1)}, u32[]{:S(2)}, u32[]{:S(2)}) collective-permute-start(bf16[8,64,256]{2,1,0:T(8,128)(2,1)S(1)} %pad_maximum_fusion.2), channel_id=1, source_target_pairs={{0,4},{1,5},{2,6},{3,7},{4,0},{5,1},{6,2},{7,3},{8,12},{9,13},{10,... | collective-permute-start | bytes 786440 | tf_op jit(solution)/shard_map/far_sums/ppermute | solution.py:300
  121.9 7.6 %collective-permute-done.7 = bf16[8,64,256]{2,1,0:T(8,128)(2,1)S(1)} collective-permute-done((bf16[8,64,256]{2,1,0:T(8,128)(2,1)S(1)}, bf16[8,64,256]{2,1,0:T(8,128)(2,1)S(1)}, u32[]{:S(2)}, u32[]{:S(2)}) %collective-permute-start.7) | collective-permute-done | bytes 262176 | tf_op jit(solution)/shard_map/far_sums/ppermute | solution.py:300
  129.6 3.3 %collective-permute-start.8 = (bf16[16,64,256]{2,1,0:T(8,128)(2,1)S(1)}, bf16[16,64,256]{2,1,0:T(8,128)(2,1)S(1)}, u32[]{:S(2)}, u32[]{:S(2)}) collective-permute-start(bf16[16,64,256]{2,1,0:T(8,128)(2,1)S(1)} %pad_maximum_fusion.1), channel_id=1, source_target_pairs={{0,2},{1,3},{2,0},{3,1},{4,6},{5,7},{6,4},{7,5},{8,10},{9,11},{10,... | collective-permute-start | bytes 1572872 | tf_op jit(solution)/shard_map/far_sums/ppermute | solution.py:300
  132.9 10.2 %collective-permute-done.8.refs_1_ = bf16[16,64,256]{2,1,0:T(8,128)(2,1)S(1)} collective-permute-done((bf16[16,64,256]{2,1,0:T(8,128)(2,1)S(1)}, bf16[16,64,256]{2,1,0:T(8,128)(2,1)S(1)}, u32[]{:S(2)}, u32[]{:S(2)}) %collective-permute-start.8) | collective-permute-done | bytes 524320 | tf_op jit(solution)/shard_map/far_sums/ppermute | solution.py:300
  143.9 11.7 %all-to-all-start.5 = ((bf16[4,128,256]{2,1,0:T(8,128)(2,1)}), bf16[4,128,256]{2,1,0:T(8,128)(2,1)S(1)}, u32[]{:S(2)}, u32[]{:S(2)}) async-start(bf16[4,128,256]{2,1,0:T(8,128)(2,1)} %far_sums.1), calls=%async_computation.5 | async-start | bytes 524288 | tf_op jit(solution)/shard_map/near_gather/all_to_all | solution.py:289
  155.7 1.9 %collective-permute-start.9 = (bf16[32,64,256]{2,1,0:T(8,128)(2,1)S(1)}, bf16[32,64,256]{2,1,0:T(8,128)(2,1)S(1)}, u32[]{:S(2)}, u32[]{:S(2)}) collective-permute-start(bf16[32,64,256]{2,1,0:T(8,128)(2,1)S(1)} %pad_maximum_fusion), channel_id=1, source_target_pairs={{0,1},{1,0},{2,3},{3,2},{4,5},{5,4},{6,7},{7,6},{8,9},{9,8},{10,11... | collective-permute-start | bytes 3145736 | tf_op jit(solution)/shard_map/near_gather/ppermute | solution.py:300
  157.6 2.6 %collective-permute-done.9.refs_1_ = bf16[32,64,256]{2,1,0:T(8,128)(2,1)S(1)} collective-permute-done((bf16[32,64,256]{2,1,0:T(8,128)(2,1)S(1)}, bf16[32,64,256]{2,1,0:T(8,128)(2,1)S(1)}, u32[]{:S(2)}, u32[]{:S(2)}) %collective-permute-start.9) | collective-permute-done | bytes 1048608 | tf_op jit(solution)/shard_map/near_gather/ppermute | solution.py:300
  160.2 5.5 %all-to-all-done.5.refs_0_ = bf16[4,128,256]{2,1,0:T(8,128)(2,1)S(1)} async-done(((bf16[4,128,256]{2,1,0:T(8,128)(2,1)}), bf16[4,128,256]{2,1,0:T(8,128)(2,1)S(1)}, u32[]{:S(2)}, u32[]{:S(2)}) %all-to-all-start.5) | async-done | bytes 262176 | tf_op jit(solution)/shard_map/near_gather/all_to_all | solution.py:289
  166.8 3.5 %all-to-all-start.6 = ((bf16[4,4,128,256]{3,2,1,0:T(8,128)(2,1)}), bf16[4,4,128,256]{3,2,1,0:T(8,128)(2,1)S(1)}, u32[]{:S(2)}, u32[]{:S(2)}) async-start(bf16[4,4,128,256]{3,2,1,0:T(8,128)(2,1)} %copy-done), calls=%async_computation.6 | async-start | bytes 2097152 | tf_op jit(solution)/shard_map/quad_gather/all_to_all | solution.py:289
  171.9 3.2 %quad_gather.2 = bf16[64,64,256]{2,1,0:T(8,128)(2,1)} custom-call(s32[16]{0:T(128)S(1)} %stack.64.refs_0_.order_ref, bf16[16,256,256]{2,1,0:T(8,128)(2,1)S(1)} %copy-done.2, bf16[64,64,256]{2,1,0:T(8,128)(2,1)S(1)} %constant_dynamic-update-slice_fusion.grads_ref), custom_call_target="tpu_custom_call" | custom-call | tf_op jit(solution)/shard_map/quad_gather/pallas_call | solution.py:246
  175.1 4.7 %all-to-all-done.6 = bf16[4,4,128,256]{3,2,1,0:T(8,128)(2,1)S(1)} async-done(((bf16[4,4,128,256]{3,2,1,0:T(8,128)(2,1)}), bf16[4,4,128,256]{3,2,1,0:T(8,128)(2,1)S(1)}, u32[]{:S(2)}, u32[]{:S(2)}) %all-to-all-start.6) | async-done | bytes 1048608 | tf_op jit(solution)/shard_map/quad_gather/all_to_all | solution.py:289
  179.7 1.4 quad_gather.3
  (38 shorter events, 7.9 us)
Async XLA Ops:
  0.6 18.7 %copy-start.6 = (s32[64,64,16]{1,2,0:T(8,128)S(1)}, s32[64,64,16]{1,2,0:T(8,128)}, u32[]{:S(2)}) copy-start(s32[64,64,16]{1,2,0:T(8,128)} %param.5) | copy-start | bytes 786436
  2.6 17.2 %copy-start.5 = (bf16[64,1024]{1,0:T(8,128)(2,1)S(1)}, bf16[64,1024]{1,0:T(8,128)(2,1)}, u32[]{:S(2)}) copy-start(bf16[64,1024]{1,0:T(8,128)(2,1)} %refs_3_.1) | copy-start | bytes 393220
  2.6 28.5 %copy-start.3 = (bf16[1024,256]{1,0:T(8,128)(2,1)S(1)}, bf16[1024,256]{1,0:T(8,128)(2,1)}, u32[]{:S(2)}) copy-start(bf16[1024,256]{1,0:T(8,128)(2,1)} %down_ref.3) | copy-start | bytes 1572868
  2.6 28.5 %copy-start.4 = (bf16[256,1024]{1,0:T(8,128)(2,1)S(1)}, bf16[256,1024]{1,0:T(8,128)(2,1)}, u32[]{:S(2)}) copy-start(bf16[256,1024]{1,0:T(8,128)(2,1)} %up_ref.3) | copy-start | bytes 1572868
  2.6 28.5 %all-to-all-start = ((bf16[16,64,256]{2,1,0:T(8,128)(2,1)}), bf16[16,64,256]{2,1,0:T(8,128)(2,1)S(1)}, u32[]{:S(2)}, u32[]{:S(2)}) async-start(bf16[16,64,256]{2,1,0:T(8,128)(2,1)} %inputs.2), calls=%async_computation | async-start | bytes 1048576 | tf_op jit(solution)/shard_map/inputs/all_to_all | solution.py:289
  19.8 9.2 %collective-permute-start = (bf16[96,256]{1,0:T(8,128)(2,1)S(1)}, bf16[96,256]{1,0:T(8,128)(2,1)S(1)}, u32[]{:S(2)}, u32[]{:S(2)}) collective-permute-start(bf16[96,256]{1,0:T(8,128)(2,1)S(1)} %get-tuple-element.22), channel_id=1, source_target_pairs={{0,16},{16,0},{32,48},{48,32},{64,80},{80,64},{96,112},{112,96},{1... | collective-permute-start | bytes 147464 | tf_op jit(solution)/shard_map/inputs/ppermute | solution.py:296
  21.7 7.3 %collective-permute-start.1 = (bf16[96,256]{1,0:T(8,128)(2,1)S(1)}, bf16[96,256]{1,0:T(8,128)(2,1)S(1)}, u32[]{:S(2)}, u32[]{:S(2)}) collective-permute-start(bf16[96,256]{1,0:T(8,128)(2,1)S(1)} %get-tuple-element.23), channel_id=1, source_target_pairs={{0,512},{16,528},{32,544},{48,560},{64,576},{80,592},{96,608},{112... | collective-permute-start | bytes 147464 | tf_op jit(solution)/shard_map/inputs/ppermute | solution.py:296
  23.7 7.4 %collective-permute-start.2 = (bf16[96,256]{1,0:T(8,128)(2,1)S(1)}, bf16[96,256]{1,0:T(8,128)(2,1)S(1)}, u32[]{:S(2)}, u32[]{:S(2)}) collective-permute-start(bf16[96,256]{1,0:T(8,128)(2,1)S(1)} %get-tuple-element.24), channel_id=1, source_target_pairs={{0,528},{16,512},{32,560},{48,544},{64,592},{80,576},{96,624},{112... | collective-permute-start | bytes 147464 | tf_op jit(solution)/shard_map/inputs/ppermute | solution.py:296
  34.2 18.1 %all-to-all-start.1 = ((bf16[64,8,256]{2,1,0:T(8,128)(2,1)}), bf16[64,8,256]{2,1,0:T(8,128)(2,1)S(1)}, u32[]{:S(2)}, u32[]{:S(2)}) async-start(bf16[64,8,256]{2,1,0:T(8,128)(2,1)} %bitcast.5), calls=%async_computation.1 | async-start | bytes 524288 | tf_op jit(solution)/shard_map/ranks/all_to_all | solution.py:289
  46.2 1.3 copy-start.1
  67.4 21.6 %all-to-all-start.3 = ((bf16[4,128,256]{2,1,0:T(8,128)(2,1)}), bf16[4,128,256]{2,1,0:T(8,128)(2,1)S(1)}, u32[]{:S(2)}, u32[]{:S(2)}) async-start(bf16[4,128,256]{2,1,0:T(8,128)(2,1)} %bitcast.23), calls=%async_computation.3 | async-start | bytes 524288 | tf_op jit(solution)/shard_map/near_sums/all_to_all | solution.py:289
  70.8 9.2 %collective-permute-start.3 = (bf16[2,64,256]{2,1,0:T(8,128)(2,1)S(1)}, bf16[2,64,256]{2,1,0:T(8,128)(2,1)S(1)}, u32[]{:S(2)}, u32[]{:S(2)}) collective-permute-start(bf16[2,64,256]{2,1,0:T(8,128)(2,1)S(1)} %get-tuple-element.29), channel_id=1, source_target_pairs={{0,16},{16,0},{32,48},{48,32},{64,80},{80,64},{96,112},{112,96},{1... | collective-permute-start | bytes 196616 | tf_op jit(solution)/shard_map/near_sums/ppermute | solution.py:296
  73.5 6.5 %collective-permute-start.4 = (bf16[2,64,256]{2,1,0:T(8,128)(2,1)S(1)}, bf16[2,64,256]{2,1,0:T(8,128)(2,1)S(1)}, u32[]{:S(2)}, u32[]{:S(2)}) collective-permute-start(bf16[2,64,256]{2,1,0:T(8,128)(2,1)S(1)} %get-tuple-element.30), channel_id=1, source_target_pairs={{0,512},{16,528},{32,544},{48,560},{64,576},{80,592},{96,608},{112... | collective-permute-start | bytes 196616 | tf_op jit(solution)/shard_map/near_sums/ppermute | solution.py:296
  76.0 7.4 %collective-permute-start.5 = (bf16[2,64,256]{2,1,0:T(8,128)(2,1)S(1)}, bf16[2,64,256]{2,1,0:T(8,128)(2,1)S(1)}, u32[]{:S(2)}, u32[]{:S(2)}) collective-permute-start(bf16[2,64,256]{2,1,0:T(8,128)(2,1)S(1)} %get-tuple-element.31), channel_id=1, source_target_pairs={{0,528},{16,512},{32,560},{48,544},{64,592},{80,576},{96,624},{112... | collective-permute-start | bytes 196616 | tf_op jit(solution)/shard_map/near_sums/ppermute | solution.py:296
  89.7 53.4 %all-to-all-start.4 = ((bf16[4,128,256]{2,1,0:T(8,128)(2,1)}), bf16[4,128,256]{2,1,0:T(8,128)(2,1)S(1)}, u32[]{:S(2)}, u32[]{:S(2)}) async-start(bf16[4,128,256]{2,1,0:T(8,128)(2,1)} %near_sums.3), calls=%async_computation.4 | async-start | bytes 524288 | tf_op jit(solution)/shard_map/far_sums/all_to_all | solution.py:289
  110.6 8.5 %collective-permute-start.6 = (bf16[4,64,256]{2,1,0:T(8,128)(2,1)S(1)}, bf16[4,64,256]{2,1,0:T(8,128)(2,1)S(1)}, u32[]{:S(2)}, u32[]{:S(2)}) collective-permute-start(bf16[4,64,256]{2,1,0:T(8,128)(2,1)S(1)} %get-tuple-element.34.refs_1_), channel_id=1, source_target_pairs={{0,8},{1,9},{2,10},{3,11},{4,12},{5,13},{6,14},{7,15},{8,0},{9,1},... | collective-permute-start | bytes 393224 | tf_op jit(solution)/shard_map/far_sums/ppermute | solution.py:300
  119.1 10.4 %collective-permute-start.7 = (bf16[8,64,256]{2,1,0:T(8,128)(2,1)S(1)}, bf16[8,64,256]{2,1,0:T(8,128)(2,1)S(1)}, u32[]{:S(2)}, u32[]{:S(2)}) collective-permute-start(bf16[8,64,256]{2,1,0:T(8,128)(2,1)S(1)} %pad_maximum_fusion.2), channel_id=1, source_target_pairs={{0,4},{1,5},{2,6},{3,7},{4,0},{5,1},{6,2},{7,3},{8,12},{9,13},{10,... | collective-permute-start | bytes 786440 | tf_op jit(solution)/shard_map/far_sums/ppermute | solution.py:300
  129.6 13.6 %collective-permute-start.8 = (bf16[16,64,256]{2,1,0:T(8,128)(2,1)S(1)}, bf16[16,64,256]{2,1,0:T(8,128)(2,1)S(1)}, u32[]{:S(2)}, u32[]{:S(2)}) collective-permute-start(bf16[16,64,256]{2,1,0:T(8,128)(2,1)S(1)} %pad_maximum_fusion.1), channel_id=1, source_target_pairs={{0,2},{1,3},{2,0},{3,1},{4,6},{5,7},{6,4},{7,5},{8,10},{9,11},{10,... | collective-permute-start | bytes 1572872 | tf_op jit(solution)/shard_map/far_sums/ppermute | solution.py:300
  143.9 21.8 %all-to-all-start.5 = ((bf16[4,128,256]{2,1,0:T(8,128)(2,1)}), bf16[4,128,256]{2,1,0:T(8,128)(2,1)S(1)}, u32[]{:S(2)}, u32[]{:S(2)}) async-start(bf16[4,128,256]{2,1,0:T(8,128)(2,1)} %far_sums.1), calls=%async_computation.5 | async-start | bytes 524288 | tf_op jit(solution)/shard_map/near_gather/all_to_all | solution.py:289
  155.7 4.6 %collective-permute-start.9 = (bf16[32,64,256]{2,1,0:T(8,128)(2,1)S(1)}, bf16[32,64,256]{2,1,0:T(8,128)(2,1)S(1)}, u32[]{:S(2)}, u32[]{:S(2)}) collective-permute-start(bf16[32,64,256]{2,1,0:T(8,128)(2,1)S(1)} %pad_maximum_fusion), channel_id=1, source_target_pairs={{0,1},{1,0},{2,3},{3,2},{4,5},{5,4},{6,7},{7,6},{8,9},{9,8},{10,11... | collective-permute-start | bytes 3145736 | tf_op jit(solution)/shard_map/near_gather/ppermute | solution.py:300
  165.8 1.0 copy-start
  166.8 12.9 %all-to-all-start.6 = ((bf16[4,4,128,256]{3,2,1,0:T(8,128)(2,1)}), bf16[4,4,128,256]{3,2,1,0:T(8,128)(2,1)S(1)}, u32[]{:S(2)}, u32[]{:S(2)}) async-start(bf16[4,4,128,256]{3,2,1,0:T(8,128)(2,1)} %copy-done), calls=%async_computation.6 | async-start | bytes 2097152 | tf_op jit(solution)/shard_map/quad_gather/all_to_all | solution.py:289
  170.3 1.6 copy-start.2

commit v7 on v6

--- a/solution.py
+++ b/solution.py
@@ -296,9 +296,12 @@
             got.append(lax.ppermute(values[step], "dp", pairs))
         return got
 
+    def other(value, mask):
+        return lax.ppermute(value, "mp", [(index, index ^ mask) for index in range(ways)])
+
     def double(value, mask):
-        other = lax.ppermute(value, "mp", [(index, index ^ mask) for index in range(ways)])
-        return jnp.concatenate([value, other], axis=0), other
+        arrived = other(value, mask)
+        return jnp.concatenate([value, arrived], axis=0), arrived
 
     with jax.named_scope("inputs"):
         table_parts = call_sliced(
@@ -351,12 +354,14 @@
         near_copies = call(add_body, shape_of((windows,) + slab), near_parts, after=(grads,))
     with jax.named_scope("far_sums"):
         far_parts = exchange(near_copies, "dp", far)
-        for mask in steps[:-1]:
-            grads, arrived = double(grads, mask)
+        first, second, third, last = steps
+        masks = (first, second, first ^ second)
+        grads = jnp.concatenate([grads] + [other(grads, mask) for mask in masks], axis=0)
+        grads, arrived = double(grads, third)
         far_copies = call(add_body, shape_of((window,) + slab), far_parts, after=(arrived,))
     with jax.named_scope("near_gather"):
         sums = exchange(far_copies, "dp", near)
-        grads, arrived = double(grads, steps[-1])
+        grads, arrived = double(grads, last)
         quad_copies = call(
             copy_body, shape_of((QUAD, window) + slab), sums, after=(arrived,)
         )

time: 182 us -> 183 us (level)
  waiting for transfers between devices: 51.7 us -> 42.7 us
  starting transfers between devices: 94.4 us -> 101 us
  local copies, waits for them, and re-layouts: 4.4 us -> 6.97 us
    ppermute x4 -> x5, waiting for transfers between devices: 26.4 us -> 17.9 us  [other(): lax.ppermute(value, 'mp', [(index, index ^ mask) for index in range(ways)])]
    ppermute x4 -> x5, starting transfers between devices: 10.5 us -> 16.8 us  [other(): lax.ppermute(value, 'mp', [(index, index ^ mask) for index in range(ways)])]
    unnamed x18 -> x20, local copies, waits for them, and re-layouts: 3.74 us -> 5.27 us
  transfers between devices with their start and end apart: 16 -> 17, of which waited for: 10 -> 10; matrix products, arithmetic and copies ran while one was open for 1% -> 1% of each run, Pallas kernels for 4% -> 4%
where the time goes in v7:
time: 183 us; the launch traced here: 182 us
  starting transfers between devices  101 us (55%)
  waiting for transfers between devices  42.7 us (23%)
  Pallas kernels  16.5 us (9%)
  blocking collectives  14 us (8%)
  local copies, waits for them, and re-layouts  6.97 us (4%)
    all_to_all x6, starting transfers between devices, exchange(): lax.all_to_all(value, axis, 0, 0, axis_index_groups=groups, tiled=True)  65.5 us
    all_to_all x6, waiting for transfers between devices, exchange(): lax.all_to_all(value, axis, 0, 0, axis_index_groups=groups, tiled=True)  19.4 us
    ppermute x6, starting transfers between devices, swap(): got.append(lax.ppermute(values[step], 'dp', pairs))  18.4 us
    ppermute x5, waiting for transfers between devices, other(): lax.ppermute(value, 'mp', [(index, index ^ mask) for index in range(ways)])  17.9 us
    ppermute x5, starting transfers between devices, other(): lax.ppermute(value, 'mp', [(index, index ^ mask) for index in range(ways)])  16.8 us
    all_to_all x1, blocking collectives, exchange(): lax.all_to_all(value, axis, 0, 0, axis_index_groups=groups, tiled=True)  14 us
    pallas_call x8, Pallas kernels, call(): pl.pallas_call(run, out_shape=out_shape, in_specs=[pl.BlockSpec(memory_sp...  7.34 us
    pallas_call x3, Pallas kernels, call_sliced(): pl.pallas_call(body, out_shape=out_shape, grid_spec=pltpu.PrefetchScalarG...  6.02 us
  transfers between devices with their start and end apart: 17, of which 10 were waited for; matrix products, arithmetic and copies ran while one was open for 1% of the time, Pallas kernels for 4%

profile of v7, /device:TPU:2, one launch (start us, length us, event | category | flops | bytes accessed | tf_op | source)
XLA Modules:
  0.0 181.9 jit_solution(2622861472340365621)
XLA Ops:
  0.7 1.9 %inputs.2 = bf16[16,64,256]{2,1,0:T(8,128)(2,1)} custom-call(s32[1]{0:T(128)} %bitcast.quad_ref.refs_0_, bf16[16,4,64,256]{3,2,1,0:T(8,128)(2,1)} %bitcast.29), custom_call_target="tpu_custom_call" | custom-call | tf_op jit(solution)/shard_map/inputs/pallas_call | solution.py:72
  2.6 16.7 %all-to-all-start = ((bf16[16,64,256]{2,1,0:T(8,128)(2,1)}), bf16[16,64,256]{2,1,0:T(8,128)(2,1)S(1)}, u32[]{:S(2)}, u32[]{:S(2)}) async-start(bf16[16,64,256]{2,1,0:T(8,128)(2,1)} %inputs.2), calls=%async_computation | async-start | bytes 1048576 | tf_op jit(solution)/shard_map/inputs/all_to_all | solution.py:289
  19.8 1.9 %collective-permute-start = (bf16[96,256]{1,0:T(8,128)(2,1)S(1)}, bf16[96,256]{1,0:T(8,128)(2,1)S(1)}, u32[]{:S(2)}, u32[]{:S(2)}) collective-permute-start(bf16[96,256]{1,0:T(8,128)(2,1)S(1)} %get-tuple-element.22), channel_id=1, source_target_pairs={{0,16},{16,0},{32,48},{48,32},{64,80},{80,64},{96,112},{112,96},{1... | collective-permute-start | bytes 147464 | tf_op jit(solution)/shard_map/inputs/ppermute | solution.py:296
  21.7 1.9 %collective-permute-start.1 = (bf16[96,256]{1,0:T(8,128)(2,1)S(1)}, bf16[96,256]{1,0:T(8,128)(2,1)S(1)}, u32[]{:S(2)}, u32[]{:S(2)}) collective-permute-start(bf16[96,256]{1,0:T(8,128)(2,1)S(1)} %get-tuple-element.23), channel_id=1, source_target_pairs={{0,512},{16,528},{32,544},{48,560},{64,576},{80,592},{96,608},{112... | collective-permute-start | bytes 147464 | tf_op jit(solution)/shard_map/inputs/ppermute | solution.py:296
  23.6 5.4 %collective-permute-start.2 = (bf16[96,256]{1,0:T(8,128)(2,1)S(1)}, bf16[96,256]{1,0:T(8,128)(2,1)S(1)}, u32[]{:S(2)}, u32[]{:S(2)}) collective-permute-start(bf16[96,256]{1,0:T(8,128)(2,1)S(1)} %get-tuple-element.24), channel_id=1, source_target_pairs={{0,528},{16,512},{32,560},{48,544},{64,592},{80,576},{96,624},{112... | collective-permute-start | bytes 147464 | tf_op jit(solution)/shard_map/inputs/ppermute | solution.py:296
  29.0 2.0 %collective-permute-done.2.packed3_ref = bf16[96,256]{1,0:T(8,128)(2,1)S(1)} collective-permute-done((bf16[96,256]{1,0:T(8,128)(2,1)S(1)}, bf16[96,256]{1,0:T(8,128)(2,1)S(1)}, u32[]{:S(2)}, u32[]{:S(2)}) %collective-permute-start.2) | collective-permute-done | bytes 49184 | tf_op jit(solution)/shard_map/inputs/ppermute | solution.py:296
  31.1 3.1 %forward.1 = (bf16[2,256,256]{2,1,0:T(8,128)(2,1)S(1)}, bf16[2,256,256]{2,1,0:T(8,128)(2,1)}) custom-call(s32[1]{0:T(128)} %bitcast.quad_ref.refs_0_, bf16[1024,256]{1,0:T(8,128)(2,1)S(1)} %bitcast.26, bf16[96,256]{1,0:T(8,128)(2,1)S(1)} %get-tuple-element.21.packed0_ref, bf16[96,256]{1,0:T(8,128)(2,1)S(1)} %collective-permute-done.packed1_ref, ...), custom_call_target="tpu_custom_call" | custom-call | tf_op jit(solution)/shard_map/forward/pallas_call | solution.py:72
  34.2 9.3 %all-to-all-start.1 = ((bf16[64,8,256]{2,1,0:T(8,128)(2,1)}), bf16[64,8,256]{2,1,0:T(8,128)(2,1)S(1)}, u32[]{:S(2)}, u32[]{:S(2)}) async-start(bf16[64,8,256]{2,1,0:T(8,128)(2,1)} %bitcast.5), calls=%async_computation.1 | async-start | bytes 524288 | tf_op jit(solution)/shard_map/ranks/all_to_all | solution.py:289
  43.6 2.6 %counts.1 = (bf16[16,256,256]{2,1,0:T(8,128)(2,1)S(1)}, f32[8,128]{1,0:T(8,128)S(1)}) custom-call(s32[16]{0:T(128)S(1)} %stack.64.refs_0_.order_ref, s32[16,4096]{1,0:T(8,128)S(1)} %reshape.39.refs_2_.refs_1_), custom_call_target="tpu_custom_call" | custom-call | tf_op jit(solution)/shard_map/counts/pallas_call | solution.py:48
  47.5 4.8 %all-to-all-done.1.refs_0_ = bf16[64,8,256]{2,1,0:T(8,128)(2,1)S(1)} async-done(((bf16[64,8,256]{2,1,0:T(8,128)(2,1)}), bf16[64,8,256]{2,1,0:T(8,128)(2,1)S(1)}, u32[]{:S(2)}, u32[]{:S(2)}) %all-to-all-start.1) | async-done | bytes 262176 | tf_op jit(solution)/shard_map/ranks/all_to_all | solution.py:289
  52.4 14.0 %all_to_all.35 = bf16[64,8,256]{2,1,0:T(8,128)(2,1)S(1)} all-to-all(bf16[64,8,256]{2,1,0:T(8,128)(2,1)S(1)} %ranks.1), channel_id=1, replica_groups={{0,16,512,528,1,17,513,529,2,18,514,530,3,19,515,531,4,20,516,532,5,21,..., dimensions={0} | all-to-all | bytes 524288 | tf_op jit(solution)/shard_map/ranks/all_to_all | solution.py:289
  67.4 3.4 %all-to-all-start.3 = ((bf16[4,128,256]{2,1,0:T(8,128)(2,1)}), bf16[4,128,256]{2,1,0:T(8,128)(2,1)S(1)}, u32[]{:S(2)}, u32[]{:S(2)}) async-start(bf16[4,128,256]{2,1,0:T(8,128)(2,1)} %bitcast.23), calls=%async_computation.3 | async-start | bytes 524288 | tf_op jit(solution)/shard_map/near_sums/all_to_all | solution.py:289
  70.8 2.7 %collective-permute-start.3 = (bf16[2,64,256]{2,1,0:T(8,128)(2,1)S(1)}, bf16[2,64,256]{2,1,0:T(8,128)(2,1)S(1)}, u32[]{:S(2)}, u32[]{:S(2)}) collective-permute-start(bf16[2,64,256]{2,1,0:T(8,128)(2,1)S(1)} %get-tuple-element.29), channel_id=1, source_target_pairs={{0,16},{16,0},{32,48},{48,32},{64,80},{80,64},{96,112},{112,96},{1... | collective-permute-start | bytes 196616 | tf_op jit(solution)/shard_map/near_sums/ppermute | solution.py:296
  73.5 2.5 %collective-permute-start.4 = (bf16[2,64,256]{2,1,0:T(8,128)(2,1)S(1)}, bf16[2,64,256]{2,1,0:T(8,128)(2,1)S(1)}, u32[]{:S(2)}, u32[]{:S(2)}) collective-permute-start(bf16[2,64,256]{2,1,0:T(8,128)(2,1)S(1)} %get-tuple-element.30), channel_id=1, source_target_pairs={{0,512},{16,528},{32,544},{48,560},{64,576},{80,592},{96,608},{112... | collective-permute-start | bytes 196616 | tf_op jit(solution)/shard_map/near_sums/ppermute | solution.py:296
  76.0 4.0 %collective-permute-start.5 = (bf16[2,64,256]{2,1,0:T(8,128)(2,1)S(1)}, bf16[2,64,256]{2,1,0:T(8,128)(2,1)S(1)}, u32[]{:S(2)}, u32[]{:S(2)}) collective-permute-start(bf16[2,64,256]{2,1,0:T(8,128)(2,1)S(1)} %get-tuple-element.31), channel_id=1, source_target_pairs={{0,528},{16,512},{32,560},{48,544},{64,592},{80,576},{96,624},{112... | collective-permute-start | bytes 196616 | tf_op jit(solution)/shard_map/near_sums/ppermute | solution.py:296
  80.0 3.4 %collective-permute-done.5.refs_4_ = bf16[2,64,256]{2,1,0:T(8,128)(2,1)S(1)} collective-permute-done((bf16[2,64,256]{2,1,0:T(8,128)(2,1)S(1)}, bf16[2,64,256]{2,1,0:T(8,128)(2,1)S(1)}, u32[]{:S(2)}, u32[]{:S(2)}) %collective-permute-start.5) | collective-permute-done | bytes 65568 | tf_op jit(solution)/shard_map/near_sums/ppermute | solution.py:296
  84.1 4.9 %all-to-all-done.3.refs_0_ = bf16[4,128,256]{2,1,0:T(8,128)(2,1)S(1)} async-done(((bf16[4,128,256]{2,1,0:T(8,128)(2,1)}), bf16[4,128,256]{2,1,0:T(8,128)(2,1)S(1)}, u32[]{:S(2)}, u32[]{:S(2)}) %all-to-all-start.3) | async-done | bytes 262176 | tf_op jit(solution)/shard_map/near_sums/all_to_all | solution.py:289
  89.7 20.9 %all-to-all-start.4 = ((bf16[4,128,256]{2,1,0:T(8,128)(2,1)}), bf16[4,128,256]{2,1,0:T(8,128)(2,1)S(1)}, u32[]{:S(2)}, u32[]{:S(2)}) async-start(bf16[4,128,256]{2,1,0:T(8,128)(2,1)} %near_sums.3), calls=%async_computation.4 | async-start | bytes 524288 | tf_op jit(solution)/shard_map/far_sums/all_to_all | solution.py:289
  110.6 2.5 %collective-permute-start.6 = (bf16[4,64,256]{2,1,0:T(8,128)(2,1)S(1)}, bf16[4,64,256]{2,1,0:T(8,128)(2,1)S(1)}, u32[]{:S(2)}, u32[]{:S(2)}) collective-permute-start(bf16[4,64,256]{2,1,0:T(8,128)(2,1)S(1)} %get-tuple-element.34.refs_1_), channel_id=1, source_target_pairs={{0,8},{1,9},{2,10},{3,11},{4,12},{5,13},{6,14},{7,15},{8,0},{9,1},... | collective-permute-start | bytes 393224 | tf_op jit(solution)/shard_map/far_sums/ppermute | solution.py:300
  113.1 3.6 %collective-permute-start.7 = (bf16[4,64,256]{2,1,0:T(8,128)(2,1)S(1)}, bf16[4,64,256]{2,1,0:T(8,128)(2,1)S(1)}, u32[]{:S(2)}, u32[]{:S(2)}) collective-permute-start(bf16[4,64,256]{2,1,0:T(8,128)(2,1)S(1)} %get-tuple-element.34.refs_1_), channel_id=1, source_target_pairs={{0,4},{1,5},{2,6},{3,7},{4,0},{5,1},{6,2},{7,3},{8,12},{9,13},{10,... | collective-permute-start | bytes 393224 | tf_op jit(solution)/shard_map/far_sums/ppermute | solution.py:300
  116.6 6.2 %collective-permute-start.8 = (bf16[4,64,256]{2,1,0:T(8,128)(2,1)S(1)}, bf16[4,64,256]{2,1,0:T(8,128)(2,1)S(1)}, u32[]{:S(2)}, u32[]{:S(2)}) collective-permute-start(bf16[4,64,256]{2,1,0:T(8,128)(2,1)S(1)} %get-tuple-element.34.refs_1_), channel_id=1, source_target_pairs={{0,12},{1,13},{2,14},{3,15},{4,8},{5,9},{6,10},{7,11},{8,4},{9,5},... | collective-permute-start | bytes 393224 | tf_op jit(solution)/shard_map/far_sums/ppermute | solution.py:300
  122.9 4.6 %collective-permute-done.8 = bf16[4,64,256]{2,1,0:T(8,128)(2,1)S(1)} collective-permute-done((bf16[4,64,256]{2,1,0:T(8,128)(2,1)S(1)}, bf16[4,64,256]{2,1,0:T(8,128)(2,1)S(1)}, u32[]{:S(2)}, u32[]{:S(2)}) %collective-permute-start.8) | collective-permute-done | bytes 131104 | tf_op jit(solution)/shard_map/far_sums/ppermute | solution.py:300
  127.5 2.6 %collective-permute-start.9 = (bf16[16,64,256]{2,1,0:T(8,128)(2,1)S(1)}, bf16[16,64,256]{2,1,0:T(8,128)(2,1)S(1)}, u32[]{:S(2)}, u32[]{:S(2)}) collective-permute-start(bf16[16,64,256]{2,1,0:T(8,128)(2,1)S(1)} %pad_maximum_fusion), channel_id=1, source_target_pairs={{0,2},{1,3},{2,0},{3,1},{4,6},{5,7},{6,4},{7,5},{8,10},{9,11},{10,... | collective-permute-start | bytes 1572872 | tf_op jit(solution)/shard_map/far_sums/ppermute | solution.py:300
  130.1 10.7 %collective-permute-done.9.refs_1_ = bf16[16,64,256]{2,1,0:T(8,128)(2,1)S(1)} collective-permute-done((bf16[16,64,256]{2,1,0:T(8,128)(2,1)S(1)}, bf16[16,64,256]{2,1,0:T(8,128)(2,1)S(1)}, u32[]{:S(2)}, u32[]{:S(2)}) %collective-permute-start.9) | collective-permute-done | bytes 524320 | tf_op jit(solution)/shard_map/far_sums/ppermute | solution.py:300
  140.9 2.2 %all-to-all-done.4.refs_0_ = bf16[4,128,256]{2,1,0:T(8,128)(2,1)S(1)} async-done(((bf16[4,128,256]{2,1,0:T(8,128)(2,1)}), bf16[4,128,256]{2,1,0:T(8,128)(2,1)S(1)}, u32[]{:S(2)}, u32[]{:S(2)}) %all-to-all-start.4) | async-done | bytes 262176 | tf_op jit(solution)/shard_map/far_sums/all_to_all | solution.py:289
  143.9 11.7 %all-to-all-start.5 = ((bf16[4,128,256]{2,1,0:T(8,128)(2,1)}), bf16[4,128,256]{2,1,0:T(8,128)(2,1)S(1)}, u32[]{:S(2)}, u32[]{:S(2)}) async-start(bf16[4,128,256]{2,1,0:T(8,128)(2,1)} %far_sums.1), calls=%async_computation.5 | async-start | bytes 524288 | tf_op jit(solution)/shard_map/near_gather/all_to_all | solution.py:289
  157.1 1.9 %collective-permute-start.10 = (bf16[32,64,256]{2,1,0:T(8,128)(2,1)S(1)}, bf16[32,64,256]{2,1,0:T(8,128)(2,1)S(1)}, u32[]{:S(2)}, u32[]{:S(2)}) collective-permute-start(bf16[32,64,256]{2,1,0:T(8,128)(2,1)S(1)} %get-tuple-element.38), channel_id=1, source_target_pairs={{0,1},{1,0},{2,3},{3,2},{4,5},{5,4},{6,7},{7,6},{8,9},{9,8},{10,11... | collective-permute-start | bytes 3145736 | tf_op jit(solution)/shard_map/near_gather/ppermute | solution.py:300
  159.0 2.6 %collective-permute-done.10.refs_1_ = bf16[32,64,256]{2,1,0:T(8,128)(2,1)S(1)} collective-permute-done((bf16[32,64,256]{2,1,0:T(8,128)(2,1)S(1)}, bf16[32,64,256]{2,1,0:T(8,128)(2,1)S(1)}, u32[]{:S(2)}, u32[]{:S(2)}) %collective-permute-start.10) | collective-permute-done | bytes 1048608 | tf_op jit(solution)/shard_map/near_gather/ppermute | solution.py:300
  161.6 4.1 %all-to-all-done.5.refs_0_ = bf16[4,128,256]{2,1,0:T(8,128)(2,1)S(1)} async-done(((bf16[4,128,256]{2,1,0:T(8,128)(2,1)}), bf16[4,128,256]{2,1,0:T(8,128)(2,1)S(1)}, u32[]{:S(2)}, u32[]{:S(2)}) %all-to-all-start.5) | async-done | bytes 262176 | tf_op jit(solution)/shard_map/near_gather/all_to_all | solution.py:289
  166.7 3.5 %all-to-all-start.6 = ((bf16[4,4,128,256]{3,2,1,0:T(8,128)(2,1)}), bf16[4,4,128,256]{3,2,1,0:T(8,128)(2,1)S(1)}, u32[]{:S(2)}, u32[]{:S(2)}) async-start(bf16[4,4,128,256]{3,2,1,0:T(8,128)(2,1)} %near_gather.1), calls=%async_computation.6 | async-start | bytes 2097152 | tf_op jit(solution)/shard_map/quad_gather/all_to_all | solution.py:289
  173.8 3.2 %quad_gather.2 = bf16[64,64,256]{2,1,0:T(8,128)(2,1)} custom-call(s32[16]{0:T(128)S(1)} %stack.64.refs_0_.order_ref, bf16[16,256,256]{2,1,0:T(8,128)(2,1)S(1)} %copy-done.3, bf16[64,64,256]{2,1,0:T(8,128)(2,1)S(1)} %copy-done.1), custom_call_target="tpu_custom_call" | custom-call | tf_op jit(solution)/shard_map/quad_gather/pallas_call | solution.py:246
  177.0 3.5 %all-to-all-done.6 = bf16[4,4,128,256]{3,2,1,0:T(8,128)(2,1)S(1)} async-done(((bf16[4,4,128,256]{3,2,1,0:T(8,128)(2,1)}), bf16[4,4,128,256]{3,2,1,0:T(8,128)(2,1)S(1)}, u32[]{:S(2)}, u32[]{:S(2)}) %all-to-all-start.6) | async-done | bytes 1048608 | tf_op jit(solution)/shard_map/quad_gather/all_to_all | solution.py:289
  (41 shorter events, 12.8 us)
Async XLA Ops:
  0.6 18.7 %copy-start.7 = (s32[64,64,16]{1,2,0:T(8,128)S(1)}, s32[64,64,16]{1,2,0:T(8,128)}, u32[]{:S(2)}) copy-start(s32[64,64,16]{1,2,0:T(8,128)} %param.5) | copy-start | bytes 786436
  2.6 17.2 %copy-start.6 = (bf16[64,1024]{1,0:T(8,128)(2,1)S(1)}, bf16[64,1024]{1,0:T(8,128)(2,1)}, u32[]{:S(2)}) copy-start(bf16[64,1024]{1,0:T(8,128)(2,1)} %refs_3_.1) | copy-start | bytes 393220
  2.6 28.5 %copy-start.4 = (bf16[1024,256]{1,0:T(8,128)(2,1)S(1)}, bf16[1024,256]{1,0:T(8,128)(2,1)}, u32[]{:S(2)}) copy-start(bf16[1024,256]{1,0:T(8,128)(2,1)} %down_ref.3) | copy-start | bytes 1572868
  2.6 28.5 %copy-start.5 = (bf16[256,1024]{1,0:T(8,128)(2,1)S(1)}, bf16[256,1024]{1,0:T(8,128)(2,1)}, u32[]{:S(2)}) copy-start(bf16[256,1024]{1,0:T(8,128)(2,1)} %up_ref.3) | copy-start | bytes 1572868
  2.6 28.5 %all-to-all-start = ((bf16[16,64,256]{2,1,0:T(8,128)(2,1)}), bf16[16,64,256]{2,1,0:T(8,128)(2,1)S(1)}, u32[]{:S(2)}, u32[]{:S(2)}) async-start(bf16[16,64,256]{2,1,0:T(8,128)(2,1)} %inputs.2), calls=%async_computation | async-start | bytes 1048576 | tf_op jit(solution)/shard_map/inputs/all_to_all | solution.py:289
  19.8 9.2 %collective-permute-start = (bf16[96,256]{1,0:T(8,128)(2,1)S(1)}, bf16[96,256]{1,0:T(8,128)(2,1)S(1)}, u32[]{:S(2)}, u32[]{:S(2)}) collective-permute-start(bf16[96,256]{1,0:T(8,128)(2,1)S(1)} %get-tuple-element.22), channel_id=1, source_target_pairs={{0,16},{16,0},{32,48},{48,32},{64,80},{80,64},{96,112},{112,96},{1... | collective-permute-start | bytes 147464 | tf_op jit(solution)/shard_map/inputs/ppermute | solution.py:296
  21.7 7.3 %collective-permute-start.1 = (bf16[96,256]{1,0:T(8,128)(2,1)S(1)}, bf16[96,256]{1,0:T(8,128)(2,1)S(1)}, u32[]{:S(2)}, u32[]{:S(2)}) collective-permute-start(bf16[96,256]{1,0:T(8,128)(2,1)S(1)} %get-tuple-element.23), channel_id=1, source_target_pairs={{0,512},{16,528},{32,544},{48,560},{64,576},{80,592},{96,608},{112... | collective-permute-start | bytes 147464 | tf_op jit(solution)/shard_map/inputs/ppermute | solution.py:296
  23.6 7.4 %collective-permute-start.2 = (bf16[96,256]{1,0:T(8,128)(2,1)S(1)}, bf16[96,256]{1,0:T(8,128)(2,1)S(1)}, u32[]{:S(2)}, u32[]{:S(2)}) collective-permute-start(bf16[96,256]{1,0:T(8,128)(2,1)S(1)} %get-tuple-element.24), channel_id=1, source_target_pairs={{0,528},{16,512},{32,560},{48,544},{64,592},{80,576},{96,624},{112... | collective-permute-start | bytes 147464 | tf_op jit(solution)/shard_map/inputs/ppermute | solution.py:296
  34.2 18.1 %all-to-all-start.1 = ((bf16[64,8,256]{2,1,0:T(8,128)(2,1)}), bf16[64,8,256]{2,1,0:T(8,128)(2,1)S(1)}, u32[]{:S(2)}, u32[]{:S(2)}) async-start(bf16[64,8,256]{2,1,0:T(8,128)(2,1)} %bitcast.5), calls=%async_computation.1 | async-start | bytes 524288 | tf_op jit(solution)/shard_map/ranks/all_to_all | solution.py:289
  46.2 1.3 copy-start.2
  67.4 21.6 %all-to-all-start.3 = ((bf16[4,128,256]{2,1,0:T(8,128)(2,1)}), bf16[4,128,256]{2,1,0:T(8,128)(2,1)S(1)}, u32[]{:S(2)}, u32[]{:S(2)}) async-start(bf16[4,128,256]{2,1,0:T(8,128)(2,1)} %bitcast.23), calls=%async_computation.3 | async-start | bytes 524288 | tf_op jit(solution)/shard_map/near_sums/all_to_all | solution.py:289
  70.8 9.2 %collective-permute-start.3 = (bf16[2,64,256]{2,1,0:T(8,128)(2,1)S(1)}, bf16[2,64,256]{2,1,0:T(8,128)(2,1)S(1)}, u32[]{:S(2)}, u32[]{:S(2)}) collective-permute-start(bf16[2,64,256]{2,1,0:T(8,128)(2,1)S(1)} %get-tuple-element.29), channel_id=1, source_target_pairs={{0,16},{16,0},{32,48},{48,32},{64,80},{80,64},{96,112},{112,96},{1... | collective-permute-start | bytes 196616 | tf_op jit(solution)/shard_map/near_sums/ppermute | solution.py:296
  73.5 6.5 %collective-permute-start.4 = (bf16[2,64,256]{2,1,0:T(8,128)(2,1)S(1)}, bf16[2,64,256]{2,1,0:T(8,128)(2,1)S(1)}, u32[]{:S(2)}, u32[]{:S(2)}) collective-permute-start(bf16[2,64,256]{2,1,0:T(8,128)(2,1)S(1)} %get-tuple-element.30), channel_id=1, source_target_pairs={{0,512},{16,528},{32,544},{48,560},{64,576},{80,592},{96,608},{112... | collective-permute-start | bytes 196616 | tf_op jit(solution)/shard_map/near_sums/ppermute | solution.py:296
  76.0 7.4 %collective-permute-start.5 = (bf16[2,64,256]{2,1,0:T(8,128)(2,1)S(1)}, bf16[2,64,256]{2,1,0:T(8,128)(2,1)S(1)}, u32[]{:S(2)}, u32[]{:S(2)}) collective-permute-start(bf16[2,64,256]{2,1,0:T(8,128)(2,1)S(1)} %get-tuple-element.31), channel_id=1, source_target_pairs={{0,528},{16,512},{32,560},{48,544},{64,592},{80,576},{96,624},{112... | collective-permute-start | bytes 196616 | tf_op jit(solution)/shard_map/near_sums/ppermute | solution.py:296
  89.7 53.4 %all-to-all-start.4 = ((bf16[4,128,256]{2,1,0:T(8,128)(2,1)}), bf16[4,128,256]{2,1,0:T(8,128)(2,1)S(1)}, u32[]{:S(2)}, u32[]{:S(2)}) async-start(bf16[4,128,256]{2,1,0:T(8,128)(2,1)} %near_sums.3), calls=%async_computation.4 | async-start | bytes 524288 | tf_op jit(solution)/shard_map/far_sums/all_to_all | solution.py:289
  110.6 12.2 %collective-permute-start.6 = (bf16[4,64,256]{2,1,0:T(8,128)(2,1)S(1)}, bf16[4,64,256]{2,1,0:T(8,128)(2,1)S(1)}, u32[]{:S(2)}, u32[]{:S(2)}) collective-permute-start(bf16[4,64,256]{2,1,0:T(8,128)(2,1)S(1)} %get-tuple-element.34.refs_1_), channel_id=1, source_target_pairs={{0,8},{1,9},{2,10},{3,11},{4,12},{5,13},{6,14},{7,15},{8,0},{9,1},... | collective-permute-start | bytes 393224 | tf_op jit(solution)/shard_map/far_sums/ppermute | solution.py:300
  113.1 9.8 %collective-permute-start.7 = (bf16[4,64,256]{2,1,0:T(8,128)(2,1)S(1)}, bf16[4,64,256]{2,1,0:T(8,128)(2,1)S(1)}, u32[]{:S(2)}, u32[]{:S(2)}) collective-permute-start(bf16[4,64,256]{2,1,0:T(8,128)(2,1)S(1)} %get-tuple-element.34.refs_1_), channel_id=1, source_target_pairs={{0,4},{1,5},{2,6},{3,7},{4,0},{5,1},{6,2},{7,3},{8,12},{9,13},{10,... | collective-permute-start | bytes 393224 | tf_op jit(solution)/shard_map/far_sums/ppermute | solution.py:300
  116.6 10.8 %collective-permute-start.8 = (bf16[4,64,256]{2,1,0:T(8,128)(2,1)S(1)}, bf16[4,64,256]{2,1,0:T(8,128)(2,1)S(1)}, u32[]{:S(2)}, u32[]{:S(2)}) collective-permute-start(bf16[4,64,256]{2,1,0:T(8,128)(2,1)S(1)} %get-tuple-element.34.refs_1_), channel_id=1, source_target_pairs={{0,12},{1,13},{2,14},{3,15},{4,8},{5,9},{6,10},{7,11},{8,4},{9,5},... | collective-permute-start | bytes 393224 | tf_op jit(solution)/shard_map/far_sums/ppermute | solution.py:300
  127.5 13.4 %collective-permute-start.9 = (bf16[16,64,256]{2,1,0:T(8,128)(2,1)S(1)}, bf16[16,64,256]{2,1,0:T(8,128)(2,1)S(1)}, u32[]{:S(2)}, u32[]{:S(2)}) collective-permute-start(bf16[16,64,256]{2,1,0:T(8,128)(2,1)S(1)} %pad_maximum_fusion), channel_id=1, source_target_pairs={{0,2},{1,3},{2,0},{3,1},{4,6},{5,7},{6,4},{7,5},{8,10},{9,11},{10,... | collective-permute-start | bytes 1572872 | tf_op jit(solution)/shard_map/far_sums/ppermute | solution.py:300
  143.9 21.8 %all-to-all-start.5 = ((bf16[4,128,256]{2,1,0:T(8,128)(2,1)}), bf16[4,128,256]{2,1,0:T(8,128)(2,1)S(1)}, u32[]{:S(2)}, u32[]{:S(2)}) async-start(bf16[4,128,256]{2,1,0:T(8,128)(2,1)} %far_sums.1), calls=%async_computation.5 | async-start | bytes 524288 | tf_op jit(solution)/shard_map/near_gather/all_to_all | solution.py:289
  155.7 1.4 copy-start
  157.1 4.5 %collective-permute-start.10 = (bf16[32,64,256]{2,1,0:T(8,128)(2,1)S(1)}, bf16[32,64,256]{2,1,0:T(8,128)(2,1)S(1)}, u32[]{:S(2)}, u32[]{:S(2)}) collective-permute-start(bf16[32,64,256]{2,1,0:T(8,128)(2,1)S(1)} %get-tuple-element.38), channel_id=1, source_target_pairs={{0,1},{1,0},{2,3},{3,2},{4,5},{5,4},{6,7},{7,6},{8,9},{9,8},{10,11... | collective-permute-start | bytes 3145736 | tf_op jit(solution)/shard_map/near_gather/ppermute | solution.py:300
  166.7 13.7 %all-to-all-start.6 = ((bf16[4,4,128,256]{3,2,1,0:T(8,128)(2,1)}), bf16[4,4,128,256]{3,2,1,0:T(8,128)(2,1)S(1)}, u32[]{:S(2)}, u32[]{:S(2)}) async-start(bf16[4,4,128,256]{3,2,1,0:T(8,128)(2,1)} %near_gather.1), calls=%async_computation.6 | async-start | bytes 2097152 | tf_op jit(solution)/shard_map/quad_gather/all_to_all | solution.py:289
  170.3 2.0 %copy-start.3 = (bf16[16,256,256]{2,1,0:T(8,128)(2,1)S(1)}, bf16[16,256,256]{2,1,0:T(8,128)(2,1)}, u32[]{:S(2)}) copy-start(bf16[16,256,256]{2,1,0:T(8,128)(2,1)} %copy-done.2) | copy-start | bytes 6291460
  172.2 1.6 copy-start.1
